TPU v7x, 128 devices: a whole 4x4x4 slice. The times are simulated.
128 devices in a mesh: dp: 16 (over x, y), tensor: 8 (over z, core).
Axes of the slice: x: 4, y: 4, z: 4, core: 2. Of those that a mesh axis runs over, the one named last changes fastest.
Arguments:
- queries: bfloat16 [4, 128, 8192], P(None, 'dp', 'tensor'), may hold values from -16 to 16
- new_kv: bfloat16 [4, 128, 2048], P(None, 'dp', 'tensor'), may hold values from -8 to 8
- kv_pool: bfloat16 [1024, 128, 2048], P('dp', None, 'tensor'), may hold values from -4 to 4
- page_tables: int32 [128, 8], P('dp'), may hold values from 0 to 63
- lengths: int32 [128], replicated, may hold values from 1 to 1020, as said below
- parents: int32 [128], replicated, may hold values from 0 to 127, as said below
- out_weight: bfloat16 [8192, 8192], P('tensor'), may hold values from -0.09375 to 0.09375
Outputs:
- projected: bfloat16 [4, 128, 8192], P(None, 'dp', 'tensor')
- child_cache: bfloat16 [128, 1024, 2048], P('dp', None, 'tensor')
Inputs may be any that keep to these rules, and one draw needn't show every extreme that they name: Child c and old beam b are held by indices c // 8 and b // 8 of dp; a problem's beams sit on 4 aligned indices of dp (indices g with equal g // 4). Every parent belongs to its child's problem, and for every index of dp and every index of its problem, exactly 2 children held by the first have parents held by the second. `lengths`: every cache leaves room for the 4 new tokens. `page_tables`: pages may be shared between beams.
All inputs are finite; a program needn't handle non-finite values.
Results may differ from a plain program's by a relative error of at most 0.0058.
Values may be sent and summed in bfloat16 or wider, within the bound.
A program may use at most 128 MiB of HBM per device.

v0:
```python
import jax
import jax.numpy as jnp
from jax import lax
from jax.sharding import PartitionSpec as P

HD = 128
SPAN = 4
MOST = 2


def swapped(block, axis, apart):
    count = lax.axis_size(axis)
    route = []
    for low in range(count):
        high = low | 1 << apart
        if high != low and high < count:
            route += [(low, high), (high, low)]
    return lax.ppermute(block, axis, route)


def softmax_weights(scores):
    shifted = scores - jnp.max(scores, axis=-1, keepdims=True)
    exp_scores = jnp.exp(shifted)
    return exp_scores / jnp.sum(exp_scores, axis=-1, keepdims=True)


def fetch_parents(kv_pool, page_tables, local_beams):
    page_rows = page_tables[local_beams]
    fetched = kv_pool[page_rows]
    return fetched.reshape(local_beams.shape[0], -1, kv_pool.shape[2])


def assemble(fetched, parent_len, fresh):
    position = jnp.arange(fetched.shape[1], dtype=jnp.int32)
    kv_cache = jnp.where(
        position[None, :, None] < parent_len[:, None, None], fetched, jnp.zeros((), jnp.bfloat16)
    )
    for step_index in range(fresh.shape[1]):
        target = (position[None, :] == parent_len[:, None] + step_index)[:, :, None]
        kv_cache = jnp.where(target, fresh[:, step_index][:, None, :], kv_cache)
    return kv_cache


def attend(kv_cache, q_rows, parent_len):
    item_count, positions, channels = kv_cache.shape
    step_count = q_rows.shape[1]
    kv_local = channels // (2 * HD)
    group_size = q_rows.shape[2] // (HD * kv_local)
    per_head = kv_cache.reshape(item_count, positions, kv_local, 2, HD)
    q_heads = q_rows.reshape(item_count, step_count, kv_local, group_size, HD)
    scores = jnp.einsum(
        "ntkgd,nckd->ntkgc", q_heads, per_head[:, :, :, 0], preferred_element_type=jnp.float32
    ) * HD ** (-0.5)
    position = jnp.arange(positions, dtype=jnp.int32)
    limits = parent_len[:, None] + jnp.arange(step_count, dtype=jnp.int32)[None, :]
    visible = position[None, None, :] <= limits[:, :, None]
    scores = jnp.where(visible[:, :, None, None, :], scores, -1e30)
    weights = softmax_weights(scores).astype(jnp.bfloat16)
    head_out = jnp.einsum(
        "ntkgc,nckd->ntkgd", weights, per_head[:, :, :, 1], preferred_element_type=jnp.float32
    )
    return head_out.astype(jnp.bfloat16).reshape(item_count, step_count, kv_local * group_size * HD)


def sectioned(buffer, span, swapper):
    for bit in range(span.bit_length() - 1):
        stride = 1 << bit
        shaped = buffer.reshape((span // (2 * stride), 2, stride) + buffer.shape[1:])
        moved = swapper(shaped[:, 1], bit)
        shaped = jnp.concatenate([shaped[:, :1], moved[:, None]], axis=1)
        buffer = shaped.reshape(buffer.shape)
    return buffer


def local(queries, new_kv, kv_pool, page_tables, lengths, parents, out_weight):
    groups = lax.axis_size("dp")
    myself = lax.axis_index("dp")
    beam_dev = page_tables.shape[0]
    channels = kv_pool.shape[2]
    step_count = queries.shape[0]
    span = SPAN
    slot_ids = jnp.arange(beam_dev, dtype=jnp.int32)
    slot_range = jnp.arange(MOST, dtype=jnp.int32)
    relative = jnp.arange(span, dtype=jnp.int32)
    parent_grid = parents.reshape(groups, beam_dev)
    targets = jnp.bitwise_xor(myself, relative)
    target_rows = parent_grid[targets]
    target_hit = target_rows // beam_dev == myself
    target_rank = jnp.cumsum(target_hit.astype(jnp.int32), axis=1) - 1
    served = target_hit[:, None, :] & (target_rank[:, None, :] == slot_range[None, :, None])
    served_beams = jnp.sum(jnp.where(served, target_rows[:, None, :] % beam_dev, 0), axis=2)
    my_parents = lax.dynamic_index_in_dim(parent_grid, myself, 0, keepdims=False)
    my_len = lengths[my_parents]
    my_source = my_parents // beam_dev
    my_relative = jnp.bitwise_xor(my_source, myself)
    earlier = slot_ids[None, :] < slot_ids[:, None]
    same_source = my_source[:, None] == my_source[None, :]
    my_rank = jnp.sum(same_source & earlier, axis=1)
    picked = my_relative * MOST + my_rank
    q_child = jnp.transpose(queries, (1, 0, 2))
    fresh_child = jnp.transpose(new_kv, (1, 0, 2))
    fetched = fetch_parents(kv_pool, page_tables, served_beams.reshape(-1))
    fetched = fetched.reshape(span, MOST, fetched.shape[1], channels)
    received = sectioned(fetched, span, lambda half, bit: swapped(half, "dp", bit))
    own_rows = received.reshape(span * MOST, -1, channels)[picked]
    kv_cache = assemble(own_rows, my_len, fresh_child)
    attended = attend(kv_cache, q_child, my_len)
    flat_rows = jnp.transpose(attended, (1, 0, 2)).reshape(step_count * beam_dev, -1)
    partial_sums = jnp.dot(flat_rows, out_weight, preferred_element_type=jnp.float32)
    summed = lax.psum_scatter(partial_sums, "tensor", scatter_dimension=1, tiled=True)
    return (summed.astype(jnp.bfloat16).reshape(step_count, beam_dev, -1), kv_cache)


def solution(mesh):
    in_specs = (
        P(None, "dp", "tensor"),
        P(None, "dp", "tensor"),
        P("dp", None, "tensor"),
        P("dp", None),
        P(),
        P(),
        P("tensor", None),
    )
    out_specs = (P(None, "dp", "tensor"), P("dp", None, "tensor"))
    return jax.shard_map(local, mesh=mesh, in_specs=in_specs, out_specs=out_specs, check_vma=False)
```

profile of v0, /device:TPU:0, one launch (start us, length us, event | category | flops | bytes accessed | tf_op | source)
XLA Modules:
  0.0 203.2 jit_solution(14184022099374585774)
XLA Ops:
  7.2 0.0 copy-start
  7.2 0.0 reduce-scatter.2.cloned.1.call-start
  7.3 0.7 reshape.465
  8.0 0.6 gather_fusion.1
  8.6 0.2 reduce_window_sum.11
  8.8 0.1 select_reduce_fusion
  8.9 0.1 copy.17
  9.0 0.1 reshape.466
  9.1 1.2 gather_fusion.2
  10.4 0.1 reshape.500
  10.5 5.0 %gather_fusion.3 = bf16[64,128,256]{2,1,0:T(8,128)(2,1)} fusion(bf16[64,128,256]{2,1,0:T(8,128)(2,1)} %param.9, s32[1024]{0:T(1024)S(1)} %pad_clamp_fusion.1), kind=kCustom, calls=%fused_computation.3 | custom fusion | bytes 8388864 | tf_op jit(solution)/shard_map/gather | solution.py:29
  15.5 3.8 %fusion.26 = (bf16[2,1,1,2,1024,256]{5,4,3,1,0,2:T(8,128)(2,1)S(1)}, bf16[2,1,2,1024,256]{4,3,2,0,1:T(8,128)(2,1)}) fusion(bf16[2,2,1,2,1024,256]{5,4,3,1,0,2:T(8,128)(2,1)} %bitcast.124), kind=kLoop, calls=%fused_computation.97 | loop fusion | bytes 8388608 | tf_op jit(solution)/shard_map/slice | solution.py:70
  19.3 1.7 collective-permute-start
  21.0 45.9 %collective-permute-done = bf16[2,1,2,1024,256]{4,3,2,0,1:T(8,128)(2,1)} collective-permute-done((bf16[2,1,2,1024,256]{4,3,2,0,1:T(8,128)(2,1)}, bf16[2,1,2,1024,256]{4,3,2,0,1:T(8,128)(2,1)}, u32[]{:S(2)}, u32[]{:S(2)}) %collective-permute-start) | collective-permute-done | bytes 2097184 | tf_op jit(solution)/shard_map/ppermute | solution.py:18
  66.9 2.0 maximum_bitcast_fusion
  68.9 0.0 copy-start.1
  68.9 0.0 copy-start.2
  68.9 1.6 fusion.25
  70.5 3.4 %collective-permute-start.1 = (bf16[1,2,2,1024,256]{4,3,2,1,0:T(8,128)(2,1)}, bf16[1,2,2,1024,256]{4,3,2,1,0:T(8,128)(2,1)}, u32[]{:S(2)}, u32[]{:S(2)}) collective-permute-start(bf16[1,2,2,1024,256]{4,3,2,1,0:T(8,128)(2,1)} %get-tuple-element.7), channel_id=1, source_target_pairs={{0,16},{16,0},{8,24},{24,8},{32,48},{48,32},{40,56},{56,40},{64,80... | collective-permute-start | bytes 6291464 | tf_op jit(solution)/shard_map/ppermute | solution.py:18
  73.9 0.0 copy-done.1
  73.9 0.6 gather_fusion
  74.6 0.2 convert_reduce_fusion
  74.8 0.1 iota_add_fusion
  74.9 0.1 iota_compare_fusion.3
  74.9 0.0 copy-done.2
  75.0 0.1 iota_compare_fusion.2
  75.0 0.1 iota_compare_fusion
  75.2 43.8 %collective-permute-done.1 = bf16[1,2,2,1024,256]{4,3,2,1,0:T(8,128)(2,1)} collective-permute-done((bf16[1,2,2,1024,256]{4,3,2,1,0:T(8,128)(2,1)}, bf16[1,2,2,1024,256]{4,3,2,1,0:T(8,128)(2,1)}, u32[]{:S(2)}, u32[]{:S(2)}) %collective-permute-start.1) | collective-permute-done | bytes 2097184 | tf_op jit(solution)/shard_map/ppermute | solution.py:18
  119.0 4.0 %pad_maximum_fusion = bf16[1,2,2,2,1024,256]{5,4,3,2,1,0:T(8,128)(2,1)} fusion(bf16[1,1,2,2,1024,256]{5,4,3,2,1,0:T(8,128)(2,1)} %bitcast.15, bf16[1,1,2,2,1024,256]{5,4,3,2,1,0:T(8,128)(2,1)S(1)} %get-tuple-element.6), kind=kLoop, calls=%fused_computation.6 | loop fusion | flops 2097152 | bytes 8388608 | tf_op jit(solution)/shard_map/concatenate | solution.py:70
  122.9 4.9 %gather_fusion.4 = bf16[8,1024,256]{2,1,0:T(8,128)(2,1)} fusion(bf16[8,1024,256]{2,1,0:T(8,128)(2,1)} %bitcast.122, s32[1024]{0:T(1024)S(1)} %pad_clamp_fusion), kind=kCustom, calls=%fused_computation.4 | custom fusion | bytes 8388640 | tf_op jit(solution)/shard_map/gather | solution.py:105
  127.9 6.4 %copy.19 = bf16[8,1024,256]{1,2,0:T(8,128)(2,1)} copy(bf16[8,1024,256]{2,1,0:T(8,128)(2,1)} %gather_fusion.4) | data formatting | bytes 8388608 | tf_op jit(solution)/shard_map/gather | solution.py:105
  134.3 6.2 %copy.20 = bf16[8,1024,1,2,128]{4,1,0,3,2:T(8,128)(2,1)} copy(bf16[8,1024,1,2,128]{1,4,3,0,2:T(8,128)(2,1)} %bitcast.123) | data formatting | bytes 8388608 | tf_op jit(solution)/shard_map/gather | solution.py:105
  140.5 8.1 %select_select_fusion.1 = bf16[8,1024,1,2,128]{4,1,0,3,2:T(8,128)(2,1)S(1)} fusion(bf16[8,1024,1,2,128]{4,1,0,3,2:T(8,128)(2,1)} %copy.20, pred[8,1024]{1,0:T(8,128)(4,1)S(1)} %get-tuple-element.22, pred[8,1024]{1,0:T(8,128)(4,1)S(1)} %get-tuple-element.21, pred[8,1024]{1,0:T(8,128)(4,1)S(1)} %get-tuple-element.27, pred[8,1024]{1,0:T(8,128)(4,1)S(1)} %get-tuple-element.28, ...), kind=kLoop, calls=%fused_computation.8 | loop fusion | flops 10485760 | bytes 8445952 | tf_op jit(solution)/shard_map/jit(_where)/select_n | solution.py:40
  148.6 0.0 copy-done
  148.6 0.9 fusion.27
  149.5 0.3 fusion.7
  149.8 0.5 fusion.6
  150.3 9.7 %fusion.10 = f32[32,8192]{1,0:T(8,128)} fusion(bf16[1024,8192]{1,0:T(8,128)(2,1)} %param.13, bf16[8,4,1024]{2,1,0:T(4,128)(2,1)S(1)} %reshape.471), kind=kOutput, calls=%fused_computation.26 | convolution fusion | flops 536870912 | bytes 17891328 | tf_op jit(solution)/shard_map/dot_general | solution.py:109
  160.1 0.0 reduce-scatter.2.cloned.1.call-update
  160.1 8.8 %select_select_fusion = bf16[8,1024,256]{2,1,0:T(8,128)(2,1)} fusion(bf16[8,1024,256]{2,1,0:T(8,128)(2,1)} %gather_fusion.4, pred[8,1024]{1,0:T(8,128)(4,1)S(1)} %get-tuple-element.22, pred[8,1024]{1,0:T(8,128)(4,1)S(1)} %get-tuple-element.21, pred[8,1024]{1,0:T(8,128)(4,1)S(1)} %get-tuple-element.27, pred[8,1024]{1,0:T(8,128)(4,1)S(1)} %get-tuple-element.28, ...), kind=kLoop, calls=%fused_computation.7 | loop fusion | flops 10485760 | bytes 8445952 | tf_op jit(solution)/shard_map/jit(_where)/select_n | solution.py:40
  168.8 26.0 %reduce-scatter.2.cloned.1.call-done = f32[32,1024]{1,0:T(8,128)} async-done(((f32[32,8192]{1,0:T(8,128)}), f32[32,1024]{1,0:T(8,128)}) %reduce-scatter.2.cloned.1.call-update) | async-done | bytes 131088 | tf_op jit(solution)/shard_map/reduce_scatter | solution.py:110
  194.8 1.5 convert_bitcast_fusion
  (17 shorter events, 0.2 us)
Async XLA Ops:
  7.2 141.4 %copy-start = (bf16[4,8,1024]{2,1,0:T(8,128)(2,1)S(1)}, bf16[4,8,1024]{2,1,0:T(8,128)(2,1)}, u32[]{:S(2)}) copy-start(bf16[4,8,1024]{2,1,0:T(8,128)(2,1)} %param.7) | copy-start | bytes 196612
  7.2 187.6 %reduce-scatter.2.cloned.1.call-start = ((), (), s32[]{:S(2)}) async-start(), calls=%async_computation.1 | async-start | bytes 1179648 | tf_op jit(solution)/shard_map/reduce_scatter | solution.py:110
  19.3 47.6 %collective-permute-start = (bf16[2,1,2,1024,256]{4,3,2,0,1:T(8,128)(2,1)}, bf16[2,1,2,1024,256]{4,3,2,0,1:T(8,128)(2,1)}, u32[]{:S(2)}, u32[]{:S(2)}) collective-permute-start(bf16[2,1,2,1024,256]{4,3,2,0,1:T(8,128)(2,1)} %get-tuple-element.9), channel_id=1, source_target_pairs={{0,8},{8,0},{16,24},{24,16},{32,40},{40,32},{48,56},{56,48},{64,72... | collective-permute-start | bytes 6291464 | tf_op jit(solution)/shard_map/ppermute | solution.py:18
  68.9 5.0 %copy-start.1 = (s32[128]{0:T(128)S(1)}, s32[128]{0:T(128)}, u32[]{:S(2)}) copy-start(s32[128]{0:T(128)} %param.11) | copy-start | bytes 1540
  68.9 6.0 %copy-start.2 = (bf16[4,8,256]{2,1,0:T(8,128)(2,1)S(1)}, bf16[4,8,256]{2,1,0:T(8,128)(2,1)}, u32[]{:S(2)}) copy-start(bf16[4,8,256]{2,1,0:T(8,128)(2,1)} %param.8) | copy-start | bytes 49156
  70.5 48.4 %collective-permute-start.1 = (bf16[1,2,2,1024,256]{4,3,2,1,0:T(8,128)(2,1)}, bf16[1,2,2,1024,256]{4,3,2,1,0:T(8,128)(2,1)}, u32[]{:S(2)}, u32[]{:S(2)}) collective-permute-start(bf16[1,2,2,1024,256]{4,3,2,1,0:T(8,128)(2,1)} %get-tuple-element.7), channel_id=1, source_target_pairs={{0,16},{16,0},{8,24},{24,8},{32,48},{48,32},{40,56},{56,40},{64,80... | collective-permute-start | bytes 6291464 | tf_op jit(solution)/shard_map/ppermute | solution.py:18
Sparse Core Ops, SparseCore 0:
  160.2 34.5 reduce-scatter.1
where the time goes:
time: 204 us; the launch traced here: 203 us
  waiting for transfers between devices  116 us (57%)
  local copies, waits for them, and re-layouts  31.5 us (15%)
  other arithmetic  25.6 us (13%)
  between operations  14.2 us (7%)
  matrix products  11.1 us (5%)
  starting transfers between devices  5.06 us (2%)
    ppermute x2, waiting for transfers between devices, swapped(): return lax.ppermute(block, axis, route)  89.7 us
    reduce_scatter x1, waiting for transfers between devices, local(): lax.psum_scatter(partial_sums, 'tensor', scatter_dimension=1, tiled=True)  26 us
    gather x3, local copies, waits for them, and re-layouts, local(): own_rows = received.reshape(span * MOST, -1, channels)[picked]  17.6 us
    select_n x2, other arithmetic, assemble(): kv_cache = jnp.where(target, fresh[:, step_index][:, None, :], kv_cache)  16.8 us
    dot_general x1, matrix products, local(): jnp.dot(flat_rows, out_weight, preferred_element_type=jnp.float32)  9.72 us
    slice x2, local copies, waits for them, and re-layouts, sectioned(): shaped = jnp.concatenate([shaped[:, :1], moved[:, None]], axis=1)  5.43 us
    ppermute x2, starting transfers between devices, swapped(): return lax.ppermute(block, axis, route)  5.02 us
    gather x1, local copies, waits for them, and re-layouts, fetch_parents(): fetched = kv_pool[page_rows]  5.02 us
  transfers between devices with their start and end apart: 3, of which 3 were waited for; matrix products, arithmetic and copies ran while one was open for 5% of the time, Pallas kernels for 0%

commit v1 on v0

v1 whole, which is shorter than its diff:
```python
import functools

import jax
import jax.numpy as jnp
from jax import lax
from jax.experimental import pallas as pl
from jax.experimental.pallas import tpu as pltpu
from jax.sharding import PartitionSpec as P

HD = 128
SPAN = 4
MOST = 2
BEAMS = 8
STEPS = 4
PAGE = 128
MESH = pl.DeviceIdType.MESH


def slots_of_children(parents, me):
    taken = [jnp.int32(0) for _ in range(SPAN)]
    slots, owners = [], []
    for child in range(BEAMS):
        parent = parents[me * BEAMS + child]
        apart = jnp.bitwise_and(parent // BEAMS - me, SPAN - 1)
        slot = jnp.int32(0)
        for distance in range(SPAN):
            hit = apart == distance
            slot = jnp.where(hit, distance * MOST + taken[distance], slot)
            taken[distance] = taken[distance] + hit.astype(jnp.int32)
        slots.append(slot)
        owners.append(parent)
    return slots, owners


def served_beams(parents, me, target):
    count = jnp.int32(0)
    beams = [jnp.int32(0) for _ in range(MOST)]
    for child in range(BEAMS):
        parent = parents[target * BEAMS + child]
        hit = parent // BEAMS == me
        for rank in range(MOST):
            beams[rank] = jnp.where(hit & (count == rank), parent % BEAMS, beams[rank])
        count = count + hit.astype(jnp.int32)
    return beams


def exchange_kernel(
    q_ref, new_ref, pool_ref, table_ref, len_ref, par_ref, w_ref,
    recv_ref, proj_ref,
    pool_v, w_v, stage, q_send, q_recv, att, p_send, p_recv, r_send, lens,
    pool_sem, w_sem, own_sem, qs_sem, qr_sem, bs_sem, br_sem, ps_sem, pr_sem, rs_sem, rr_sem,
):
    me = lax.axis_index("dp")
    mine = lax.axis_index("tensor")
    shards = lax.axis_size("tensor")
    y = lax.rem(me, SPAN)
    base = me - y
    context = stage.shape[1] // MOST
    wide = q_ref.shape[2]
    heads = wide // HD
    rows = MOST * STEPS

    def peer(distance):
        return base + lax.rem(y + distance, SPAN)

    pool_copy = pltpu.make_async_copy(pool_ref, pool_v, pool_sem)
    pool_copy.start()
    barrier = pltpu.get_barrier_semaphore()
    for distance in range(1, SPAN):
        pl.semaphore_signal(barrier, inc=1, device_id={"dp": peer(distance)}, device_id_type=MESH)
    for other in range(1, shards):
        pl.semaphore_signal(barrier, inc=1, device_id={"tensor": lax.rem(mine + other, shards)}, device_id_type=MESH)
    w_copies = []
    for block in range(shards):
        copy = pltpu.make_async_copy(w_ref.at[:, pl.ds(block * wide, wide)], w_v.at[block], w_sem.at[block])
        copy.start()
        w_copies.append(copy)

    slots, _ = slots_of_children(par_ref, me)
    row = lax.broadcasted_iota(jnp.int32, (SPAN * rows, BEAMS), 0)
    col = lax.broadcasted_iota(jnp.int32, (SPAN * rows, BEAMS), 1)
    slot_at = jnp.zeros_like(col)
    for child in range(BEAMS):
        slot_at = jnp.where(col == child, slots[child], slot_at)
    q_sorted = jnp.zeros((SPAN * rows, wide), jnp.float32)
    new_sorted = jnp.zeros((SPAN * rows, 2 * HD), jnp.float32)
    for step in range(STEPS):
        pick = jnp.where((row // STEPS == slot_at) & (row % STEPS == step), 1.0, 0.0).astype(jnp.bfloat16)
        q_sorted += jnp.dot(pick, q_ref[step], preferred_element_type=jnp.float32)
        new_sorted += jnp.dot(pick, new_ref[step], preferred_element_type=jnp.float32)
    both = jnp.concatenate([q_sorted, new_sorted], axis=1)
    half = both.shape[1] // 2
    for distance in range(SPAN):
        part = both[distance * rows:(distance + 1) * rows]
        part = jnp.concatenate([part[:, :half], part[:, half:]], axis=0).astype(jnp.bfloat16)
        if distance == 0:
            q_recv[0] = part
        else:
            q_send[distance] = part

    pl.semaphore_wait(barrier, SPAN - 1 + shards - 1)

    q_copies = []
    for distance in range(1, SPAN):
        copy = pltpu.make_async_remote_copy(
            src_ref=q_send.at[distance], dst_ref=q_recv.at[distance],
            send_sem=qs_sem.at[distance], recv_sem=qr_sem.at[distance],
            device_id={"dp": peer(distance)}, device_id_type=MESH,
        )
        copy.start()
        q_copies.append(copy)

    pool_copy.wait()
    served = {}
    for distance in range(SPAN):
        served[distance] = served_beams(par_ref, me, peer(SPAN - distance))
        for rank in range(MOST):
            lens[distance * MOST + rank] = len_ref[me * BEAMS + served[distance][rank]]

    b_copies = []
    for rank in range(MOST):
        for distance in (2, 1, 3, 0):
            beam = served[distance][rank]

            def put(index, carry, distance=distance, rank=rank, beam=beam):
                at = pl.multiple_of(rank * context + index * PAGE, PAGE)
                stage[distance, pl.ds(at, PAGE), :] = pool_v[table_ref[beam, index]]
                return carry

            lax.fori_loop(0, context // PAGE, put, 0)
            span = pl.ds(rank * context, context)
            if distance == 0:
                copy = pltpu.make_async_copy(stage.at[0, span], recv_ref.at[0, span], own_sem.at[rank])
            else:
                copy = pltpu.make_async_remote_copy(
                    src_ref=stage.at[distance, span], dst_ref=recv_ref.at[distance, span],
                    send_sem=bs_sem.at[distance * MOST + rank], recv_sem=br_sem.at[distance * MOST + rank],
                    device_id={"dp": peer(SPAN - distance)}, device_id_type=MESH,
                )
            copy.start()
            b_copies.append(copy)

    for copy in q_copies:
        copy.wait()

    def attend(distance, carry):
        message = q_recv[distance].astype(jnp.float32)
        message = jnp.concatenate([message[:rows], message[rows:]], axis=1)
        q_rows = jnp.concatenate([message[:, h * HD:(h + 1) * HD] for h in range(heads)], axis=0).astype(jnp.bfloat16)
        fresh = message[:, wide:].astype(jnp.bfloat16)
        old_len = lens[distance * MOST]
        last_len = lens[distance * MOST + 1]
        contract = (((1,), (1,)), ((), ()))
        scale = HD ** -0.5
        scores = lax.dot_general(q_rows, stage[distance, :, 0:HD], contract, preferred_element_type=jnp.float32) * scale
        fresh_scores = lax.dot_general(q_rows, fresh[:, :HD], contract, preferred_element_type=jnp.float32) * scale
        rank_at = lax.broadcasted_iota(jnp.int32, scores.shape, 0) // STEPS % MOST
        position = lax.broadcasted_iota(jnp.int32, scores.shape, 1) - rank_at * context
        limit = jnp.where(rank_at == 0, old_len, last_len)
        scores = jnp.where((position >= 0) & (position < limit), scores, -1e30)
        f_row = lax.broadcasted_iota(jnp.int32, fresh_scores.shape, 0)
        f_col = lax.broadcasted_iota(jnp.int32, fresh_scores.shape, 1)
        seen = (f_row // STEPS % MOST == f_col // STEPS) & (f_col % STEPS <= f_row % STEPS)
        fresh_scores = jnp.where(seen, fresh_scores, -1e30)
        top = jnp.maximum(jnp.max(scores, axis=1, keepdims=True), jnp.max(fresh_scores, axis=1, keepdims=True))
        exp_old = jnp.exp(scores - top)
        exp_new = jnp.exp(fresh_scores - top)
        total = jnp.sum(exp_old, axis=1, keepdims=True) + jnp.sum(exp_new, axis=1, keepdims=True)
        w_old = (exp_old / total).astype(jnp.bfloat16)
        w_new = (exp_new / total).astype(jnp.bfloat16)
        out = jnp.dot(w_old, stage[distance, :, HD:2 * HD], preferred_element_type=jnp.float32)
        out += jnp.dot(w_new, fresh[:, HD:], preferred_element_type=jnp.float32)
        out = jnp.concatenate([out[h * rows:(h + 1) * rows] for h in range(heads)], axis=1)
        att[pl.ds(pl.multiple_of(distance * rows, rows), rows), :] = out
        return carry

    lax.fori_loop(0, SPAN, attend, 0)
    attended = att[...].astype(jnp.bfloat16)
    for copy in w_copies:
        copy.wait()

    def p_copy(other):
        return pltpu.make_async_remote_copy(
            src_ref=p_send.at[other], dst_ref=p_recv.at[other],
            send_sem=ps_sem.at[other], recv_sem=pr_sem.at[other],
            device_id={"tensor": lax.rem(mine + other, shards)}, device_id_type=MESH,
        )

    def project(other, carry):
        product = jnp.dot(attended, w_v[lax.rem(mine + other, shards)], preferred_element_type=jnp.float32)
        p_send[other] = product.astype(jnp.bfloat16)
        p_copy(other).start()
        return carry

    lax.fori_loop(1, shards, project, 0)
    own = jnp.dot(attended, w_v[mine], preferred_element_type=jnp.float32)

    def gather_sums(other, total):
        p_copy(other).wait()
        return total + p_recv[other].astype(jnp.float32)

    summed = lax.fori_loop(1, shards, gather_sums, own)
    half = wide // 2
    r_copies = []
    for distance in range(SPAN):
        part = summed[distance * rows:(distance + 1) * rows]
        r_send[distance] = jnp.concatenate([part[:, :half], part[:, half:]], axis=0).astype(jnp.bfloat16)
        if distance == 0:
            copy = pltpu.make_async_copy(r_send.at[0], proj_ref.at[0], own_sem.at[MOST])
        else:
            copy = pltpu.make_async_remote_copy(
                src_ref=r_send.at[distance], dst_ref=proj_ref.at[distance],
                send_sem=rs_sem.at[distance], recv_sem=rr_sem.at[distance],
                device_id={"dp": peer(SPAN - distance)}, device_id_type=MESH,
            )
        copy.start()
        r_copies.append(copy)
    for copy in r_copies:
        copy.wait()
    for copy in b_copies:
        copy.wait()


def finish_kernel(recv_ref, raw_ref, new_ref, len_ref, par_ref, proj_ref, cache_ref, held, in_sem, out_sem):
    me = lax.axis_index("dp")
    context = held.shape[1]
    slots, owners = slots_of_children(par_ref, me)

    def fetch(child):
        return pltpu.make_async_copy(recv_ref.at[slots[child]], held.at[child], in_sem.at[child])

    def put(child):
        return pltpu.make_async_copy(held.at[child], cache_ref.at[child], out_sem.at[child])

    for child in range(BEAMS):
        fetch(child).start()
    fresh = [new_ref[step].astype(jnp.float32) for step in range(STEPS)]
    for child in range(BEAMS):
        fetch(child).wait()
        length = len_ref[owners[child]]

        def fix(index, carry, child=child, length=length):
            at = pl.multiple_of(index * PAGE, PAGE)
            position = at + lax.broadcasted_iota(jnp.int32, (PAGE, 2 * HD), 0)
            page = held[child, pl.ds(at, PAGE), :].astype(jnp.float32)
            page = jnp.where(position < length, page, 0.0)
            for step in range(STEPS):
                page = jnp.where(position == length + step, fresh[step][child:child + 1], page)
            held[child, pl.ds(at, PAGE), :] = page.astype(jnp.bfloat16)
            return carry

        lax.fori_loop(length // PAGE, context // PAGE, fix, 0)
        put(child).start()

    rows = MOST * STEPS
    raw = []
    for distance in range(SPAN):
        part = raw_ref[distance].astype(jnp.float32)
        raw.append(jnp.concatenate([part[:rows], part[rows:]], axis=1))
    raw = jnp.concatenate(raw, axis=0).astype(jnp.bfloat16)
    row = lax.broadcasted_iota(jnp.int32, (BEAMS, SPAN * rows), 0)
    col = lax.broadcasted_iota(jnp.int32, (BEAMS, SPAN * rows), 1)
    slot_at = jnp.zeros_like(col)
    for child in range(BEAMS):
        slot_at = jnp.where(row == child, slots[child], slot_at)
    for step in range(STEPS):
        pick = jnp.where(col == slot_at * STEPS + step, 1.0, 0.0).astype(jnp.bfloat16)
        proj_ref[step] = jnp.dot(pick, raw, preferred_element_type=jnp.float32).astype(jnp.bfloat16)
    for child in range(BEAMS):
        put(child).wait()


def local(shards, queries, new_kv, kv_pool, page_tables, lengths, parents, out_weight):
    wide = queries.shape[2]
    channels = kv_pool.shape[2]
    context = page_tables.shape[1] * kv_pool.shape[1]
    rows = MOST * STEPS
    vmem = pl.BlockSpec(memory_space=pltpu.VMEM)
    smem = pl.BlockSpec(memory_space=pltpu.SMEM)
    hbm = pl.BlockSpec(memory_space=pl.ANY)
    dma = pltpu.SemaphoreType.DMA
    bf16 = jnp.bfloat16
    with jax.named_scope("exchange"):
        recv, raw = pl.pallas_call(
            exchange_kernel,
            out_shape=(
                jax.ShapeDtypeStruct((SPAN, MOST * context, channels), bf16),
                jax.ShapeDtypeStruct((SPAN, 2 * rows, wide // 2), bf16),
            ),
            in_specs=[vmem, vmem, hbm, smem, smem, smem, hbm],
            out_specs=(hbm, hbm),
            scratch_shapes=[
                pltpu.VMEM(kv_pool.shape, bf16),
                pltpu.VMEM((shards, out_weight.shape[0], wide), bf16),
                pltpu.VMEM((SPAN, MOST * context, channels), bf16),
                pltpu.VMEM((SPAN, 2 * rows, (wide + channels) // 2), bf16),
                pltpu.VMEM((SPAN, 2 * rows, (wide + channels) // 2), bf16),
                pltpu.VMEM((SPAN * rows, wide), jnp.float32),
                pltpu.VMEM((shards, SPAN * rows, wide), bf16),
                pltpu.VMEM((shards, SPAN * rows, wide), bf16),
                pltpu.VMEM((SPAN, 2 * rows, wide // 2), bf16),
                pltpu.SMEM((SPAN * MOST,), jnp.int32),
                dma, dma((shards,)), dma((MOST + 1,)),
                dma((SPAN,)), dma((SPAN,)),
                dma((SPAN * MOST,)), dma((SPAN * MOST,)),
                dma((shards,)), dma((shards,)),
                dma((SPAN,)), dma((SPAN,)),
            ],
            compiler_params=pltpu.CompilerParams(
                collective_id=0, has_side_effects=True, vmem_limit_bytes=48 * 1024 * 1024
            ),
            name="exchange",
        )(queries, new_kv, kv_pool, page_tables, lengths, parents, out_weight)
    with jax.named_scope("finish"):
        return pl.pallas_call(
            finish_kernel,
            out_shape=(
                jax.ShapeDtypeStruct(queries.shape, bf16),
                jax.ShapeDtypeStruct((BEAMS, context, channels), bf16),
            ),
            in_specs=[hbm, vmem, vmem, smem, smem],
            out_specs=(vmem, hbm),
            scratch_shapes=[pltpu.VMEM((BEAMS, context, channels), bf16), dma((BEAMS,)), dma((BEAMS,))],
            compiler_params=pltpu.CompilerParams(vmem_limit_bytes=24 * 1024 * 1024),
            name="finish",
        )(recv.reshape(BEAMS, context, channels), raw, new_kv, lengths, parents)


def solution(mesh):
    in_specs = (
        P(None, "dp", "tensor"),
        P(None, "dp", "tensor"),
        P("dp", None, "tensor"),
        P("dp", None),
        P(),
        P(),
        P("tensor", None),
    )
    out_specs = (P(None, "dp", "tensor"), P("dp", None, "tensor"))
    body = functools.partial(local, mesh.shape["tensor"])
    return jax.shard_map(body, mesh=mesh, in_specs=in_specs, out_specs=out_specs, check_vma=False)
```

time: 204 us -> 65.1 us (0.32)
  waiting for transfers between devices: 116 us -> 0 us
  Pallas kernels: 0 us -> 59.9 us
  local copies, waits for them, and re-layouts: 31.5 us -> 3.55 us
  other arithmetic: 25.6 us -> 0 us
  between operations: 14.2 us -> 0.65 us
  matrix products: 11.1 us -> 0 us
  starting transfers between devices: 5.06 us -> 0 us
    ppermute x2 -> x0, waiting for transfers between devices: 89.7 us -> none  [swapped(): return lax.ppermute(block, axis, route)]
    pallas_call x0 -> x2, Pallas kernels: none -> 59.9 us  [the longest x1 55.9 us: local(): pl.pallas_call(exchange_kernel, out_shape=(jax.ShapeDtypeStruct((SPAN, MO...]
    reduce_scatter x1 -> x0, waiting for transfers between devices: 26 us -> none  [local(): lax.psum_scatter(partial_sums, 'tensor', scatter_dimension=1, tiled=True)]
    gather x7 -> x0, local copies, waits for them, and re-layouts: 25.1 us -> none  [the longest x3 17.6 us: local(): own_rows = received.reshape(span * MOST, -1, channels)[picked]]
    select_n x9 -> x0, other arithmetic: 16.9 us -> none  [the longest x2 16.8 us: assemble(): kv_cache = jnp.where(target, fresh[:, step_index][:, None, :], kv_cache)]
    dot_general x3 -> x0, matrix products: 11.1 us -> none  [the longest x1 9.72 us: local(): jnp.dot(flat_rows, out_weight, preferred_element_type=jnp.float32)]
    slice x2 -> x0, local copies, waits for them, and re-layouts: 5.43 us -> none  [sectioned(): shaped = jnp.concatenate([shaped[:, :1], moved[:, None]], axis=1)]
    ppermute x2 -> x0, starting transfers between devices: 5.02 us -> none  [swapped(): return lax.ppermute(block, axis, route)]
  transfers between devices with their start and end apart: 3 -> 0, of which waited for: 3 -> 0; matrix products, arithmetic and copies ran while one was open for 5% -> 0% of each run, Pallas kernels for 0% -> 0%
where the time goes in v1:
time: 65.1 us; the launch traced here: 64.1 us
  Pallas kernels  59.9 us (92%)
  local copies, waits for them, and re-layouts  3.55 us (5%)
    pallas_call x1, Pallas kernels, local(): pl.pallas_call(exchange_kernel, out_shape=(jax.ShapeDtypeStruct((SPAN, MO...  55.9 us
    pallas_call x1, Pallas kernels, local(): pl.pallas_call(finish_kernel, out_shape=(jax.ShapeDtypeStruct(queries.sha...  3.96 us
    unnamed x10, local copies, waits for them, and re-layouts  3.55 us

profile of v1, /device:TPU:0, one launch (start us, length us, event | category | flops | bytes accessed | tf_op | source)
XLA Modules:
  0.0 64.1 jit_solution(13333896899945026424)
XLA Ops:
  0.6 0.0 copy-start
  0.6 0.8 %copy-done = bf16[4,8,1024]{2,1,0:T(8,128)(2,1)S(1)} copy-done((bf16[4,8,1024]{2,1,0:T(8,128)(2,1)S(1)}, bf16[4,8,1024]{2,1,0:T(8,128)(2,1)}, u32[]{:S(2)}) %copy-start) | copy-done | bytes 65560
  1.5 0.0 copy-start.1
  1.5 0.7 %copy-done.1 = bf16[4,8,256]{2,1,0:T(8,128)(2,1)S(1)} copy-done((bf16[4,8,256]{2,1,0:T(8,128)(2,1)S(1)}, bf16[4,8,256]{2,1,0:T(8,128)(2,1)}, u32[]{:S(2)}) %copy-start.1) | copy-done | bytes 16408
  2.2 0.0 copy-start.2
  2.2 0.7 %copy-done.2 = s32[8,8]{1,0:T(8,128)S(1)} copy-done((s32[8,8]{1,0:T(8,128)S(1)}, s32[8,8]{1,0:T(8,128)}, u32[]{:S(2)}) %copy-start.2) | copy-done | bytes 280
  2.9 0.0 copy-start.3
  2.9 0.7 %copy-done.3 = s32[128]{0:T(128)S(1)} copy-done((s32[128]{0:T(128)S(1)}, s32[128]{0:T(128)}, u32[]{:S(2)}) %copy-start.3) | copy-done | bytes 536
  3.5 0.0 copy-start.4
  3.5 0.7 %copy-done.4 = s32[128]{0:T(128)S(1)} copy-done((s32[128]{0:T(128)S(1)}, s32[128]{0:T(128)}, u32[]{:S(2)}) %copy-start.4) | copy-done | bytes 536
  4.2 55.9 %exchange.1 = (bf16[4,2048,256]{2,1,0:T(8,128)(2,1)S(1)}, bf16[4,16,512]{2,1,0:T(8,128)(2,1)S(1)}) custom-call(bf16[4,8,1024]{2,1,0:T(8,128)(2,1)S(1)} %copy-done, bf16[4,8,256]{2,1,0:T(8,128)(2,1)S(1)} %copy-done.1, bf16[64,128,256]{2,1,0:T(8,128)(2,1)} %pool_ref.1, s32[8,8]{1,0:T(8,128)S(1)} %copy-done.2, s32[128]{0:T(128)S(1)} %copy-done.3, ...), custom_call_target="tpu_custom_call" | custom-call | tf_op jit(solution)/shard_map/exchange/exchange/pallas_call | solution.py:284
  60.1 4.0 %finish.1 = (bf16[4,8,1024]{2,1,0:T(8,128)(2,1)}, bf16[8,1024,256]{2,1,0:T(8,128)(2,1)}) custom-call(bf16[8,1024,256]{2,1,0:T(8,128)(2,1)S(1)} %bitcast.1, bf16[4,16,512]{2,1,0:T(8,128)(2,1)S(1)} %get-tuple-element.5.raw_ref, bf16[4,8,256]{2,1,0:T(8,128)(2,1)S(1)} %copy-done.1, s32[128]{0:T(128)S(1)} %copy-done.3, s32[128]{0:T(128)S(1)} %copy-done.4), custom_call_target="tpu_custom_call" | custom-call | tf_op jit(solution)/shard_map/finish/finish/pallas_call | solution.py:315
Async XLA Ops:
  0.6 0.8 %copy-start = (bf16[4,8,1024]{2,1,0:T(8,128)(2,1)S(1)}, bf16[4,8,1024]{2,1,0:T(8,128)(2,1)}, u32[]{:S(2)}) copy-start(bf16[4,8,1024]{2,1,0:T(8,128)(2,1)} %q_ref.1) | copy-start | bytes 196612
  1.5 0.7 %copy-start.1 = (bf16[4,8,256]{2,1,0:T(8,128)(2,1)S(1)}, bf16[4,8,256]{2,1,0:T(8,128)(2,1)}, u32[]{:S(2)}) copy-start(bf16[4,8,256]{2,1,0:T(8,128)(2,1)} %new_ref.3) | copy-start | bytes 49156
  2.2 0.7 %copy-start.2 = (s32[8,8]{1,0:T(8,128)S(1)}, s32[8,8]{1,0:T(8,128)}, u32[]{:S(2)}) copy-start(s32[8,8]{1,0:T(8,128)} %table_ref.1) | copy-start | bytes 772
  2.9 0.7 %copy-start.3 = (s32[128]{0:T(128)S(1)}, s32[128]{0:T(128)}, u32[]{:S(2)}) copy-start(s32[128]{0:T(128)} %len_ref.3) | copy-start | bytes 1540
  3.5 0.7 %copy-start.4 = (s32[128]{0:T(128)S(1)}, s32[128]{0:T(128)}, u32[]{:S(2)}) copy-start(s32[128]{0:T(128)} %par_ref.3) | copy-start | bytes 1540

commit v2 on v1

--- a/solution.py
+++ b/solution.py
@@ -45,10 +45,11 @@
 
 
 def exchange_kernel(
-    q_ref, new_ref, pool_ref, table_ref, len_ref, par_ref, w_ref,
+    q_hbm, new_hbm, pool_ref, table_hbm, len_hbm, par_hbm, w_ref,
     recv_ref, proj_ref,
+    q_ref, new_ref, table_ref, len_ref, par_ref,
     pool_v, w_v, stage, q_send, q_recv, att, p_send, p_recv, r_send, lens,
-    pool_sem, w_sem, own_sem, qs_sem, qr_sem, bs_sem, br_sem, ps_sem, pr_sem, rs_sem, rr_sem,
+    in_sem, pool_sem, w_sem, own_sem, qs_sem, qr_sem, bs_sem, br_sem, ps_sem, pr_sem, rs_sem, rr_sem,
 ):
     me = lax.axis_index("dp")
     mine = lax.axis_index("tensor")
@@ -56,13 +57,19 @@
     y = lax.rem(me, SPAN)
     base = me - y
     context = stage.shape[1] // MOST
-    wide = q_ref.shape[2]
+    wide = q_hbm.shape[2]
     heads = wide // HD
     rows = MOST * STEPS
 
     def peer(distance):
         return base + lax.rem(y + distance, SPAN)
 
+    in_copies = []
+    operands = ((par_hbm, par_ref), (q_hbm, q_ref), (new_hbm, new_ref), (table_hbm, table_ref), (len_hbm, len_ref))
+    for at, (source, target) in enumerate(operands):
+        copy = pltpu.make_async_copy(source, target, in_sem.at[at])
+        copy.start()
+        in_copies.append(copy)
     pool_copy = pltpu.make_async_copy(pool_ref, pool_v, pool_sem)
     pool_copy.start()
     barrier = pltpu.get_barrier_semaphore()
@@ -70,11 +77,8 @@
         pl.semaphore_signal(barrier, inc=1, device_id={"dp": peer(distance)}, device_id_type=MESH)
     for other in range(1, shards):
         pl.semaphore_signal(barrier, inc=1, device_id={"tensor": lax.rem(mine + other, shards)}, device_id_type=MESH)
-    w_copies = []
-    for block in range(shards):
-        copy = pltpu.make_async_copy(w_ref.at[:, pl.ds(block * wide, wide)], w_v.at[block], w_sem.at[block])
-        copy.start()
-        w_copies.append(copy)
+    for copy in in_copies:
+        copy.wait()
 
     slots, _ = slots_of_children(par_ref, me)
     row = lax.broadcasted_iota(jnp.int32, (SPAN * rows, BEAMS), 0)
@@ -111,6 +115,11 @@
         q_copies.append(copy)
 
     pool_copy.wait()
+    w_copies = []
+    for block in range(shards):
+        copy = pltpu.make_async_copy(w_ref.at[:, pl.ds(block * wide, wide)], w_v.at[block], w_sem.at[block])
+        copy.start()
+        w_copies.append(copy)
     served = {}
     for distance in range(SPAN):
         served[distance] = served_beams(par_ref, me, peer(SPAN - distance))
@@ -221,36 +230,48 @@
         copy.wait()
 
 
-def finish_kernel(recv_ref, raw_ref, new_ref, len_ref, par_ref, proj_ref, cache_ref, held, in_sem, out_sem):
+def finish_kernel(recv_ref, raw_ref, new_hbm, len_hbm, par_hbm, proj_ref, cache_ref, new_ref, len_ref, par_ref, edge, zeros, in_sem, out_sem):
     me = lax.axis_index("dp")
-    context = held.shape[1]
+    pages = recv_ref.shape[1] // PAGE
+    operands = ((par_hbm, par_ref), (len_hbm, len_ref), (new_hbm, new_ref))
+    in_copies = [pltpu.make_async_copy(source, target, in_sem.at[at]) for at, (source, target) in enumerate(operands)]
+    for copy in in_copies:
+        copy.start()
+    zeros[...] = jnp.zeros_like(zeros)
+    for copy in in_copies:
+        copy.wait()
     slots, owners = slots_of_children(par_ref, me)
-
-    def fetch(child):
-        return pltpu.make_async_copy(recv_ref.at[slots[child]], held.at[child], in_sem.at[child])
-
-    def put(child):
-        return pltpu.make_async_copy(held.at[child], cache_ref.at[child], out_sem.at[child])
-
-    for child in range(BEAMS):
-        fetch(child).start()
     fresh = [new_ref[step].astype(jnp.float32) for step in range(STEPS)]
     for child in range(BEAMS):
-        fetch(child).wait()
+        slot = slots[child]
         length = len_ref[owners[child]]
-
-        def fix(index, carry, child=child, length=length):
+        first = length // PAGE
+        last = (length + STEPS - 1) // PAGE
+
+        def whole(index, carry, child=child, slot=slot):
+            span = pl.ds(pl.multiple_of(index * PAGE, PAGE), PAGE)
+            pltpu.make_async_copy(recv_ref.at[slot, span], cache_ref.at[child, span], out_sem).start()
+            return carry
+
+        def clear(index, carry, child=child):
+            span = pl.ds(pl.multiple_of(index * PAGE, PAGE), PAGE)
+            pltpu.make_async_copy(zeros, cache_ref.at[child, span], out_sem).start()
+            return carry
+
+        def fix(index, carry, child=child, slot=slot, length=length, first=first):
             at = pl.multiple_of(index * PAGE, PAGE)
             position = at + lax.broadcasted_iota(jnp.int32, (PAGE, 2 * HD), 0)
-            page = held[child, pl.ds(at, PAGE), :].astype(jnp.float32)
+            page = recv_ref[slot, pl.ds(at, PAGE), :].astype(jnp.float32)
             page = jnp.where(position < length, page, 0.0)
             for step in range(STEPS):
                 page = jnp.where(position == length + step, fresh[step][child:child + 1], page)
-            held[child, pl.ds(at, PAGE), :] = page.astype(jnp.bfloat16)
+            edge[child * 2 + index - first] = page.astype(jnp.bfloat16)
+            pltpu.make_async_copy(edge.at[child * 2 + index - first], cache_ref.at[child, pl.ds(at, PAGE)], out_sem).start()
             return carry
 
-        lax.fori_loop(length // PAGE, context // PAGE, fix, 0)
-        put(child).start()
+        lax.fori_loop(0, first, whole, 0)
+        lax.fori_loop(last + 1, pages, clear, 0)
+        lax.fori_loop(first, last + 1, fix, 0)
 
     rows = MOST * STEPS
     raw = []
@@ -266,8 +287,7 @@
     for step in range(STEPS):
         pick = jnp.where(col == slot_at * STEPS + step, 1.0, 0.0).astype(jnp.bfloat16)
         proj_ref[step] = jnp.dot(pick, raw, preferred_element_type=jnp.float32).astype(jnp.bfloat16)
-    for child in range(BEAMS):
-        put(child).wait()
+    pltpu.make_async_copy(recv_ref, cache_ref, out_sem).wait()
 
 
 def local(shards, queries, new_kv, kv_pool, page_tables, lengths, parents, out_weight):
@@ -276,8 +296,8 @@
     context = page_tables.shape[1] * kv_pool.shape[1]
     rows = MOST * STEPS
     vmem = pl.BlockSpec(memory_space=pltpu.VMEM)
-    smem = pl.BlockSpec(memory_space=pltpu.SMEM)
-    hbm = pl.BlockSpec(memory_space=pl.ANY)
+    hbm = pl.BlockSpec(memory_space=pltpu.HBM)
+    free = pl.BlockSpec(memory_space=pl.ANY)
     dma = pltpu.SemaphoreType.DMA
     bf16 = jnp.bfloat16
     with jax.named_scope("exchange"):
@@ -287,9 +307,14 @@
                 jax.ShapeDtypeStruct((SPAN, MOST * context, channels), bf16),
                 jax.ShapeDtypeStruct((SPAN, 2 * rows, wide // 2), bf16),
             ),
-            in_specs=[vmem, vmem, hbm, smem, smem, smem, hbm],
-            out_specs=(hbm, hbm),
+            in_specs=[hbm] * 7,
+            out_specs=(free, free),
             scratch_shapes=[
+                pltpu.VMEM(queries.shape, bf16),
+                pltpu.VMEM(new_kv.shape, bf16),
+                pltpu.SMEM(page_tables.shape, jnp.int32),
+                pltpu.SMEM(lengths.shape, jnp.int32),
+                pltpu.SMEM(parents.shape, jnp.int32),
                 pltpu.VMEM(kv_pool.shape, bf16),
                 pltpu.VMEM((shards, out_weight.shape[0], wide), bf16),
                 pltpu.VMEM((SPAN, MOST * context, channels), bf16),
@@ -300,7 +325,7 @@
                 pltpu.VMEM((shards, SPAN * rows, wide), bf16),
                 pltpu.VMEM((SPAN, 2 * rows, wide // 2), bf16),
                 pltpu.SMEM((SPAN * MOST,), jnp.int32),
-                dma, dma((shards,)), dma((MOST + 1,)),
+                dma((5,)), dma, dma((shards,)), dma((MOST + 1,)),
                 dma((SPAN,)), dma((SPAN,)),
                 dma((SPAN * MOST,)), dma((SPAN * MOST,)),
                 dma((shards,)), dma((shards,)),
@@ -318,9 +343,16 @@
                 jax.ShapeDtypeStruct(queries.shape, bf16),
                 jax.ShapeDtypeStruct((BEAMS, context, channels), bf16),
             ),
-            in_specs=[hbm, vmem, vmem, smem, smem],
+            in_specs=[vmem, vmem, hbm, hbm, hbm],
             out_specs=(vmem, hbm),
-            scratch_shapes=[pltpu.VMEM((BEAMS, context, channels), bf16), dma((BEAMS,)), dma((BEAMS,))],
+            scratch_shapes=[
+                pltpu.VMEM(new_kv.shape, bf16),
+                pltpu.SMEM(lengths.shape, jnp.int32),
+                pltpu.SMEM(parents.shape, jnp.int32),
+                pltpu.VMEM((2 * BEAMS, PAGE, channels), bf16),
+                pltpu.VMEM((PAGE, channels), bf16),
+                dma((3,)), dma,
+            ],
             compiler_params=pltpu.CompilerParams(vmem_limit_bytes=24 * 1024 * 1024),
             name="finish",
         )(recv.reshape(BEAMS, context, channels), raw, new_kv, lengths, parents)

time: 65.1 us -> 63.6 us (0.977)
  Pallas kernels: 59.9 us -> 58.7 us
    pallas_call x1, Pallas kernels: 3.96 us -> 3.28 us  [local(): pl.pallas_call(finish_kernel, out_shape=(jax.ShapeDtypeStruct(queries.sha...]
where the time goes in v2:
time: 63.6 us; the launch traced here: 62.9 us
  Pallas kernels  58.7 us (92%)
  local copies, waits for them, and re-layouts  3.55 us (6%)
  between operations  0.65 us (1%)
    pallas_call x1, Pallas kernels, local(): pl.pallas_call(exchange_kernel, out_shape=(jax.ShapeDtypeStruct((SPAN, MO...  55.4 us
    unnamed x10, local copies, waits for them, and re-layouts  3.55 us
    pallas_call x1, Pallas kernels, local(): pl.pallas_call(finish_kernel, out_shape=(jax.ShapeDtypeStruct(queries.sha...  3.28 us

profile of v2, /device:TPU:0, one launch (start us, length us, event | category | flops | bytes accessed | tf_op | source)
XLA Modules:
  0.0 62.9 jit_solution(11662854350790356909)
XLA Ops:
  0.6 0.0 copy-start
  0.6 0.8 %copy-done = bf16[4,8,1024]{2,1,0:T(8,128)(2,1)S(1)} copy-done((bf16[4,8,1024]{2,1,0:T(8,128)(2,1)S(1)}, bf16[4,8,1024]{2,1,0:T(8,128)(2,1)}, u32[]{:S(2)}) %copy-start) | copy-done | bytes 65560
  1.5 0.0 copy-start.1
  1.5 0.7 %copy-done.1 = bf16[4,8,256]{2,1,0:T(8,128)(2,1)S(1)} copy-done((bf16[4,8,256]{2,1,0:T(8,128)(2,1)S(1)}, bf16[4,8,256]{2,1,0:T(8,128)(2,1)}, u32[]{:S(2)}) %copy-start.1) | copy-done | bytes 16408
  2.2 0.0 copy-start.2
  2.2 0.7 %copy-done.2 = s32[8,8]{1,0:T(8,128)S(1)} copy-done((s32[8,8]{1,0:T(8,128)S(1)}, s32[8,8]{1,0:T(8,128)}, u32[]{:S(2)}) %copy-start.2) | copy-done | bytes 280
  2.9 0.0 copy-start.3
  2.9 0.7 %copy-done.3 = s32[128]{0:T(128)S(1)} copy-done((s32[128]{0:T(128)S(1)}, s32[128]{0:T(128)}, u32[]{:S(2)}) %copy-start.3) | copy-done | bytes 536
  3.5 0.0 copy-start.4
  3.5 0.7 %copy-done.4 = s32[128]{0:T(128)S(1)} copy-done((s32[128]{0:T(128)S(1)}, s32[128]{0:T(128)}, u32[]{:S(2)}) %copy-start.4) | copy-done | bytes 536
  4.2 55.4 %exchange.1 = (bf16[4,2048,256]{2,1,0:T(8,128)(2,1)S(1)}, bf16[4,16,512]{2,1,0:T(8,128)(2,1)S(1)}) custom-call(bf16[4,8,1024]{2,1,0:T(8,128)(2,1)S(1)} %copy-done, bf16[4,8,256]{2,1,0:T(8,128)(2,1)S(1)} %copy-done.1, bf16[64,128,256]{2,1,0:T(8,128)(2,1)} %pool_ref.1, s32[8,8]{1,0:T(8,128)S(1)} %copy-done.2, s32[128]{0:T(128)S(1)} %copy-done.3, ...), custom_call_target="tpu_custom_call" | custom-call | tf_op jit(solution)/shard_map/exchange/exchange/pallas_call | solution.py:304
  59.6 3.3 %finish.1 = (bf16[4,8,1024]{2,1,0:T(8,128)(2,1)}, bf16[8,1024,256]{2,1,0:T(8,128)(2,1)}) custom-call(bf16[8,1024,256]{2,1,0:T(8,128)(2,1)S(1)} %bitcast.1, bf16[4,16,512]{2,1,0:T(8,128)(2,1)S(1)} %get-tuple-element.5.raw_ref, bf16[4,8,256]{2,1,0:T(8,128)(2,1)S(1)} %copy-done.1, s32[128]{0:T(128)S(1)} %copy-done.3, s32[128]{0:T(128)S(1)} %copy-done.4), custom_call_target="tpu_custom_call" | custom-call | tf_op jit(solution)/shard_map/finish/finish/pallas_call | solution.py:340
Async XLA Ops:
  0.6 0.8 %copy-start = (bf16[4,8,1024]{2,1,0:T(8,128)(2,1)S(1)}, bf16[4,8,1024]{2,1,0:T(8,128)(2,1)}, u32[]{:S(2)}) copy-start(bf16[4,8,1024]{2,1,0:T(8,128)(2,1)} %q_hbm.1) | copy-start | bytes 196612
  1.5 0.7 %copy-start.1 = (bf16[4,8,256]{2,1,0:T(8,128)(2,1)S(1)}, bf16[4,8,256]{2,1,0:T(8,128)(2,1)}, u32[]{:S(2)}) copy-start(bf16[4,8,256]{2,1,0:T(8,128)(2,1)} %new_hbm.3) | copy-start | bytes 49156
  2.2 0.7 %copy-start.2 = (s32[8,8]{1,0:T(8,128)S(1)}, s32[8,8]{1,0:T(8,128)}, u32[]{:S(2)}) copy-start(s32[8,8]{1,0:T(8,128)} %table_hbm.1) | copy-start | bytes 772
  2.9 0.7 %copy-start.3 = (s32[128]{0:T(128)S(1)}, s32[128]{0:T(128)}, u32[]{:S(2)}) copy-start(s32[128]{0:T(128)} %len_hbm.3) | copy-start | bytes 1540
  3.5 0.7 %copy-start.4 = (s32[128]{0:T(128)S(1)}, s32[128]{0:T(128)}, u32[]{:S(2)}) copy-start(s32[128]{0:T(128)} %par_hbm.3) | copy-start | bytes 1540

commit v3 on v2

--- a/solution.py
+++ b/solution.py
@@ -64,19 +64,19 @@
     def peer(distance):
         return base + lax.rem(y + distance, SPAN)
 
-    in_copies = []
-    operands = ((par_hbm, par_ref), (q_hbm, q_ref), (new_hbm, new_ref), (table_hbm, table_ref), (len_hbm, len_ref))
-    for at, (source, target) in enumerate(operands):
-        copy = pltpu.make_async_copy(source, target, in_sem.at[at])
-        copy.start()
-        in_copies.append(copy)
-    pool_copy = pltpu.make_async_copy(pool_ref, pool_v, pool_sem)
-    pool_copy.start()
     barrier = pltpu.get_barrier_semaphore()
     for distance in range(1, SPAN):
         pl.semaphore_signal(barrier, inc=1, device_id={"dp": peer(distance)}, device_id_type=MESH)
     for other in range(1, shards):
         pl.semaphore_signal(barrier, inc=1, device_id={"tensor": lax.rem(mine + other, shards)}, device_id_type=MESH)
+    in_copies = []
+    operands = ((par_hbm, par_ref), (q_hbm, q_ref), (new_hbm, new_ref), (table_hbm, table_ref), (len_hbm, len_ref))
+    for at, (source, target) in enumerate(operands):
+        copy = pltpu.make_async_copy(source, target, in_sem.at[at])
+        copy.start()
+        in_copies.append(copy)
+    pool_copy = pltpu.make_async_copy(pool_ref, pool_v, pool_sem)
+    pool_copy.start()
     for copy in in_copies:
         copy.wait()
 
@@ -335,7 +335,10 @@
                 collective_id=0, has_side_effects=True, vmem_limit_bytes=48 * 1024 * 1024
             ),
             name="exchange",
-        )(queries, new_kv, kv_pool, page_tables, lengths, parents, out_weight)
+        )(*(
+            pltpu.with_memory_space_constraint(operand, pltpu.HBM)
+            for operand in (queries, new_kv, kv_pool, page_tables, lengths, parents, out_weight)
+        ))
     with jax.named_scope("finish"):
         return pl.pallas_call(
             finish_kernel,

time: 63.6 us -> 59.9 us (0.942)
  local copies, waits for them, and re-layouts: 3.55 us -> 0.01 us
    unnamed x10 -> x6, local copies, waits for them, and re-layouts: 3.55 us -> 0.01 us
where the time goes in v3:
time: 59.9 us; the launch traced here: 59.4 us
  Pallas kernels  58.7 us (98%)
  between operations  0.69 us (1%)
    pallas_call x1, Pallas kernels, local(): pl.pallas_call(exchange_kernel, out_shape=(jax.ShapeDtypeStruct((SPAN, MO...  55.4 us
    pallas_call x1, Pallas kernels, local(): pl.pallas_call(finish_kernel, out_shape=(jax.ShapeDtypeStruct(queries.sha...  3.28 us

profile of v3, /device:TPU:0, one launch (start us, length us, event | category | flops | bytes accessed | tf_op | source)
XLA Modules:
  0.0 59.4 jit_solution(4831786971398981910)
XLA Ops:
  0.6 0.0 copy-start.2
  0.6 0.0 copy-start.1
  0.7 0.0 copy-start
  0.7 55.4 %exchange.1 = (bf16[4,2048,256]{2,1,0:T(8,128)(2,1)S(1)}, bf16[4,16,512]{2,1,0:T(8,128)(2,1)S(1)}) custom-call(bf16[4,8,1024]{2,1,0:T(8,128)(2,1)} %q_hbm.1, bf16[4,8,256]{2,1,0:T(8,128)(2,1)} %new_hbm.3, bf16[64,128,256]{2,1,0:T(8,128)(2,1)} %pool_ref.1, s32[8,8]{1,0:T(8,128)} %table_hbm.1, s32[128]{0:T(128)} %len_hbm.3, s32[128]{0:T(128)} %par_hbm.3, ...), custom_call_target="tpu_custom_call" | custom-call | tf_op jit(solution)/shard_map/exchange/exchange/pallas_call | solution.py:304
  56.1 0.0 copy-done.2
  56.1 0.0 copy-done.1
  56.1 0.0 copy-done
  56.1 3.3 %finish.1 = (bf16[4,8,1024]{2,1,0:T(8,128)(2,1)}, bf16[8,1024,256]{2,1,0:T(8,128)(2,1)}) custom-call(bf16[8,1024,256]{2,1,0:T(8,128)(2,1)S(1)} %bitcast.1, bf16[4,16,512]{2,1,0:T(8,128)(2,1)S(1)} %get-tuple-element.5.raw_ref, bf16[4,8,256]{2,1,0:T(8,128)(2,1)S(1)} %copy-done, s32[128]{0:T(128)S(1)} %copy-done.1, s32[128]{0:T(128)S(1)} %copy-done.2), custom_call_target="tpu_custom_call" | custom-call | tf_op jit(solution)/shard_map/finish/finish/pallas_call | solution.py:343
Async XLA Ops:
  0.6 55.5 %copy-start.2 = (s32[128]{0:T(128)S(1)}, s32[128]{0:T(128)}, u32[]{:S(2)}) copy-start(s32[128]{0:T(128)} %par_hbm.3) | copy-start | bytes 1540
  0.6 55.5 %copy-start.1 = (s32[128]{0:T(128)S(1)}, s32[128]{0:T(128)}, u32[]{:S(2)}) copy-start(s32[128]{0:T(128)} %len_hbm.3) | copy-start | bytes 1540
  0.7 55.5 %copy-start = (bf16[4,8,256]{2,1,0:T(8,128)(2,1)S(1)}, bf16[4,8,256]{2,1,0:T(8,128)(2,1)}, u32[]{:S(2)}) copy-start(bf16[4,8,256]{2,1,0:T(8,128)(2,1)} %new_hbm.3) | copy-start | bytes 49156

commit v4 on v3

--- a/solution.py
+++ b/solution.py
@@ -49,7 +49,7 @@
     recv_ref, proj_ref,
     q_ref, new_ref, table_ref, len_ref, par_ref,
     pool_v, w_v, stage, q_send, q_recv, att, p_send, p_recv, r_send, lens,
-    in_sem, pool_sem, w_sem, own_sem, qs_sem, qr_sem, bs_sem, br_sem, ps_sem, pr_sem, rs_sem, rr_sem,
+    in_sem, pool_sem, w_sem, own_sem, qs_sem, qr_sem, bs_sem, br_sem, ps_sem, pr_sem, rs_sem, rr_sem, here_sem,
 ):
     me = lax.axis_index("dp")
     mine = lax.axis_index("tensor")
@@ -68,7 +68,9 @@
     for distance in range(1, SPAN):
         pl.semaphore_signal(barrier, inc=1, device_id={"dp": peer(distance)}, device_id_type=MESH)
     for other in range(1, shards):
-        pl.semaphore_signal(barrier, inc=1, device_id={"tensor": lax.rem(mine + other, shards)}, device_id_type=MESH)
+        @pl.when(mine + other < shards)
+        def _(other=other):
+            pl.semaphore_signal(barrier, inc=1, device_id={"tensor": mine + other}, device_id_type=MESH)
     in_copies = []
     operands = ((par_hbm, par_ref), (q_hbm, q_ref), (new_hbm, new_ref), (table_hbm, table_ref), (len_hbm, len_ref))
     for at, (source, target) in enumerate(operands):
@@ -102,7 +104,11 @@
         else:
             q_send[distance] = part
 
-    pl.semaphore_wait(barrier, SPAN - 1 + shards - 1)
+    pl.semaphore_wait(barrier, SPAN - 1 + mine)
+    for other in range(1, shards):
+        @pl.when(mine >= other)
+        def _(other=other):
+            pl.semaphore_signal(here_sem, inc=1, device_id={"tensor": mine - other}, device_id_type=MESH)
 
     q_copies = []
     for distance in range(1, SPAN):
@@ -200,6 +206,10 @@
         p_send[other] = product.astype(jnp.bfloat16)
         p_copy(other).start()
         return carry
+
+    @pl.when(mine < shards - 1)
+    def _():
+        pl.semaphore_wait(here_sem, shards - 1 - mine)
 
     lax.fori_loop(1, shards, project, 0)
     own = jnp.dot(attended, w_v[mine], preferred_element_type=jnp.float32)
@@ -330,6 +340,7 @@
                 dma((SPAN * MOST,)), dma((SPAN * MOST,)),
                 dma((shards,)), dma((shards,)),
                 dma((SPAN,)), dma((SPAN,)),
+                pltpu.SemaphoreType.REGULAR,
             ],
             compiler_params=pltpu.CompilerParams(
                 collective_id=0, has_side_effects=True, vmem_limit_bytes=48 * 1024 * 1024

time: 59.9 us -> 57.8 us (0.965)
  Pallas kernels: 58.7 us -> 56.2 us
    pallas_call x1, Pallas kernels: 55.4 us -> 52.9 us  [local(): pl.pallas_call(exchange_kernel, out_shape=(jax.ShapeDtypeStruct((SPAN, MO...]
where the time goes in v4:
time: 57.8 us; the launch traced here: 56.9 us
  Pallas kernels  56.2 us (97%)
  between operations  0.69 us (1%)
    pallas_call x1, Pallas kernels, local(): pl.pallas_call(exchange_kernel, out_shape=(jax.ShapeDtypeStruct((SPAN, MO...  52.9 us
    pallas_call x1, Pallas kernels, local(): pl.pallas_call(finish_kernel, out_shape=(jax.ShapeDtypeStruct(queries.sha...  3.28 us

profile of v4, /device:TPU:0, one launch (start us, length us, event | category | flops | bytes accessed | tf_op | source)
XLA Modules:
  0.0 56.9 jit_solution(9793565405891520205)
XLA Ops:
  0.6 0.0 copy-start.2
  0.6 0.0 copy-start.1
  0.7 0.0 copy-start
  0.7 52.9 %exchange.1 = (bf16[4,2048,256]{2,1,0:T(8,128)(2,1)S(1)}, bf16[4,16,512]{2,1,0:T(8,128)(2,1)S(1)}) custom-call(bf16[4,8,1024]{2,1,0:T(8,128)(2,1)} %q_hbm.1, bf16[4,8,256]{2,1,0:T(8,128)(2,1)} %new_hbm.3, bf16[64,128,256]{2,1,0:T(8,128)(2,1)} %pool_ref.1, s32[8,8]{1,0:T(8,128)} %table_hbm.1, s32[128]{0:T(128)} %len_hbm.3, s32[128]{0:T(128)} %par_hbm.3, ...), custom_call_target="tpu_custom_call" | custom-call | tf_op jit(solution)/shard_map/exchange/exchange/pallas_call | solution.py:314
  53.6 0.0 copy-done.2
  53.6 0.0 copy-done.1
  53.6 0.0 copy-done
  53.6 3.3 %finish.1 = (bf16[4,8,1024]{2,1,0:T(8,128)(2,1)}, bf16[8,1024,256]{2,1,0:T(8,128)(2,1)}) custom-call(bf16[8,1024,256]{2,1,0:T(8,128)(2,1)S(1)} %bitcast.1, bf16[4,16,512]{2,1,0:T(8,128)(2,1)S(1)} %get-tuple-element.5.raw_ref, bf16[4,8,256]{2,1,0:T(8,128)(2,1)S(1)} %copy-done, s32[128]{0:T(128)S(1)} %copy-done.1, s32[128]{0:T(128)S(1)} %copy-done.2), custom_call_target="tpu_custom_call" | custom-call | tf_op jit(solution)/shard_map/finish/finish/pallas_call | solution.py:354
Async XLA Ops:
  0.6 52.9 %copy-start.2 = (s32[128]{0:T(128)S(1)}, s32[128]{0:T(128)}, u32[]{:S(2)}) copy-start(s32[128]{0:T(128)} %par_hbm.3) | copy-start | bytes 1540
  0.6 52.9 %copy-start.1 = (s32[128]{0:T(128)S(1)}, s32[128]{0:T(128)}, u32[]{:S(2)}) copy-start(s32[128]{0:T(128)} %len_hbm.3) | copy-start | bytes 1540
  0.7 52.9 %copy-start = (bf16[4,8,256]{2,1,0:T(8,128)(2,1)S(1)}, bf16[4,8,256]{2,1,0:T(8,128)(2,1)}, u32[]{:S(2)}) copy-start(bf16[4,8,256]{2,1,0:T(8,128)(2,1)} %new_hbm.3) | copy-start | bytes 49156

commit v5 on v4

--- a/solution.py
+++ b/solution.py
@@ -13,6 +13,8 @@
 BEAMS = 8
 STEPS = 4
 PAGE = 128
+CUTS = 4
+CUT = PAGE // CUTS
 MESH = pl.DeviceIdType.MESH
 
 
@@ -48,7 +50,7 @@
     q_hbm, new_hbm, pool_ref, table_hbm, len_hbm, par_hbm, w_ref,
     recv_ref, proj_ref,
     q_ref, new_ref, table_ref, len_ref, par_ref,
-    pool_v, w_v, stage, q_send, q_recv, att, p_send, p_recv, r_send, lens,
+    pool_0, pool_1, pool_2, pool_3, w_v, stage, q_send, q_recv, att, p_send, p_recv, r_send, lens, beams,
     in_sem, pool_sem, w_sem, own_sem, qs_sem, qr_sem, bs_sem, br_sem, ps_sem, pr_sem, rs_sem, rr_sem, here_sem,
 ):
     me = lax.axis_index("dp")
@@ -56,7 +58,9 @@
     shards = lax.axis_size("tensor")
     y = lax.rem(me, SPAN)
     base = me - y
-    context = stage.shape[1] // MOST
+    pages = stage.shape[1] // MOST
+    context = pages * PAGE
+    pools = (pool_0, pool_1, pool_2, pool_3)
     wide = q_hbm.shape[2]
     heads = wide // HD
     rows = MOST * STEPS
@@ -77,8 +81,11 @@
         copy = pltpu.make_async_copy(source, target, in_sem.at[at])
         copy.start()
         in_copies.append(copy)
-    pool_copy = pltpu.make_async_copy(pool_ref, pool_v, pool_sem)
-    pool_copy.start()
+    pool_copies = []
+    for cut in range(CUTS):
+        copy = pltpu.make_async_copy(pool_ref.at[:, pl.ds(cut * CUT, CUT), :], pools[cut], pool_sem.at[cut])
+        copy.start()
+        pool_copies.append(copy)
     for copy in in_copies:
         copy.wait()
 
@@ -120,40 +127,43 @@
         copy.start()
         q_copies.append(copy)
 
-    pool_copy.wait()
+    for distance in range(SPAN):
+        served = served_beams(par_ref, me, peer(SPAN - distance))
+        for rank in range(MOST):
+            beams[distance * MOST + rank] = served[rank]
+            lens[distance * MOST + rank] = len_ref[me * BEAMS + served[rank]]
+
+    def put(distance, cut):
+        def body(index, carry):
+            beam = beams[distance * MOST + index // pages]
+            stage[distance, index, pl.ds(cut * CUT, CUT), :] = pools[cut][table_ref[beam, lax.rem(index, pages)]]
+            return carry
+
+        lax.fori_loop(0, MOST * pages, body, 0)
+
+    b_copies = []
+    for cut in range(CUTS):
+        pool_copies[cut].wait()
+        rows_at = pl.ds(cut * CUT, CUT)
+        for distance in (2, 1, 3):
+            put(distance, cut)
+            copy = pltpu.make_async_remote_copy(
+                src_ref=stage.at[distance, :, rows_at], dst_ref=recv_ref.at[distance, :, rows_at],
+                send_sem=bs_sem.at[distance * CUTS + cut], recv_sem=br_sem.at[distance * CUTS + cut],
+                device_id={"dp": peer(SPAN - distance)}, device_id_type=MESH,
+            )
+            copy.start()
+            b_copies.append(copy)
     w_copies = []
     for block in range(shards):
         copy = pltpu.make_async_copy(w_ref.at[:, pl.ds(block * wide, wide)], w_v.at[block], w_sem.at[block])
         copy.start()
         w_copies.append(copy)
-    served = {}
-    for distance in range(SPAN):
-        served[distance] = served_beams(par_ref, me, peer(SPAN - distance))
-        for rank in range(MOST):
-            lens[distance * MOST + rank] = len_ref[me * BEAMS + served[distance][rank]]
-
-    b_copies = []
-    for rank in range(MOST):
-        for distance in (2, 1, 3, 0):
-            beam = served[distance][rank]
-
-            def put(index, carry, distance=distance, rank=rank, beam=beam):
-                at = pl.multiple_of(rank * context + index * PAGE, PAGE)
-                stage[distance, pl.ds(at, PAGE), :] = pool_v[table_ref[beam, index]]
-                return carry
-
-            lax.fori_loop(0, context // PAGE, put, 0)
-            span = pl.ds(rank * context, context)
-            if distance == 0:
-                copy = pltpu.make_async_copy(stage.at[0, span], recv_ref.at[0, span], own_sem.at[rank])
-            else:
-                copy = pltpu.make_async_remote_copy(
-                    src_ref=stage.at[distance, span], dst_ref=recv_ref.at[distance, span],
-                    send_sem=bs_sem.at[distance * MOST + rank], recv_sem=br_sem.at[distance * MOST + rank],
-                    device_id={"dp": peer(SPAN - distance)}, device_id_type=MESH,
-                )
-            copy.start()
-            b_copies.append(copy)
+    for cut in range(CUTS):
+        put(0, cut)
+    copy = pltpu.make_async_copy(stage.at[0], recv_ref.at[0], own_sem.at[0])
+    copy.start()
+    b_copies.append(copy)
 
     for copy in q_copies:
         copy.wait()
@@ -167,7 +177,7 @@
         last_len = lens[distance * MOST + 1]
         contract = (((1,), (1,)), ((), ()))
         scale = HD ** -0.5
-        scores = lax.dot_general(q_rows, stage[distance, :, 0:HD], contract, preferred_element_type=jnp.float32) * scale
+        scores = lax.dot_general(q_rows, stage[distance, :, :, 0:HD].reshape(MOST * context, HD), contract, preferred_element_type=jnp.float32) * scale
         fresh_scores = lax.dot_general(q_rows, fresh[:, :HD], contract, preferred_element_type=jnp.float32) * scale
         rank_at = lax.broadcasted_iota(jnp.int32, scores.shape, 0) // STEPS % MOST
         position = lax.broadcasted_iota(jnp.int32, scores.shape, 1) - rank_at * context
@@ -183,7 +193,7 @@
         total = jnp.sum(exp_old, axis=1, keepdims=True) + jnp.sum(exp_new, axis=1, keepdims=True)
         w_old = (exp_old / total).astype(jnp.bfloat16)
         w_new = (exp_new / total).astype(jnp.bfloat16)
-        out = jnp.dot(w_old, stage[distance, :, HD:2 * HD], preferred_element_type=jnp.float32)
+        out = jnp.dot(w_old, stage[distance, :, :, HD:2 * HD].reshape(MOST * context, HD), preferred_element_type=jnp.float32)
         out += jnp.dot(w_new, fresh[:, HD:], preferred_element_type=jnp.float32)
         out = jnp.concatenate([out[h * rows:(h + 1) * rows] for h in range(heads)], axis=1)
         att[pl.ds(pl.multiple_of(distance * rows, rows), rows), :] = out
@@ -225,7 +235,7 @@
         part = summed[distance * rows:(distance + 1) * rows]
         r_send[distance] = jnp.concatenate([part[:, :half], part[:, half:]], axis=0).astype(jnp.bfloat16)
         if distance == 0:
-            copy = pltpu.make_async_copy(r_send.at[0], proj_ref.at[0], own_sem.at[MOST])
+            copy = pltpu.make_async_copy(r_send.at[0], proj_ref.at[0], own_sem.at[1])
         else:
             copy = pltpu.make_async_remote_copy(
                 src_ref=r_send.at[distance], dst_ref=proj_ref.at[distance],
@@ -242,7 +252,7 @@
 
 def finish_kernel(recv_ref, raw_ref, new_hbm, len_hbm, par_hbm, proj_ref, cache_ref, new_ref, len_ref, par_ref, edge, zeros, in_sem, out_sem):
     me = lax.axis_index("dp")
-    pages = recv_ref.shape[1] // PAGE
+    pages = recv_ref.shape[1]
     operands = ((par_hbm, par_ref), (len_hbm, len_ref), (new_hbm, new_ref))
     in_copies = [pltpu.make_async_copy(source, target, in_sem.at[at]) for at, (source, target) in enumerate(operands)]
     for copy in in_copies:
@@ -251,7 +261,8 @@
     for copy in in_copies:
         copy.wait()
     slots, owners = slots_of_children(par_ref, me)
-    fresh = [new_ref[step].astype(jnp.float32) for step in range(STEPS)]
+    fresh = jnp.concatenate([new_ref[step].astype(jnp.float32) for step in range(STEPS)], axis=0).astype(jnp.bfloat16)
+    fresh_row = lax.broadcasted_iota(jnp.int32, (PAGE, STEPS * BEAMS), 1)
     for child in range(BEAMS):
         slot = slots[child]
         length = len_ref[owners[child]]
@@ -259,24 +270,22 @@
         last = (length + STEPS - 1) // PAGE
 
         def whole(index, carry, child=child, slot=slot):
-            span = pl.ds(pl.multiple_of(index * PAGE, PAGE), PAGE)
-            pltpu.make_async_copy(recv_ref.at[slot, span], cache_ref.at[child, span], out_sem).start()
+            pltpu.make_async_copy(recv_ref.at[slot, index], cache_ref.at[child, index], out_sem).start()
             return carry
 
         def clear(index, carry, child=child):
-            span = pl.ds(pl.multiple_of(index * PAGE, PAGE), PAGE)
-            pltpu.make_async_copy(zeros, cache_ref.at[child, span], out_sem).start()
+            pltpu.make_async_copy(zeros, cache_ref.at[child, index], out_sem).start()
             return carry
 
         def fix(index, carry, child=child, slot=slot, length=length, first=first):
-            at = pl.multiple_of(index * PAGE, PAGE)
-            position = at + lax.broadcasted_iota(jnp.int32, (PAGE, 2 * HD), 0)
-            page = recv_ref[slot, pl.ds(at, PAGE), :].astype(jnp.float32)
-            page = jnp.where(position < length, page, 0.0)
-            for step in range(STEPS):
-                page = jnp.where(position == length + step, fresh[step][child:child + 1], page)
-            edge[child * 2 + index - first] = page.astype(jnp.bfloat16)
-            pltpu.make_async_copy(edge.at[child * 2 + index - first], cache_ref.at[child, pl.ds(at, PAGE)], out_sem).start()
+            position = index * PAGE + lax.broadcasted_iota(jnp.int32, (PAGE, 2 * HD), 0)
+            behind = index * PAGE - length + lax.broadcasted_iota(jnp.int32, (PAGE, STEPS * BEAMS), 0)
+            pick = jnp.where((fresh_row // BEAMS == behind) & (fresh_row % BEAMS == child), 1.0, 0.0).astype(jnp.bfloat16)
+            added = jnp.dot(pick, fresh, preferred_element_type=jnp.float32)
+            page = jnp.where(position < length, recv_ref[slot, index].astype(jnp.float32), added)
+            at = child * 2 + index - first
+            edge[at] = page.astype(jnp.bfloat16)
+            pltpu.make_async_copy(edge.at[at], cache_ref.at[child, index], out_sem).start()
             return carry
 
         lax.fori_loop(0, first, whole, 0)
@@ -303,7 +312,7 @@
 def local(shards, queries, new_kv, kv_pool, page_tables, lengths, parents, out_weight):
     wide = queries.shape[2]
     channels = kv_pool.shape[2]
-    context = page_tables.shape[1] * kv_pool.shape[1]
+    pages = page_tables.shape[1]
     rows = MOST * STEPS
     vmem = pl.BlockSpec(memory_space=pltpu.VMEM)
     hbm = pl.BlockSpec(memory_space=pltpu.HBM)
@@ -314,7 +323,7 @@
         recv, raw = pl.pallas_call(
             exchange_kernel,
             out_shape=(
-                jax.ShapeDtypeStruct((SPAN, MOST * context, channels), bf16),
+                jax.ShapeDtypeStruct((SPAN, MOST * pages, PAGE, channels), bf16),
                 jax.ShapeDtypeStruct((SPAN, 2 * rows, wide // 2), bf16),
             ),
             in_specs=[hbm] * 7,
@@ -325,9 +334,9 @@
                 pltpu.SMEM(page_tables.shape, jnp.int32),
                 pltpu.SMEM(lengths.shape, jnp.int32),
                 pltpu.SMEM(parents.shape, jnp.int32),
-                pltpu.VMEM(kv_pool.shape, bf16),
+                *[pltpu.VMEM((kv_pool.shape[0], CUT, channels), bf16) for _ in range(CUTS)],
                 pltpu.VMEM((shards, out_weight.shape[0], wide), bf16),
-                pltpu.VMEM((SPAN, MOST * context, channels), bf16),
+                pltpu.VMEM((SPAN, MOST * pages, PAGE, channels), bf16),
                 pltpu.VMEM((SPAN, 2 * rows, (wide + channels) // 2), bf16),
                 pltpu.VMEM((SPAN, 2 * rows, (wide + channels) // 2), bf16),
                 pltpu.VMEM((SPAN * rows, wide), jnp.float32),
@@ -335,9 +344,10 @@
                 pltpu.VMEM((shards, SPAN * rows, wide), bf16),
                 pltpu.VMEM((SPAN, 2 * rows, wide // 2), bf16),
                 pltpu.SMEM((SPAN * MOST,), jnp.int32),
-                dma((5,)), dma, dma((shards,)), dma((MOST + 1,)),
+                pltpu.SMEM((SPAN * MOST,), jnp.int32),
+                dma((5,)), dma((CUTS,)), dma((shards,)), dma((2,)),
                 dma((SPAN,)), dma((SPAN,)),
-                dma((SPAN * MOST,)), dma((SPAN * MOST,)),
+                dma((SPAN * CUTS,)), dma((SPAN * CUTS,)),
                 dma((shards,)), dma((shards,)),
                 dma((SPAN,)), dma((SPAN,)),
                 pltpu.SemaphoreType.REGULAR,
@@ -351,11 +361,11 @@
             for operand in (queries, new_kv, kv_pool, page_tables, lengths, parents, out_weight)
         ))
     with jax.named_scope("finish"):
-        return pl.pallas_call(
+        projected, cache = pl.pallas_call(
             finish_kernel,
             out_shape=(
                 jax.ShapeDtypeStruct(queries.shape, bf16),
-                jax.ShapeDtypeStruct((BEAMS, context, channels), bf16),
+                jax.ShapeDtypeStruct((BEAMS, pages, PAGE, channels), bf16),
             ),
             in_specs=[vmem, vmem, hbm, hbm, hbm],
             out_specs=(vmem, hbm),
@@ -369,7 +379,8 @@
             ],
             compiler_params=pltpu.CompilerParams(vmem_limit_bytes=24 * 1024 * 1024),
             name="finish",
-        )(recv.reshape(BEAMS, context, channels), raw, new_kv, lengths, parents)
+        )(recv.reshape(BEAMS, pages, PAGE, channels), raw, new_kv, lengths, parents)
+        return projected, cache.reshape(BEAMS, pages * PAGE, channels)
 
 
 def solution(mesh):

time: 57.8 us -> 58.5 us (1.012)
  Pallas kernels: 56.2 us -> 57 us
where the time goes in v5:
time: 58.5 us; the launch traced here: 57.7 us
  Pallas kernels  57 us (97%)
  between operations  0.69 us (1%)
    pallas_call x1, Pallas kernels, local(): pl.pallas_call(exchange_kernel, out_shape=(jax.ShapeDtypeStruct((SPAN, MO...  53.4 us
    pallas_call x1, Pallas kernels, local(): pl.pallas_call(finish_kernel, out_shape=(jax.ShapeDtypeStruct(queries.sha...  3.54 us

profile of v5, /device:TPU:0, one launch (start us, length us, event | category | flops | bytes accessed | tf_op | source)
XLA Modules:
  0.0 57.7 jit_solution(17427794467376158653)
XLA Ops:
  0.6 0.0 copy-start.2
  0.6 0.0 copy-start.1
  0.7 0.0 copy-start
  0.7 53.4 %exchange.1 = (bf16[4,16,128,256]{3,2,1,0:T(8,128)(2,1)S(1)}, bf16[4,16,512]{2,1,0:T(8,128)(2,1)S(1)}) custom-call(bf16[4,8,1024]{2,1,0:T(8,128)(2,1)} %q_hbm.1, bf16[4,8,256]{2,1,0:T(8,128)(2,1)} %new_hbm.3, bf16[64,128,256]{2,1,0:T(8,128)(2,1)} %pool_ref.1, s32[8,8]{1,0:T(8,128)} %table_hbm.1, s32[128]{0:T(128)} %len_hbm.3, s32[128]{0:T(128)} %par_hbm.3, ...), custom_call_target="tpu_custom_call" | custom-call | tf_op jit(solution)/shard_map/exchange/exchange/pallas_call | solution.py:323
  54.1 0.0 copy-done.2
  54.1 0.0 copy-done.1
  54.1 0.0 copy-done
  54.1 3.5 %finish.1 = (bf16[4,8,1024]{2,1,0:T(8,128)(2,1)}, bf16[8,8,128,256]{3,2,1,0:T(8,128)(2,1)}) custom-call(bf16[8,8,128,256]{3,2,1,0:T(8,128)(2,1)S(1)} %bitcast.2, bf16[4,16,512]{2,1,0:T(8,128)(2,1)S(1)} %get-tuple-element.7.raw_ref, bf16[4,8,256]{2,1,0:T(8,128)(2,1)S(1)} %copy-done, s32[128]{0:T(128)S(1)} %copy-done.1, s32[128]{0:T(128)S(1)} %copy-done.2), custom_call_target="tpu_custom_call" | custom-call | tf_op jit(solution)/shard_map/finish/finish/pallas_call | solution.py:364
Async XLA Ops:
  0.6 53.5 %copy-start.2 = (s32[128]{0:T(128)S(1)}, s32[128]{0:T(128)}, u32[]{:S(2)}) copy-start(s32[128]{0:T(128)} %par_hbm.3) | copy-start | bytes 1540
  0.6 53.5 %copy-start.1 = (s32[128]{0:T(128)S(1)}, s32[128]{0:T(128)}, u32[]{:S(2)}) copy-start(s32[128]{0:T(128)} %len_hbm.3) | copy-start | bytes 1540
  0.7 53.5 %copy-start = (bf16[4,8,256]{2,1,0:T(8,128)(2,1)S(1)}, bf16[4,8,256]{2,1,0:T(8,128)(2,1)}, u32[]{:S(2)}) copy-start(bf16[4,8,256]{2,1,0:T(8,128)(2,1)} %new_hbm.3) | copy-start | bytes 49156

commit v6 on v4

--- a/solution.py
+++ b/solution.py
@@ -132,7 +132,8 @@
         for rank in range(MOST):
             lens[distance * MOST + rank] = len_ref[me * BEAMS + served[distance][rank]]
 
-    b_copies = []
+    b_copies, late = [], []
+    half = context // 2
     for rank in range(MOST):
         for distance in (2, 1, 3, 0):
             beam = served[distance][rank]
@@ -143,17 +144,22 @@
                 return carry
 
             lax.fori_loop(0, context // PAGE, put, 0)
-            span = pl.ds(rank * context, context)
-            if distance == 0:
-                copy = pltpu.make_async_copy(stage.at[0, span], recv_ref.at[0, span], own_sem.at[rank])
-            else:
-                copy = pltpu.make_async_remote_copy(
-                    src_ref=stage.at[distance, span], dst_ref=recv_ref.at[distance, span],
-                    send_sem=bs_sem.at[distance * MOST + rank], recv_sem=br_sem.at[distance * MOST + rank],
-                    device_id={"dp": peer(SPAN - distance)}, device_id_type=MESH,
-                )
-            copy.start()
-            b_copies.append(copy)
+            for part in range(2):
+                span = pl.ds(rank * context + part * half, half)
+                at = (distance * MOST + rank) * 2 + part
+                if distance == 0:
+                    copy = pltpu.make_async_copy(stage.at[0, span], recv_ref.at[0, span], bs_sem.at[at])
+                else:
+                    copy = pltpu.make_async_remote_copy(
+                        src_ref=stage.at[distance, span], dst_ref=recv_ref.at[distance, span],
+                        send_sem=bs_sem.at[at], recv_sem=br_sem.at[at],
+                        device_id={"dp": peer(SPAN - distance)}, device_id_type=MESH,
+                    )
+                b_copies.append(copy)
+                if distance > 0 and rank == MOST - 1 and part == 1:
+                    late.append(copy)
+                else:
+                    copy.start()
 
     for copy in q_copies:
         copy.wait()
@@ -225,7 +231,7 @@
         part = summed[distance * rows:(distance + 1) * rows]
         r_send[distance] = jnp.concatenate([part[:, :half], part[:, half:]], axis=0).astype(jnp.bfloat16)
         if distance == 0:
-            copy = pltpu.make_async_copy(r_send.at[0], proj_ref.at[0], own_sem.at[MOST])
+            copy = pltpu.make_async_copy(r_send.at[0], proj_ref.at[0], own_sem)
         else:
             copy = pltpu.make_async_remote_copy(
                 src_ref=r_send.at[distance], dst_ref=proj_ref.at[distance],
@@ -234,6 +240,8 @@
             )
         copy.start()
         r_copies.append(copy)
+    for copy in late:
+        copy.start()
     for copy in r_copies:
         copy.wait()
     for copy in b_copies:
@@ -335,9 +343,9 @@
                 pltpu.VMEM((shards, SPAN * rows, wide), bf16),
                 pltpu.VMEM((SPAN, 2 * rows, wide // 2), bf16),
                 pltpu.SMEM((SPAN * MOST,), jnp.int32),
-                dma((5,)), dma, dma((shards,)), dma((MOST + 1,)),
+                dma((5,)), dma, dma((shards,)), dma,
                 dma((SPAN,)), dma((SPAN,)),
-                dma((SPAN * MOST,)), dma((SPAN * MOST,)),
+                dma((SPAN * MOST * 2,)), dma((SPAN * MOST * 2,)),
                 dma((shards,)), dma((shards,)),
                 dma((SPAN,)), dma((SPAN,)),
                 pltpu.SemaphoreType.REGULAR,

time: 57.8 us -> 58 us (level)
  no operation moved by 1% of the time
where the time goes in v6:
time: 58 us; the launch traced here: 57 us
  Pallas kernels  56.3 us (97%)
  between operations  0.69 us (1%)
    pallas_call x1, Pallas kernels, local(): pl.pallas_call(exchange_kernel, out_shape=(jax.ShapeDtypeStruct((SPAN, MO...  53 us
    pallas_call x1, Pallas kernels, local(): pl.pallas_call(finish_kernel, out_shape=(jax.ShapeDtypeStruct(queries.sha...  3.28 us

profile of v6, /device:TPU:0, one launch (start us, length us, event | category | flops | bytes accessed | tf_op | source)
XLA Modules:
  0.0 57.0 jit_solution(3639780119549014776)
XLA Ops:
  0.6 0.0 copy-start.2
  0.6 0.0 copy-start.1
  0.7 0.0 copy-start
  0.7 53.0 %exchange.1 = (bf16[4,2048,256]{2,1,0:T(8,128)(2,1)S(1)}, bf16[4,16,512]{2,1,0:T(8,128)(2,1)S(1)}) custom-call(bf16[4,8,1024]{2,1,0:T(8,128)(2,1)} %q_hbm.1, bf16[4,8,256]{2,1,0:T(8,128)(2,1)} %new_hbm.3, bf16[64,128,256]{2,1,0:T(8,128)(2,1)} %pool_ref.1, s32[8,8]{1,0:T(8,128)} %table_hbm.1, s32[128]{0:T(128)} %len_hbm.3, s32[128]{0:T(128)} %par_hbm.3, ...), custom_call_target="tpu_custom_call" | custom-call | tf_op jit(solution)/shard_map/exchange/exchange/pallas_call | solution.py:322
  53.7 0.0 copy-done.2
  53.7 0.0 copy-done.1
  53.7 0.0 copy-done
  53.7 3.3 %finish.1 = (bf16[4,8,1024]{2,1,0:T(8,128)(2,1)}, bf16[8,1024,256]{2,1,0:T(8,128)(2,1)}) custom-call(bf16[8,1024,256]{2,1,0:T(8,128)(2,1)S(1)} %bitcast.1, bf16[4,16,512]{2,1,0:T(8,128)(2,1)S(1)} %get-tuple-element.5.raw_ref, bf16[4,8,256]{2,1,0:T(8,128)(2,1)S(1)} %copy-done, s32[128]{0:T(128)S(1)} %copy-done.1, s32[128]{0:T(128)S(1)} %copy-done.2), custom_call_target="tpu_custom_call" | custom-call | tf_op jit(solution)/shard_map/finish/finish/pallas_call | solution.py:362
Async XLA Ops:
  0.6 53.0 %copy-start.2 = (s32[128]{0:T(128)S(1)}, s32[128]{0:T(128)}, u32[]{:S(2)}) copy-start(s32[128]{0:T(128)} %par_hbm.3) | copy-start | bytes 1540
  0.6 53.0 %copy-start.1 = (s32[128]{0:T(128)S(1)}, s32[128]{0:T(128)}, u32[]{:S(2)}) copy-start(s32[128]{0:T(128)} %len_hbm.3) | copy-start | bytes 1540
  0.7 53.0 %copy-start = (bf16[4,8,256]{2,1,0:T(8,128)(2,1)S(1)}, bf16[4,8,256]{2,1,0:T(8,128)(2,1)}, u32[]{:S(2)}) copy-start(bf16[4,8,256]{2,1,0:T(8,128)(2,1)} %new_hbm.3) | copy-start | bytes 49156

commit v7 on v4

--- a/solution.py
+++ b/solution.py
@@ -13,7 +13,65 @@
 BEAMS = 8
 STEPS = 4
 PAGE = 128
+GRAIN = 64
+PER_CHILD = 16
+VIA = 20
+MORE = 8
+REST = 25
+FIRST = VIA + MORE
+LINK = FIRST + REST
 MESH = pl.DeviceIdType.MESH
+
+
+def grains(length):
+    return (length + (GRAIN - 1)) >> 6
+
+
+def choose(values, index):
+    out = values[0]
+    for at in range(1, len(values)):
+        out = jnp.where(index == at, values[at], out)
+    return out
+
+
+def ring_plan(parents, lengths, ring):
+    flows = [[jnp.int32(0)] * SPAN for _ in range(SPAN)]
+    for target in range(SPAN):
+        seen = []
+        for child in range(BEAMS):
+            parent = parents[(ring * SPAN + target) * BEAMS + child]
+            count = grains(lengths[parent])
+            for other in seen:
+                count = jnp.where(parent == other, 0, count)
+            seen.append(parent)
+            source = (parent >> 3) & (SPAN - 1)
+            for at in range(SPAN):
+                if at != target:
+                    ahead = (target - at) % SPAN
+                    flows[at][ahead] = flows[at][ahead] + jnp.where(source == at, count, 0)
+    up = [flow[1] for flow in flows]
+    far = [flow[2] for flow in flows]
+    down = [flow[3] for flow in flows]
+    via_up = [jnp.minimum(count >> 1, VIA) for count in far]
+    for at in range(SPAN):
+        via_down = [far[i] - via_up[i] for i in range(SPAN)]
+        nxt, prv = (at + 1) % SPAN, (at - 1) % SPAN
+        load_up = jnp.maximum(up[at] + via_up[prv], up[nxt] + via_up[nxt])
+        load_down = jnp.maximum(down[at] + via_down[nxt], down[prv] + via_down[prv])
+        best = (load_down + far[at] - load_up) >> 1
+        via_up[at] = jnp.minimum(jnp.maximum(best, jnp.maximum(far[at] - VIA, 0)), jnp.minimum(far[at], VIA))
+    via_down = [far[i] - via_up[i] for i in range(SPAN)]
+    return up, down, via_up, via_down
+
+
+def overfull(plan):
+    up, down, via_up, via_down = plan
+    out = jnp.int32(0)
+    for at in range(SPAN):
+        load_up = up[at] + via_up[at] + via_up[(at - 1) % SPAN]
+        load_down = down[at] + via_down[at] + via_down[(at + 1) % SPAN]
+        out = jnp.maximum(out, jnp.where(jnp.maximum(load_up, load_down) > LINK, 1, 0))
+    return out
 
 
 def slots_of_children(parents, me):
@@ -46,17 +104,18 @@
 
 def exchange_kernel(
     q_hbm, new_hbm, pool_ref, table_hbm, len_hbm, par_hbm, w_ref,
-    recv_ref, proj_ref,
+    recv_ref, proj_ref, meta_ref, over_ref,
     q_ref, new_ref, table_ref, len_ref, par_ref,
-    pool_v, w_v, stage, q_send, q_recv, att, p_send, p_recv, r_send, lens,
-    in_sem, pool_sem, w_sem, own_sem, qs_sem, qr_sem, bs_sem, br_sem, ps_sem, pr_sem, rs_sem, rr_sem, here_sem,
+    pool_v, w_v, stage, first_send, first_recv, rest_send, q_send, q_recv, att, p_send, p_recv, r_send, lens, beams,
+    in_sem, pool_sem, w_sem, own_sem, land_sem, qs_sem, qr_sem, bs_sem, br_sem, ps_sem, pr_sem, rs_sem, rr_sem, here_sem,
 ):
     me = lax.axis_index("dp")
     mine = lax.axis_index("tensor")
     shards = lax.axis_size("tensor")
     y = lax.rem(me, SPAN)
     base = me - y
-    context = stage.shape[1] // MOST
+    context = stage.shape[1] * GRAIN // MOST
+    rings = lax.axis_size("dp") // SPAN
     wide = q_hbm.shape[2]
     heads = wide // HD
     rows = MOST * STEPS
@@ -82,7 +141,9 @@
     for copy in in_copies:
         copy.wait()
 
-    slots, _ = slots_of_children(par_ref, me)
+    slots, owners = slots_of_children(par_ref, me)
+    plan = ring_plan(par_ref, len_ref, me >> 2)
+    up, down, via_up, via_down = plan
     row = lax.broadcasted_iota(jnp.int32, (SPAN * rows, BEAMS), 0)
     col = lax.broadcasted_iota(jnp.int32, (SPAN * rows, BEAMS), 1)
     slot_at = jnp.zeros_like(col)
@@ -120,40 +181,64 @@
         copy.start()
         q_copies.append(copy)
 
+    flows = {}
+    for ahead in range(SPAN):
+        served = served_beams(par_ref, me, peer(ahead))
+        distance = (SPAN - ahead) % SPAN
+        held = [len_ref[me * BEAMS + served[rank]] for rank in range(MOST)]
+        for rank in range(MOST):
+            beams[distance * MOST + rank] = served[rank]
+            lens[distance * MOST + rank] = held[rank]
+        flows[ahead] = (served[0], served[1], grains(held[0]))
+
+    def grain_at(flow, number):
+        first, second, cut = flow
+        later = number >= cut
+        number = jnp.where(later, number - cut, number)
+        number = jnp.minimum(jnp.maximum(number, 0), PER_CHILD - 1)
+        return table_ref[jnp.where(later, second, first), number >> 1] * 2 + (number & 1)
+
+    sides = (
+        (flows[1], choose(via_up, y), jnp.int32(0), choose(via_up, (y - 1) & 3), peer(1)),
+        (flows[3], choose(via_down, y), choose(via_up, y), choose(via_down, (y + 1) & 3), peer(3)),
+    )
     pool_copy.wait()
+    b_copies = []
+    cuts = (0, VIA // 2, VIA, FIRST)
+    for part in range(3):
+        for side, (flow, mine_via, skip, _, target) in enumerate(sides):
+            def put(at, carry, side=side, flow=flow, mine_via=mine_via, skip=skip):
+                far = at < mine_via
+                chosen = tuple(jnp.where(far, one, two) for one, two in zip(flows[2], flow))
+                number = jnp.where(far, skip + at, at - mine_via)
+                first_send[side, at] = pool_v[grain_at(chosen, number)]
+                return carry
+
+            lax.fori_loop(cuts[part], cuts[part + 1], put, 0)
+            span = pl.ds(cuts[part], cuts[part + 1] - cuts[part])
+            copy = pltpu.make_async_remote_copy(
+                src_ref=first_send.at[side, span], dst_ref=first_recv.at[side, span],
+                send_sem=bs_sem.at[side * 4 + part], recv_sem=br_sem.at[side * 4 + part],
+                device_id={"dp": target}, device_id_type=MESH,
+            )
+            copy.start()
+            b_copies.append(copy)
     w_copies = []
     for block in range(shards):
         copy = pltpu.make_async_copy(w_ref.at[:, pl.ds(block * wide, wide)], w_v.at[block], w_sem.at[block])
         copy.start()
         w_copies.append(copy)
-    served = {}
-    for distance in range(SPAN):
-        served[distance] = served_beams(par_ref, me, peer(SPAN - distance))
-        for rank in range(MOST):
-            lens[distance * MOST + rank] = len_ref[me * BEAMS + served[distance][rank]]
-
-    b_copies = []
-    for rank in range(MOST):
-        for distance in (2, 1, 3, 0):
-            beam = served[distance][rank]
-
-            def put(index, carry, distance=distance, rank=rank, beam=beam):
-                at = pl.multiple_of(rank * context + index * PAGE, PAGE)
-                stage[distance, pl.ds(at, PAGE), :] = pool_v[table_ref[beam, index]]
-                return carry
-
-            lax.fori_loop(0, context // PAGE, put, 0)
-            span = pl.ds(rank * context, context)
-            if distance == 0:
-                copy = pltpu.make_async_copy(stage.at[0, span], recv_ref.at[0, span], own_sem.at[rank])
-            else:
-                copy = pltpu.make_async_remote_copy(
-                    src_ref=stage.at[distance, span], dst_ref=recv_ref.at[distance, span],
-                    send_sem=bs_sem.at[distance * MOST + rank], recv_sem=br_sem.at[distance * MOST + rank],
-                    device_id={"dp": peer(SPAN - distance)}, device_id_type=MESH,
-                )
-            copy.start()
-            b_copies.append(copy)
+
+    def put_all(index, carry):
+        slot = index >> 4
+        number = index & (PER_CHILD - 1)
+        grain = table_ref[beams[slot], number >> 1] * 2 + (number & 1)
+        stage[index >> 5, index & (MOST * PER_CHILD - 1)] = pool_v[grain]
+        return carry
+
+    lax.fori_loop(0, SPAN * MOST * PER_CHILD, put_all, 0)
+    own_copy = pltpu.make_async_copy(stage.at[0], recv_ref.at[pl.ds(2 * LINK, MOST * PER_CHILD)], own_sem.at[0])
+    own_copy.start()
 
     for copy in q_copies:
         copy.wait()
@@ -167,7 +252,7 @@
         last_len = lens[distance * MOST + 1]
         contract = (((1,), (1,)), ((), ()))
         scale = HD ** -0.5
-        scores = lax.dot_general(q_rows, stage[distance, :, 0:HD], contract, preferred_element_type=jnp.float32) * scale
+        scores = lax.dot_general(q_rows, stage[distance, :, :, 0:HD].reshape(MOST * context, HD), contract, preferred_element_type=jnp.float32) * scale
         fresh_scores = lax.dot_general(q_rows, fresh[:, :HD], contract, preferred_element_type=jnp.float32) * scale
         rank_at = lax.broadcasted_iota(jnp.int32, scores.shape, 0) // STEPS % MOST
         position = lax.broadcasted_iota(jnp.int32, scores.shape, 1) - rank_at * context
@@ -183,13 +268,35 @@
         total = jnp.sum(exp_old, axis=1, keepdims=True) + jnp.sum(exp_new, axis=1, keepdims=True)
         w_old = (exp_old / total).astype(jnp.bfloat16)
         w_new = (exp_new / total).astype(jnp.bfloat16)
-        out = jnp.dot(w_old, stage[distance, :, HD:2 * HD], preferred_element_type=jnp.float32)
+        out = jnp.dot(w_old, stage[distance, :, :, HD:2 * HD].reshape(MOST * context, HD), preferred_element_type=jnp.float32)
         out += jnp.dot(w_new, fresh[:, HD:], preferred_element_type=jnp.float32)
         out = jnp.concatenate([out[h * rows:(h + 1) * rows] for h in range(heads)], axis=1)
         att[pl.ds(pl.multiple_of(distance * rows, rows), rows), :] = out
         return carry
 
     lax.fori_loop(0, SPAN, attend, 0)
+    for copy in b_copies:
+        copy.wait()
+    b_copies = []
+    for side, (flow, mine_via, _, passed, target) in enumerate(sides):
+        copy = pltpu.make_async_copy(first_recv.at[side], recv_ref.at[pl.ds(side * LINK, FIRST)], land_sem.at[side])
+        copy.start()
+        b_copies.append(copy)
+
+        def put_rest(at, carry, side=side, flow=flow, mine_via=mine_via, passed=passed):
+            number = FIRST - mine_via + at - passed
+            here = pool_v[grain_at(flow, number)]
+            rest_send[side, at] = jnp.where(at < passed, first_recv[side, jnp.minimum(at, VIA - 1)], here)
+            return carry
+
+        lax.fori_loop(0, REST, put_rest, 0)
+        copy = pltpu.make_async_remote_copy(
+            src_ref=rest_send.at[side], dst_ref=recv_ref.at[pl.ds(side * LINK + FIRST, REST)],
+            send_sem=bs_sem.at[side * 4 + 3], recv_sem=br_sem.at[side * 4 + 3],
+            device_id={"dp": target}, device_id_type=MESH,
+        )
+        copy.start()
+        b_copies.append(copy)
     attended = att[...].astype(jnp.bfloat16)
     for copy in w_copies:
         copy.wait()
@@ -225,7 +332,7 @@
         part = summed[distance * rows:(distance + 1) * rows]
         r_send[distance] = jnp.concatenate([part[:, :half], part[:, half:]], axis=0).astype(jnp.bfloat16)
         if distance == 0:
-            copy = pltpu.make_async_copy(r_send.at[0], proj_ref.at[0], own_sem.at[MOST])
+            copy = pltpu.make_async_copy(r_send.at[0], proj_ref.at[0], own_sem.at[1])
         else:
             copy = pltpu.make_async_remote_copy(
                 src_ref=r_send.at[distance], dst_ref=proj_ref.at[distance],
@@ -234,9 +341,94 @@
             )
         copy.start()
         r_copies.append(copy)
+
+    over_ref[0] = lax.fori_loop(
+        0, rings, lambda ring, over: jnp.maximum(over, overfull(ring_plan(par_ref, len_ref, ring))), jnp.int32(0)
+    )
+    for child in range(BEAMS):
+        slot = slots[child]
+        distance = slot >> 1
+        length = len_ref[owners[child]]
+        count = grains(length)
+        before = jnp.int32(0)
+        for other in range(BEAMS):
+            if other != child:
+                mate = (slots[other] >> 1 == distance) & (slots[other] < slot)
+                differs = owners[other] != owners[child]
+                before = jnp.where(mate & differs, grains(len_ref[owners[other]]), before)
+        from_up = choose(via_up, (y - 1) & 3), choose(via_up, (y + 2) & 3)
+        from_down = choose(via_down, (y + 1) & 3), choose(via_down, (y + 2) & 3)
+        near_via = jnp.where(distance == 3, from_up[0], from_down[0])
+        near_pass = jnp.where(distance == 3, from_up[1], from_down[1])
+        near_base = jnp.where(distance == 3, 0, LINK)
+        split = jnp.where(distance == 2, from_up[1], FIRST - near_via) - before
+        split = jnp.minimum(jnp.maximum(split, 0), PER_CHILD)
+        start = jnp.where(distance == 2, FIRST + before, near_base + near_via + before)
+        again = jnp.where(distance == 2, LINK + FIRST + before + split - from_up[1], start + split + near_pass)
+        own = distance == 0
+        meta_ref[child * 4] = length
+        meta_ref[child * 4 + 1] = jnp.where(own, 2 * LINK + (slot & 1) * PER_CHILD, start)
+        meta_ref[child * 4 + 2] = jnp.where(own, PER_CHILD, split)
+        meta_ref[child * 4 + 3] = jnp.where(own, 0, again)
+        meta_ref[BEAMS * 4 + child] = slot
     for copy in r_copies:
         copy.wait()
     for copy in b_copies:
+        copy.wait()
+    own_copy.wait()
+
+
+def full_kernel(
+    pool_ref, table_hbm, par_hbm, recv_ref,
+    table_ref, par_ref, pool_v, stage,
+    in_sem, pool_sem, own_sem, bs_sem, br_sem,
+):
+    me = lax.axis_index("dp")
+    y = lax.rem(me, SPAN)
+    base = me - y
+    context = stage.shape[1] // MOST
+
+    def peer(distance):
+        return base + lax.rem(y + distance, SPAN)
+
+    barrier = pltpu.get_barrier_semaphore()
+    for distance in range(1, SPAN):
+        pl.semaphore_signal(barrier, inc=1, device_id={"dp": peer(distance)}, device_id_type=MESH)
+    in_copies = []
+    for at, (source, target) in enumerate(((par_hbm, par_ref), (table_hbm, table_ref))):
+        copy = pltpu.make_async_copy(source, target, in_sem.at[at])
+        copy.start()
+        in_copies.append(copy)
+    pool_copy = pltpu.make_async_copy(pool_ref, pool_v, pool_sem)
+    pool_copy.start()
+    for copy in in_copies:
+        copy.wait()
+    pl.semaphore_wait(barrier, SPAN - 1)
+    pool_copy.wait()
+    copies = []
+    for distance in (2, 1, 3, 0):
+        served = served_beams(par_ref, me, peer(SPAN - distance))
+        for rank in range(MOST):
+            beam = served[rank]
+
+            def put(index, carry, distance=distance, rank=rank, beam=beam):
+                at = pl.multiple_of(rank * context + index * PAGE, PAGE)
+                stage[distance, pl.ds(at, PAGE), :] = pool_v[table_ref[beam, index]]
+                return carry
+
+            lax.fori_loop(0, context // PAGE, put, 0)
+            span = pl.ds(rank * context, context)
+            if distance == 0:
+                copy = pltpu.make_async_copy(stage.at[0, span], recv_ref.at[0, span], own_sem.at[rank])
+            else:
+                copy = pltpu.make_async_remote_copy(
+                    src_ref=stage.at[distance, span], dst_ref=recv_ref.at[distance, span],
+                    send_sem=bs_sem.at[distance * MOST + rank], recv_sem=br_sem.at[distance * MOST + rank],
+                    device_id={"dp": peer(SPAN - distance)}, device_id_type=MESH,
+                )
+            copy.start()
+            copies.append(copy)
+    for copy in copies:
         copy.wait()
 
 
@@ -300,34 +492,96 @@
     pltpu.make_async_copy(recv_ref, cache_ref, out_sem).wait()
 
 
+def place_kernel(recv_ref, raw_ref, new_ref, meta_ref, proj_ref, cache_ref, edge, zeros, out_sem):
+    total = recv_ref.shape[0]
+    zeros[...] = jnp.zeros_like(zeros)
+    fresh = [new_ref[step].astype(jnp.float32) for step in range(STEPS)]
+    slots = [meta_ref[BEAMS * 4 + child] for child in range(BEAMS)]
+    for child in range(BEAMS):
+        length, start, split, again = (meta_ref[child * 4 + at] for at in range(4))
+        first = length >> 6
+        last = (length + STEPS - 1) >> 6
+        split = jnp.minimum(split, first)
+
+        def move(source, source_at, at, count, child=child):
+            @pl.when(count > 0)
+            def _():
+                pltpu.make_async_copy(
+                    source.at[pl.ds(source_at, count)], cache_ref.at[child, pl.ds(at, count)], out_sem
+                ).start()
+
+        move(recv_ref, start, 0, split)
+        move(recv_ref, again, split, first - split)
+        move(zeros, 0, last + 1, PER_CHILD - 1 - last)
+
+        def fix(index, carry, child=child, length=length, first=first, start=start, again=again, whole=meta_ref[child * 4 + 2]):
+            position = index * GRAIN + lax.broadcasted_iota(jnp.int32, (GRAIN, 2 * HD), 0)
+            at = jnp.minimum(jnp.where(index < whole, start + index, again + index - whole), total - 1)
+            page = jnp.where(position < length, recv_ref[at].astype(jnp.float32), 0.0)
+            for step in range(STEPS):
+                page = jnp.where(position == length + step, fresh[step][child:child + 1], page)
+            edge[child * 2 + index - first] = page.astype(jnp.bfloat16)
+            pltpu.make_async_copy(edge.at[child * 2 + index - first], cache_ref.at[child, index], out_sem).start()
+            return carry
+
+        lax.fori_loop(first, last + 1, fix, 0)
+
+    rows = MOST * STEPS
+    raw = []
+    for distance in range(SPAN):
+        part = raw_ref[distance].astype(jnp.float32)
+        raw.append(jnp.concatenate([part[:rows], part[rows:]], axis=1))
+    raw = jnp.concatenate(raw, axis=0).astype(jnp.bfloat16)
+    row = lax.broadcasted_iota(jnp.int32, (BEAMS, SPAN * rows), 0)
+    col = lax.broadcasted_iota(jnp.int32, (BEAMS, SPAN * rows), 1)
+    slot_at = jnp.zeros_like(col)
+    for child in range(BEAMS):
+        slot_at = jnp.where(row == child, slots[child], slot_at)
+    for step in range(STEPS):
+        pick = jnp.where(col == slot_at * STEPS + step, 1.0, 0.0).astype(jnp.bfloat16)
+        proj_ref[step] = jnp.dot(pick, raw, preferred_element_type=jnp.float32).astype(jnp.bfloat16)
+    pltpu.make_async_copy(cache_ref, cache_ref, out_sem).wait()
+
+
 def local(shards, queries, new_kv, kv_pool, page_tables, lengths, parents, out_weight):
     wide = queries.shape[2]
     channels = kv_pool.shape[2]
     context = page_tables.shape[1] * kv_pool.shape[1]
     rows = MOST * STEPS
     vmem = pl.BlockSpec(memory_space=pltpu.VMEM)
+    smem = pl.BlockSpec(memory_space=pltpu.SMEM)
     hbm = pl.BlockSpec(memory_space=pltpu.HBM)
     free = pl.BlockSpec(memory_space=pl.ANY)
     dma = pltpu.SemaphoreType.DMA
     bf16 = jnp.bfloat16
+
+    def pinned(*operands):
+        return [pltpu.with_memory_space_constraint(operand, pltpu.HBM) for operand in operands]
+
+    grain_pool = kv_pool.reshape(-1, GRAIN, channels)
     with jax.named_scope("exchange"):
-        recv, raw = pl.pallas_call(
+        recv, raw, meta, over = pl.pallas_call(
             exchange_kernel,
             out_shape=(
-                jax.ShapeDtypeStruct((SPAN, MOST * context, channels), bf16),
+                jax.ShapeDtypeStruct((2 * LINK + MOST * PER_CHILD, GRAIN, channels), bf16),
                 jax.ShapeDtypeStruct((SPAN, 2 * rows, wide // 2), bf16),
+                jax.ShapeDtypeStruct((BEAMS * 5,), jnp.int32),
+                jax.ShapeDtypeStruct((1,), jnp.int32),
             ),
             in_specs=[hbm] * 7,
-            out_specs=(free, free),
+            out_specs=(free, free, smem, smem),
             scratch_shapes=[
                 pltpu.VMEM(queries.shape, bf16),
                 pltpu.VMEM(new_kv.shape, bf16),
                 pltpu.SMEM(page_tables.shape, jnp.int32),
                 pltpu.SMEM(lengths.shape, jnp.int32),
                 pltpu.SMEM(parents.shape, jnp.int32),
-                pltpu.VMEM(kv_pool.shape, bf16),
+                pltpu.VMEM(grain_pool.shape, bf16),
                 pltpu.VMEM((shards, out_weight.shape[0], wide), bf16),
-                pltpu.VMEM((SPAN, MOST * context, channels), bf16),
+                pltpu.VMEM((SPAN, MOST * PER_CHILD, GRAIN, channels), bf16),
+                pltpu.VMEM((2, FIRST, GRAIN, channels), bf16),
+                pltpu.VMEM((2, FIRST, GRAIN, channels), bf16),
+                pltpu.VMEM((2, REST, GRAIN, channels), bf16),
                 pltpu.VMEM((SPAN, 2 * rows, (wide + channels) // 2), bf16),
                 pltpu.VMEM((SPAN, 2 * rows, (wide + channels) // 2), bf16),
                 pltpu.VMEM((SPAN * rows, wide), jnp.float32),
@@ -335,9 +589,10 @@
                 pltpu.VMEM((shards, SPAN * rows, wide), bf16),
                 pltpu.VMEM((SPAN, 2 * rows, wide // 2), bf16),
                 pltpu.SMEM((SPAN * MOST,), jnp.int32),
-                dma((5,)), dma, dma((shards,)), dma((MOST + 1,)),
+                pltpu.SMEM((SPAN * MOST,), jnp.int32),
+                dma((5,)), dma, dma((shards,)), dma((2,)), dma((2,)),
                 dma((SPAN,)), dma((SPAN,)),
-                dma((SPAN * MOST,)), dma((SPAN * MOST,)),
+                dma((8,)), dma((8,)),
                 dma((shards,)), dma((shards,)),
                 dma((SPAN,)), dma((SPAN,)),
                 pltpu.SemaphoreType.REGULAR,
@@ -346,30 +601,70 @@
                 collective_id=0, has_side_effects=True, vmem_limit_bytes=48 * 1024 * 1024
             ),
             name="exchange",
-        )(*(
-            pltpu.with_memory_space_constraint(operand, pltpu.HBM)
-            for operand in (queries, new_kv, kv_pool, page_tables, lengths, parents, out_weight)
-        ))
-    with jax.named_scope("finish"):
-        return pl.pallas_call(
-            finish_kernel,
-            out_shape=(
-                jax.ShapeDtypeStruct(queries.shape, bf16),
-                jax.ShapeDtypeStruct((BEAMS, context, channels), bf16),
-            ),
-            in_specs=[vmem, vmem, hbm, hbm, hbm],
-            out_specs=(vmem, hbm),
-            scratch_shapes=[
-                pltpu.VMEM(new_kv.shape, bf16),
-                pltpu.SMEM(lengths.shape, jnp.int32),
-                pltpu.SMEM(parents.shape, jnp.int32),
-                pltpu.VMEM((2 * BEAMS, PAGE, channels), bf16),
-                pltpu.VMEM((PAGE, channels), bf16),
-                dma((3,)), dma,
-            ],
-            compiler_params=pltpu.CompilerParams(vmem_limit_bytes=24 * 1024 * 1024),
-            name="finish",
-        )(recv.reshape(BEAMS, context, channels), raw, new_kv, lengths, parents)
+        )(*pinned(queries, new_kv, grain_pool, page_tables, lengths, parents, out_weight))
+
+    def placed():
+        with jax.named_scope("place"):
+            projected, cache = pl.pallas_call(
+                place_kernel,
+                out_shape=(
+                    jax.ShapeDtypeStruct(queries.shape, bf16),
+                    jax.ShapeDtypeStruct((BEAMS, PER_CHILD, GRAIN, channels), bf16),
+                ),
+                in_specs=[vmem, vmem, vmem, smem],
+                out_specs=(vmem, free),
+                scratch_shapes=[
+                    pltpu.VMEM((2 * BEAMS, GRAIN, channels), bf16),
+                    pltpu.VMEM((PER_CHILD, GRAIN, channels), bf16),
+                    dma,
+                ],
+                compiler_params=pltpu.CompilerParams(vmem_limit_bytes=24 * 1024 * 1024),
+                name="place",
+            )(recv, raw, new_kv, meta)
+            return projected, cache.reshape(BEAMS, context, channels)
+
+    def resent():
+        with jax.named_scope("full"):
+            whole = pl.pallas_call(
+                full_kernel,
+                out_shape=jax.ShapeDtypeStruct((SPAN, MOST * context, channels), bf16),
+                in_specs=[hbm] * 3,
+                out_specs=free,
+                scratch_shapes=[
+                    pltpu.SMEM(page_tables.shape, jnp.int32),
+                    pltpu.SMEM(parents.shape, jnp.int32),
+                    pltpu.VMEM(kv_pool.shape, bf16),
+                    pltpu.VMEM((SPAN, MOST * context, channels), bf16),
+                    dma((2,)), dma, dma((MOST,)),
+                    dma((SPAN * MOST,)), dma((SPAN * MOST,)),
+                ],
+                compiler_params=pltpu.CompilerParams(
+                    collective_id=1, has_side_effects=True, vmem_limit_bytes=24 * 1024 * 1024
+                ),
+                name="full",
+            )(*pinned(kv_pool, page_tables, parents))
+        with jax.named_scope("finish"):
+            return pl.pallas_call(
+                finish_kernel,
+                out_shape=(
+                    jax.ShapeDtypeStruct(queries.shape, bf16),
+                    jax.ShapeDtypeStruct((BEAMS, context, channels), bf16),
+                ),
+                in_specs=[vmem, vmem, hbm, hbm, hbm],
+                out_specs=(vmem, hbm),
+                scratch_shapes=[
+                    pltpu.VMEM(new_kv.shape, bf16),
+                    pltpu.SMEM(lengths.shape, jnp.int32),
+                    pltpu.SMEM(parents.shape, jnp.int32),
+                    pltpu.VMEM((2 * BEAMS, PAGE, channels), bf16),
+                    pltpu.VMEM((PAGE, channels), bf16),
+                    dma((3,)), dma,
+                ],
+                compiler_params=pltpu.CompilerParams(vmem_limit_bytes=24 * 1024 * 1024),
+                name="finish",
+            )(whole.reshape(BEAMS, context, channels), raw, new_kv, lengths, parents)
+
+    return lax.cond(over[0] > 0, resent, placed)
 
 
 def solution(mesh):

time: 57.8 us -> 52.8 us (0.913); the launches traced: 56.9 us -> 52.7 us
  Pallas kernels: 56.2 us -> 51.4 us
    pallas_call x2, Pallas kernels: 56.2 us -> 51.4 us  [the longest x1 48.2 us: local(): pl.pallas_call(exchange_kernel, out_shape=(jax.ShapeDtypeStruct((2 * LINK...]
where the time goes in v7:
time: 52.8 us; the launch traced here: 52.7 us
  Pallas kernels  51.4 us (97%)
  between operations  1.23 us (2%)
    pallas_call x1, Pallas kernels, local(): pl.pallas_call(exchange_kernel, out_shape=(jax.ShapeDtypeStruct((2 * LINK...  48.2 us
    pallas_call x1, Pallas kernels, placed(): pl.pallas_call(place_kernel, out_shape=(jax.ShapeDtypeStruct(queries.shap...  3.18 us

profile of v7, /device:TPU:0, one launch (start us, length us, event | category | flops | bytes accessed | tf_op | source)
XLA Modules:
  0.0 52.7 jit_solution(11040935576070553425)
XLA Ops:
  0.6 0.0 copy-start
  0.6 0.0 copy-start.2
  0.7 48.2 %exchange.1 = (bf16[138,64,256]{2,1,0:T(8,128)(2,1)S(1)}, bf16[4,16,512]{2,1,0:T(8,128)(2,1)S(1)}, s32[40]{0:T(128)S(1)}, s32[1]{0:T(128)}) custom-call(bf16[4,8,1024]{2,1,0:T(8,128)(2,1)} %q_hbm.1, bf16[4,8,256]{2,1,0:T(8,128)(2,1)} %new_hbm.1, bf16[128,64,256]{2,1,0:T(8,128)(2,1)} %bitcast.5, s32[8,8]{1,0:T(8,128)} %table_hbm.1, s32[128]{0:T(128)} %len_hbm.1, ...), custom_call_target="tpu_custom_call" | custom-call | tf_op jit(solution)/shard_map/exchange/exchange/pallas_call | solution.py:563
  49.4 0.0 copy-done
  49.5 0.0 copy-done.2
  49.5 3.2 %conditional.1 = ((bf16[4,8,1024]{2,1,0:T(8,128)(2,1)}, bf16[8,1024,256]{2,1,0:T(8,128)(2,1)})) conditional(s32[]{:T(128)} %bitcast.3, (bf16[138,64,256]{2,1,0:T(8,128)(2,1)S(1)}, bf16[4,16,512]{2,1,0:T(8,128)(2,1)S(1)}, bf16[4,8,256]{2,1,0:T(8,128)(2,1)S(1)}, s32[40]{0:T(128)S(1)}) %tuple.22, (bf16[64,128,256]{2,1,0:T(8,128)(2,1)}, ...), branch_computations={%region_0.0_spmd, %region_1.0_spmd} | conditional | bytes 2084 | solution.py:667
  49.5 3.2 %place.1 = (bf16[4,8,1024]{2,1,0:T(8,128)(2,1)}, bf16[8,16,64,256]{3,2,1,0:T(8,128)(2,1)}) custom-call(bf16[138,64,256]{2,1,0:T(8,128)(2,1)S(1)} %get-tuple-element.20.recv_ref, bf16[4,16,512]{2,1,0:T(8,128)(2,1)S(1)} %get-tuple-element.21.raw_ref, bf16[4,8,256]{2,1,0:T(8,128)(2,1)S(1)} %get-tuple-element.22.new_ref, s32[40]{0:T(128)S(1)} %get-tuple-element.23.meta_ref), custom_call_target="tpu_custom_call" | custom-call | tf_op jit(solution)/shard_map/cond/branch_0_fun/place/place/pallas_call | solution.py:608
Async XLA Ops:
  0.6 48.8 %copy-start = (bf16[4,8,256]{2,1,0:T(8,128)(2,1)S(1)}, bf16[4,8,256]{2,1,0:T(8,128)(2,1)}, u32[]{:S(2)}) copy-start(bf16[4,8,256]{2,1,0:T(8,128)(2,1)} %new_hbm.1) | copy-start | bytes 49156
  0.6 48.8 %copy-start.2 = (s32[128]{0:T(128)S(1)}, s32[128]{0:T(128)}, u32[]{:S(2)}) copy-start(s32[128]{0:T(128)} %len_hbm.1) | copy-start | bytes 1540

commit v8 on v7

--- a/solution.py
+++ b/solution.py
@@ -275,21 +275,22 @@
         return carry
 
     lax.fori_loop(0, SPAN, attend, 0)
-    for copy in b_copies:
-        copy.wait()
+    for copy in b_copies[:4]:
+        copy.wait()
+    more_copies = b_copies[4:]
     b_copies = []
     for side, (flow, mine_via, _, passed, target) in enumerate(sides):
-        copy = pltpu.make_async_copy(first_recv.at[side], recv_ref.at[pl.ds(side * LINK, FIRST)], land_sem.at[side])
-        copy.start()
-        b_copies.append(copy)
+        def put_passed(at, carry, side=side, flow=flow, mine_via=mine_via, passed=passed):
+            here = pool_v[grain_at(flow, FIRST - mine_via + at - passed)]
+            rest_send[side, at] = jnp.where(at < passed, first_recv[side, at], here)
+            return carry
 
         def put_rest(at, carry, side=side, flow=flow, mine_via=mine_via, passed=passed):
-            number = FIRST - mine_via + at - passed
-            here = pool_v[grain_at(flow, number)]
-            rest_send[side, at] = jnp.where(at < passed, first_recv[side, jnp.minimum(at, VIA - 1)], here)
+            rest_send[side, at] = pool_v[grain_at(flow, FIRST - mine_via + at - passed)]
             return carry
 
-        lax.fori_loop(0, REST, put_rest, 0)
+        lax.fori_loop(0, VIA, put_passed, 0)
+        lax.fori_loop(VIA, REST, put_rest, 0)
         copy = pltpu.make_async_remote_copy(
             src_ref=rest_send.at[side], dst_ref=recv_ref.at[pl.ds(side * LINK + FIRST, REST)],
             send_sem=bs_sem.at[side * 4 + 3], recv_sem=br_sem.at[side * 4 + 3],
@@ -321,27 +322,6 @@
     lax.fori_loop(1, shards, project, 0)
     own = jnp.dot(attended, w_v[mine], preferred_element_type=jnp.float32)
 
-    def gather_sums(other, total):
-        p_copy(other).wait()
-        return total + p_recv[other].astype(jnp.float32)
-
-    summed = lax.fori_loop(1, shards, gather_sums, own)
-    half = wide // 2
-    r_copies = []
-    for distance in range(SPAN):
-        part = summed[distance * rows:(distance + 1) * rows]
-        r_send[distance] = jnp.concatenate([part[:, :half], part[:, half:]], axis=0).astype(jnp.bfloat16)
-        if distance == 0:
-            copy = pltpu.make_async_copy(r_send.at[0], proj_ref.at[0], own_sem.at[1])
-        else:
-            copy = pltpu.make_async_remote_copy(
-                src_ref=r_send.at[distance], dst_ref=proj_ref.at[distance],
-                send_sem=rs_sem.at[distance], recv_sem=rr_sem.at[distance],
-                device_id={"dp": peer(SPAN - distance)}, device_id_type=MESH,
-            )
-        copy.start()
-        r_copies.append(copy)
-
     over_ref[0] = lax.fori_loop(
         0, rings, lambda ring, over: jnp.maximum(over, overfull(ring_plan(par_ref, len_ref, ring))), jnp.int32(0)
     )
@@ -349,7 +329,6 @@
         slot = slots[child]
         distance = slot >> 1
         length = len_ref[owners[child]]
-        count = grains(length)
         before = jnp.int32(0)
         for other in range(BEAMS):
             if other != child:
@@ -365,12 +344,39 @@
         split = jnp.minimum(jnp.maximum(split, 0), PER_CHILD)
         start = jnp.where(distance == 2, FIRST + before, near_base + near_via + before)
         again = jnp.where(distance == 2, LINK + FIRST + before + split - from_up[1], start + split + near_pass)
-        own = distance == 0
+        stays = distance == 0
         meta_ref[child * 4] = length
-        meta_ref[child * 4 + 1] = jnp.where(own, 2 * LINK + (slot & 1) * PER_CHILD, start)
-        meta_ref[child * 4 + 2] = jnp.where(own, PER_CHILD, split)
-        meta_ref[child * 4 + 3] = jnp.where(own, 0, again)
+        meta_ref[child * 4 + 1] = jnp.where(stays, 2 * LINK + (slot & 1) * PER_CHILD, start)
+        meta_ref[child * 4 + 2] = jnp.where(stays, PER_CHILD, split)
+        meta_ref[child * 4 + 3] = jnp.where(stays, 0, again)
         meta_ref[BEAMS * 4 + child] = slot
+    for copy in more_copies:
+        copy.wait()
+    for side in range(2):
+        copy = pltpu.make_async_copy(first_recv.at[side], recv_ref.at[pl.ds(side * LINK, FIRST)], land_sem.at[side])
+        copy.start()
+        b_copies.append(copy)
+
+    def gather_sums(other, total):
+        p_copy(other).wait()
+        return total + p_recv[other].astype(jnp.float32)
+
+    summed = lax.fori_loop(1, shards, gather_sums, own)
+    half = wide // 2
+    r_copies = []
+    for distance in range(SPAN):
+        part = summed[distance * rows:(distance + 1) * rows]
+        r_send[distance] = jnp.concatenate([part[:, :half], part[:, half:]], axis=0).astype(jnp.bfloat16)
+        if distance == 0:
+            copy = pltpu.make_async_copy(r_send.at[0], proj_ref.at[0], own_sem.at[1])
+        else:
+            copy = pltpu.make_async_remote_copy(
+                src_ref=r_send.at[distance], dst_ref=proj_ref.at[distance],
+                send_sem=rs_sem.at[distance], recv_sem=rr_sem.at[distance],
+                device_id={"dp": peer(SPAN - distance)}, device_id_type=MESH,
+            )
+        copy.start()
+        r_copies.append(copy)
     for copy in r_copies:
         copy.wait()
     for copy in b_copies:

time: 52.8 us -> 50.7 us (0.960)
  Pallas kernels: 51.4 us -> 49 us
    pallas_call x1, Pallas kernels: 48.2 us -> 45.9 us  [local(): pl.pallas_call(exchange_kernel, out_shape=(jax.ShapeDtypeStruct((2 * LINK...]
where the time goes in v8:
time: 50.7 us; the launch traced here: 50.3 us
  Pallas kernels  49 us (97%)
  between operations  1.23 us (2%)
    pallas_call x1, Pallas kernels, local(): pl.pallas_call(exchange_kernel, out_shape=(jax.ShapeDtypeStruct((2 * LINK...  45.9 us
    pallas_call x1, Pallas kernels, placed(): pl.pallas_call(place_kernel, out_shape=(jax.ShapeDtypeStruct(queries.shap...  3.17 us

profile of v8, /device:TPU:0, one launch (start us, length us, event | category | flops | bytes accessed | tf_op | source)
XLA Modules:
  0.0 50.3 jit_solution(12412385468046323050)
XLA Ops:
  0.6 0.0 copy-start
  0.6 0.0 copy-start.2
  0.7 45.9 %exchange.1 = (bf16[138,64,256]{2,1,0:T(8,128)(2,1)S(1)}, bf16[4,16,512]{2,1,0:T(8,128)(2,1)S(1)}, s32[40]{0:T(128)S(1)}, s32[1]{0:T(128)}) custom-call(bf16[4,8,1024]{2,1,0:T(8,128)(2,1)} %q_hbm.1, bf16[4,8,256]{2,1,0:T(8,128)(2,1)} %new_hbm.1, bf16[128,64,256]{2,1,0:T(8,128)(2,1)} %bitcast.5, s32[8,8]{1,0:T(8,128)} %table_hbm.1, s32[128]{0:T(128)} %len_hbm.1, ...), custom_call_target="tpu_custom_call" | custom-call | tf_op jit(solution)/shard_map/exchange/exchange/pallas_call | solution.py:569
  47.1 0.0 copy-done
  47.1 0.0 copy-done.2
  47.1 3.2 %conditional.1 = ((bf16[4,8,1024]{2,1,0:T(8,128)(2,1)}, bf16[8,1024,256]{2,1,0:T(8,128)(2,1)})) conditional(s32[]{:T(128)} %bitcast.3, (bf16[138,64,256]{2,1,0:T(8,128)(2,1)S(1)}, bf16[4,16,512]{2,1,0:T(8,128)(2,1)S(1)}, bf16[4,8,256]{2,1,0:T(8,128)(2,1)S(1)}, s32[40]{0:T(128)S(1)}) %tuple.22, (bf16[64,128,256]{2,1,0:T(8,128)(2,1)}, ...), branch_computations={%region_0.0_spmd, %region_1.0_spmd} | conditional | bytes 2084 | solution.py:673
  47.1 3.2 %place.1 = (bf16[4,8,1024]{2,1,0:T(8,128)(2,1)}, bf16[8,16,64,256]{3,2,1,0:T(8,128)(2,1)}) custom-call(bf16[138,64,256]{2,1,0:T(8,128)(2,1)S(1)} %get-tuple-element.20.recv_ref, bf16[4,16,512]{2,1,0:T(8,128)(2,1)S(1)} %get-tuple-element.21.raw_ref, bf16[4,8,256]{2,1,0:T(8,128)(2,1)S(1)} %get-tuple-element.22.new_ref, s32[40]{0:T(128)S(1)} %get-tuple-element.23.meta_ref), custom_call_target="tpu_custom_call" | custom-call | tf_op jit(solution)/shard_map/cond/branch_0_fun/place/place/pallas_call | solution.py:614
Async XLA Ops:
  0.6 46.5 %copy-start = (bf16[4,8,256]{2,1,0:T(8,128)(2,1)S(1)}, bf16[4,8,256]{2,1,0:T(8,128)(2,1)}, u32[]{:S(2)}) copy-start(bf16[4,8,256]{2,1,0:T(8,128)(2,1)} %new_hbm.1) | copy-start | bytes 49156
  0.6 46.5 %copy-start.2 = (s32[128]{0:T(128)S(1)}, s32[128]{0:T(128)}, u32[]{:S(2)}) copy-start(s32[128]{0:T(128)} %len_hbm.1) | copy-start | bytes 1540

commit v9 on v8

--- a/solution.py
+++ b/solution.py
@@ -13,18 +13,21 @@
 BEAMS = 8
 STEPS = 4
 PAGE = 128
-GRAIN = 64
-PER_CHILD = 16
-VIA = 20
-MORE = 8
-REST = 25
+PAGES = 8
+GRAIN = 32
+PER_CHILD = 32
+PER_PAGE = PAGE // GRAIN
+TILE = 16
+VIA = 40
+MORE = 16
+REST = 46
 FIRST = VIA + MORE
 LINK = FIRST + REST
 MESH = pl.DeviceIdType.MESH
 
 
 def grains(length):
-    return (length + (GRAIN - 1)) >> 6
+    return (length + (GRAIN - 1)) // GRAIN
 
 
 def choose(values, index):
@@ -196,7 +199,7 @@
         later = number >= cut
         number = jnp.where(later, number - cut, number)
         number = jnp.minimum(jnp.maximum(number, 0), PER_CHILD - 1)
-        return table_ref[jnp.where(later, second, first), number >> 1] * 2 + (number & 1)
+        return table_ref[jnp.where(later, second, first), number >> 2] * PER_PAGE + (number & (PER_PAGE - 1))
 
     sides = (
         (flows[1], choose(via_up, y), jnp.int32(0), choose(via_up, (y - 1) & 3), peer(1)),
@@ -204,17 +207,18 @@
     )
     pool_copy.wait()
     b_copies = []
-    cuts = (0, VIA // 2, VIA, FIRST)
+    cuts = (0, 8, VIA, FIRST)
     for part in range(3):
         for side, (flow, mine_via, skip, _, target) in enumerate(sides):
             def put(at, carry, side=side, flow=flow, mine_via=mine_via, skip=skip):
-                far = at < mine_via
-                chosen = tuple(jnp.where(far, one, two) for one, two in zip(flows[2], flow))
-                number = jnp.where(far, skip + at, at - mine_via)
-                first_send[side, at] = pool_v[grain_at(chosen, number)]
+                for at in (2 * at, 2 * at + 1):
+                    far = at < mine_via
+                    chosen = tuple(jnp.where(far, one, two) for one, two in zip(flows[2], flow))
+                    number = jnp.where(far, skip + at, at - mine_via)
+                    first_send[side, at] = pool_v[grain_at(chosen, number)]
                 return carry
 
-            lax.fori_loop(cuts[part], cuts[part + 1], put, 0)
+            lax.fori_loop(cuts[part] // 2, cuts[part + 1] // 2, put, 0)
             span = pl.ds(cuts[part], cuts[part + 1] - cuts[part])
             copy = pltpu.make_async_remote_copy(
                 src_ref=first_send.at[side, span], dst_ref=first_recv.at[side, span],
@@ -230,13 +234,13 @@
         w_copies.append(copy)
 
     def put_all(index, carry):
-        slot = index >> 4
-        number = index & (PER_CHILD - 1)
-        grain = table_ref[beams[slot], number >> 1] * 2 + (number & 1)
-        stage[index >> 5, index & (MOST * PER_CHILD - 1)] = pool_v[grain]
+        slot = index // PAGES
+        page = table_ref[beams[slot], index % PAGES]
+        at = (index % (MOST * PAGES)) * PER_PAGE
+        stage[index // (MOST * PAGES), pl.ds(at, PER_PAGE)] = pool_v[pl.ds(page * PER_PAGE, PER_PAGE)]
         return carry
 
-    lax.fori_loop(0, SPAN * MOST * PER_CHILD, put_all, 0)
+    lax.fori_loop(0, SPAN * MOST * PAGES, put_all, 0)
     own_copy = pltpu.make_async_copy(stage.at[0], recv_ref.at[pl.ds(2 * LINK, MOST * PER_CHILD)], own_sem.at[0])
     own_copy.start()
 
@@ -281,16 +285,18 @@
     b_copies = []
     for side, (flow, mine_via, _, passed, target) in enumerate(sides):
         def put_passed(at, carry, side=side, flow=flow, mine_via=mine_via, passed=passed):
-            here = pool_v[grain_at(flow, FIRST - mine_via + at - passed)]
-            rest_send[side, at] = jnp.where(at < passed, first_recv[side, at], here)
+            for at in (2 * at, 2 * at + 1):
+                here = pool_v[grain_at(flow, FIRST - mine_via + at - passed)]
+                rest_send[side, at] = jnp.where(at < passed, first_recv[side, at], here)
             return carry
 
         def put_rest(at, carry, side=side, flow=flow, mine_via=mine_via, passed=passed):
-            rest_send[side, at] = pool_v[grain_at(flow, FIRST - mine_via + at - passed)]
+            for at in (2 * at, 2 * at + 1):
+                rest_send[side, at] = pool_v[grain_at(flow, FIRST - mine_via + at - passed)]
             return carry
 
-        lax.fori_loop(0, VIA, put_passed, 0)
-        lax.fori_loop(VIA, REST, put_rest, 0)
+        lax.fori_loop(0, VIA // 2, put_passed, 0)
+        lax.fori_loop(VIA // 2, REST // 2, put_rest, 0)
         copy = pltpu.make_async_remote_copy(
             src_ref=rest_send.at[side], dst_ref=recv_ref.at[pl.ds(side * LINK + FIRST, REST)],
             send_sem=bs_sem.at[side * 4 + 3], recv_sem=br_sem.at[side * 4 + 3],
@@ -503,11 +509,13 @@
     zeros[...] = jnp.zeros_like(zeros)
     fresh = [new_ref[step].astype(jnp.float32) for step in range(STEPS)]
     slots = [meta_ref[BEAMS * 4 + child] for child in range(BEAMS)]
+    per_child = cache_ref.shape[1]
+    scale = GRAIN // TILE
     for child in range(BEAMS):
         length, start, split, again = (meta_ref[child * 4 + at] for at in range(4))
-        first = length >> 6
-        last = (length + STEPS - 1) >> 6
-        split = jnp.minimum(split, first)
+        first = length // TILE
+        last = (length + STEPS - 1) // TILE
+        split = jnp.minimum(split * scale, first)
 
         def move(source, source_at, at, count, child=child):
             @pl.when(count > 0)
@@ -516,17 +524,21 @@
                     source.at[pl.ds(source_at, count)], cache_ref.at[child, pl.ds(at, count)], out_sem
                 ).start()
 
-        move(recv_ref, start, 0, split)
-        move(recv_ref, again, split, first - split)
-        move(zeros, 0, last + 1, PER_CHILD - 1 - last)
-
-        def fix(index, carry, child=child, length=length, first=first, start=start, again=again, whole=meta_ref[child * 4 + 2]):
-            position = index * GRAIN + lax.broadcasted_iota(jnp.int32, (GRAIN, 2 * HD), 0)
-            at = jnp.minimum(jnp.where(index < whole, start + index, again + index - whole), total - 1)
-            page = jnp.where(position < length, recv_ref[at].astype(jnp.float32), 0.0)
+        move(recv_ref, start * scale, 0, split)
+        move(recv_ref, again * scale, split, first - split)
+        move(zeros, 0, last + 1, per_child - 1 - last)
+    for child in range(BEAMS):
+        length, start, split, again = (meta_ref[child * 4 + at] for at in range(4))
+        first = length // TILE
+        last = (length + STEPS - 1) // TILE
+
+        def fix(index, carry, child=child, length=length, first=first, start=start * scale, split=split * scale, again=again * scale):
+            position = index * TILE + lax.broadcasted_iota(jnp.int32, (TILE, 2 * HD), 0)
+            at = jnp.minimum(jnp.where(index < split, start + index, again + index - split), total - 1)
+            part = jnp.where(position < length, recv_ref[at].astype(jnp.float32), 0.0)
             for step in range(STEPS):
-                page = jnp.where(position == length + step, fresh[step][child:child + 1], page)
-            edge[child * 2 + index - first] = page.astype(jnp.bfloat16)
+                part = jnp.where(position == length + step, fresh[step][child:child + 1], part)
+            edge[child * 2 + index - first] = part.astype(jnp.bfloat16)
             pltpu.make_async_copy(edge.at[child * 2 + index - first], cache_ref.at[child, index], out_sem).start()
             return carry
 
@@ -615,18 +627,18 @@
                 place_kernel,
                 out_shape=(
                     jax.ShapeDtypeStruct(queries.shape, bf16),
-                    jax.ShapeDtypeStruct((BEAMS, PER_CHILD, GRAIN, channels), bf16),
+                    jax.ShapeDtypeStruct((BEAMS, context // TILE, TILE, channels), bf16),
                 ),
                 in_specs=[vmem, vmem, vmem, smem],
                 out_specs=(vmem, free),
                 scratch_shapes=[
-                    pltpu.VMEM((2 * BEAMS, GRAIN, channels), bf16),
-                    pltpu.VMEM((PER_CHILD, GRAIN, channels), bf16),
+                    pltpu.VMEM((2 * BEAMS, TILE, channels), bf16),
+                    pltpu.VMEM((context // TILE, TILE, channels), bf16),
                     dma,
                 ],
                 compiler_params=pltpu.CompilerParams(vmem_limit_bytes=24 * 1024 * 1024),
                 name="place",
-            )(recv, raw, new_kv, meta)
+            )(recv.reshape(-1, TILE, channels), raw, new_kv, meta)
             return projected, cache.reshape(BEAMS, context, channels)
 
     def resent():
@@ -670,7 +682,7 @@
                 name="finish",
             )(whole.reshape(BEAMS, context, channels), raw, new_kv, lengths, parents)
 
-    return lax.cond(over[0] > 0, resent, placed)
+    return lax.switch(over[0], (placed, resent))
 
 
 def solution(mesh):

time: 50.7 us -> 49.2 us (0.970)
  Pallas kernels: 49 us -> 47.6 us
    pallas_call x1, Pallas kernels: 45.9 us -> 44.4 us  [local(): pl.pallas_call(exchange_kernel, out_shape=(jax.ShapeDtypeStruct((2 * LINK...]
where the time goes in v9:
time: 49.2 us; the launch traced here: 48.9 us
  Pallas kernels  47.6 us (97%)
  between operations  1.23 us (2%)
    pallas_call x1, Pallas kernels, local(): pl.pallas_call(exchange_kernel, out_shape=(jax.ShapeDtypeStruct((2 * LINK...  44.4 us
    pallas_call x1, Pallas kernels, placed(): pl.pallas_call(place_kernel, out_shape=(jax.ShapeDtypeStruct(queries.shap...  3.19 us

profile of v9, /device:TPU:0, one launch (start us, length us, event | category | flops | bytes accessed | tf_op | source)
XLA Modules:
  0.0 48.9 jit_solution(4852743035361737830)
XLA Ops:
  0.6 0.0 copy-start
  0.6 0.0 copy-start.2
  0.7 44.4 %exchange.1 = (bf16[268,32,256]{2,1,0:T(8,128)(2,1)S(1)}, bf16[4,16,512]{2,1,0:T(8,128)(2,1)S(1)}, s32[40]{0:T(128)S(1)}, s32[1]{0:T(128)}) custom-call(bf16[4,8,1024]{2,1,0:T(8,128)(2,1)} %q_hbm.1, bf16[4,8,256]{2,1,0:T(8,128)(2,1)} %new_hbm.1, bf16[256,32,256]{2,1,0:T(8,128)(2,1)} %bitcast.6, s32[8,8]{1,0:T(8,128)} %table_hbm.1, s32[128]{0:T(128)} %len_hbm.1, ...), custom_call_target="tpu_custom_call" | custom-call | tf_op jit(solution)/shard_map/exchange/exchange/pallas_call | solution.py:581
  45.6 0.0 copy-done
  45.6 0.0 copy-done.2
  45.6 3.2 %conditional.1 = ((bf16[4,8,1024]{2,1,0:T(8,128)(2,1)}, bf16[8,1024,256]{2,1,0:T(8,128)(2,1)})) conditional(s32[]{:T(128)} %bitcast.4, (bf16[268,32,256]{2,1,0:T(8,128)(2,1)S(1)}, bf16[4,16,512]{2,1,0:T(8,128)(2,1)S(1)}, bf16[4,8,256]{2,1,0:T(8,128)(2,1)S(1)}, s32[40]{0:T(128)S(1)}) %tuple.22, (bf16[64,128,256]{2,1,0:T(8,128)(2,1)}, ...), branch_computations={%region_0.0_spmd, %region_1.0_spmd} | conditional | bytes 2084 | solution.py:685
  45.7 3.2 %place.1 = (bf16[4,8,1024]{2,1,0:T(8,128)(2,1)}, bf16[8,64,16,256]{3,2,1,0:T(8,128)(2,1)}) custom-call(bf16[536,16,256]{2,1,0:T(8,128)(2,1)S(1)} %bitcast.7, bf16[4,16,512]{2,1,0:T(8,128)(2,1)S(1)} %get-tuple-element.21.raw_ref, bf16[4,8,256]{2,1,0:T(8,128)(2,1)S(1)} %get-tuple-element.22.new_ref, s32[40]{0:T(128)S(1)} %get-tuple-element.23.meta_ref), custom_call_target="tpu_custom_call" | custom-call | tf_op jit(solution)/shard_map/cond/branch_0_fun/place/place/pallas_call | solution.py:626
Async XLA Ops:
  0.6 45.0 %copy-start = (bf16[4,8,256]{2,1,0:T(8,128)(2,1)S(1)}, bf16[4,8,256]{2,1,0:T(8,128)(2,1)}, u32[]{:S(2)}) copy-start(bf16[4,8,256]{2,1,0:T(8,128)(2,1)} %new_hbm.1) | copy-start | bytes 49156
  0.6 45.0 %copy-start.2 = (s32[128]{0:T(128)S(1)}, s32[128]{0:T(128)}, u32[]{:S(2)}) copy-start(s32[128]{0:T(128)} %len_hbm.1) | copy-start | bytes 1540

commit v10 on v9

--- a/solution.py
+++ b/solution.py
@@ -18,11 +18,13 @@
 PER_CHILD = 32
 PER_PAGE = PAGE // GRAIN
 TILE = 16
-VIA = 40
-MORE = 16
-REST = 46
+VIA = 36
+MORE = 18
+REST = 40
+LEFT = 12
 FIRST = VIA + MORE
 LINK = FIRST + REST
+META = 7
 MESH = pl.DeviceIdType.MESH
 
 
@@ -67,13 +69,13 @@
     return up, down, via_up, via_down
 
 
-def overfull(plan):
+def heaviest(plan):
     up, down, via_up, via_down = plan
     out = jnp.int32(0)
     for at in range(SPAN):
         load_up = up[at] + via_up[at] + via_up[(at - 1) % SPAN]
         load_down = down[at] + via_down[at] + via_down[(at + 1) % SPAN]
-        out = jnp.maximum(out, jnp.where(jnp.maximum(load_up, load_down) > LINK, 1, 0))
+        out = jnp.maximum(out, jnp.maximum(load_up, load_down))
     return out
 
 
@@ -107,9 +109,9 @@
 
 def exchange_kernel(
     q_hbm, new_hbm, pool_ref, table_hbm, len_hbm, par_hbm, w_ref,
-    recv_ref, proj_ref, meta_ref, over_ref,
+    recv_ref, proj_ref, left_ref, meta_ref, over_ref,
     q_ref, new_ref, table_ref, len_ref, par_ref,
-    pool_v, w_v, stage, first_send, first_recv, rest_send, q_send, q_recv, att, p_send, p_recv, r_send, lens, beams,
+    pool_v, w_v, stage, first_send, first_recv, rest_send, left_send, q_send, q_recv, att, p_send, p_recv, r_send, lens, beams,
     in_sem, pool_sem, w_sem, own_sem, land_sem, qs_sem, qr_sem, bs_sem, br_sem, ps_sem, pr_sem, rs_sem, rr_sem, here_sem,
 ):
     me = lax.axis_index("dp")
@@ -139,8 +141,13 @@
         copy = pltpu.make_async_copy(source, target, in_sem.at[at])
         copy.start()
         in_copies.append(copy)
-    pool_copy = pltpu.make_async_copy(pool_ref, pool_v, pool_sem)
-    pool_copy.start()
+    quarter = pool_v.shape[0] // 4
+    pool_copies = []
+    for at in range(4):
+        span = pl.ds(at * quarter, quarter)
+        copy = pltpu.make_async_copy(pool_ref.at[span], pool_v.at[span], pool_sem.at[at])
+        copy.start()
+        pool_copies.append(copy)
     for copy in in_copies:
         copy.wait()
 
@@ -205,7 +212,8 @@
         (flows[1], choose(via_up, y), jnp.int32(0), choose(via_up, (y - 1) & 3), peer(1)),
         (flows[3], choose(via_down, y), choose(via_up, y), choose(via_down, (y + 1) & 3), peer(3)),
     )
-    pool_copy.wait()
+    for copy in pool_copies:
+        copy.wait()
     b_copies = []
     cuts = (0, 8, VIA, FIRST)
     for part in range(3):
@@ -256,12 +264,15 @@
         last_len = lens[distance * MOST + 1]
         contract = (((1,), (1,)), ((), ()))
         scale = HD ** -0.5
-        scores = lax.dot_general(q_rows, stage[distance, :, :, 0:HD].reshape(MOST * context, HD), contract, preferred_element_type=jnp.float32) * scale
+        half = MOST * PER_CHILD // 2
+        keys = [stage[distance, pl.ds(rank * half, half), :, 0:HD].reshape(context, HD) for rank in range(MOST)]
+        scores = [lax.dot_general(q_rows, key, contract, preferred_element_type=jnp.float32) for key in keys]
+        rank_at = lax.broadcasted_iota(jnp.int32, scores[0].shape, 0) // STEPS % MOST
+        scores = jnp.where(rank_at == 0, scores[0], scores[1]) * scale
         fresh_scores = lax.dot_general(q_rows, fresh[:, :HD], contract, preferred_element_type=jnp.float32) * scale
-        rank_at = lax.broadcasted_iota(jnp.int32, scores.shape, 0) // STEPS % MOST
-        position = lax.broadcasted_iota(jnp.int32, scores.shape, 1) - rank_at * context
+        position = lax.broadcasted_iota(jnp.int32, scores.shape, 1)
         limit = jnp.where(rank_at == 0, old_len, last_len)
-        scores = jnp.where((position >= 0) & (position < limit), scores, -1e30)
+        scores = jnp.where(position < limit, scores, -1e30)
         f_row = lax.broadcasted_iota(jnp.int32, fresh_scores.shape, 0)
         f_col = lax.broadcasted_iota(jnp.int32, fresh_scores.shape, 1)
         seen = (f_row // STEPS % MOST == f_col // STEPS) & (f_col % STEPS <= f_row % STEPS)
@@ -270,9 +281,12 @@
         exp_old = jnp.exp(scores - top)
         exp_new = jnp.exp(fresh_scores - top)
         total = jnp.sum(exp_old, axis=1, keepdims=True) + jnp.sum(exp_new, axis=1, keepdims=True)
-        w_old = (exp_old / total).astype(jnp.bfloat16)
-        w_new = (exp_new / total).astype(jnp.bfloat16)
-        out = jnp.dot(w_old, stage[distance, :, :, HD:2 * HD].reshape(MOST * context, HD), preferred_element_type=jnp.float32)
+        share = 1.0 / total
+        w_old = (exp_old * share).astype(jnp.bfloat16)
+        w_new = (exp_new * share).astype(jnp.bfloat16)
+        values = [stage[distance, pl.ds(rank * half, half), :, HD:2 * HD].reshape(context, HD) for rank in range(MOST)]
+        out = [jnp.dot(w_old, value, preferred_element_type=jnp.float32) for value in values]
+        out = jnp.where(rank_at[:, :HD] == 0, out[0], out[1])
         out += jnp.dot(w_new, fresh[:, HD:], preferred_element_type=jnp.float32)
         out = jnp.concatenate([out[h * rows:(h + 1) * rows] for h in range(heads)], axis=1)
         att[pl.ds(pl.multiple_of(distance * rows, rows), rows), :] = out
@@ -328,9 +342,19 @@
     lax.fori_loop(1, shards, project, 0)
     own = jnp.dot(attended, w_v[mine], preferred_element_type=jnp.float32)
 
-    over_ref[0] = lax.fori_loop(
-        0, rings, lambda ring, over: jnp.maximum(over, overfull(ring_plan(par_ref, len_ref, ring))), jnp.int32(0)
+    load = lax.fori_loop(
+        0, rings, lambda ring, load: jnp.maximum(load, heaviest(ring_plan(par_ref, len_ref, ring))), jnp.int32(0)
     )
+    over_ref[0] = jnp.where(load > LINK, 1, 0) + jnp.where(load > LINK + LEFT, 1, 0)
+    for side, (flow, mine_via, _, passed, _) in enumerate(sides):
+        def put_left(at, carry, side=side, flow=flow, mine_via=mine_via, passed=passed):
+            left_send[side, at] = pool_v[grain_at(flow, LINK - mine_via - passed + at)]
+            return carry
+
+        lax.fori_loop(0, LEFT, put_left, 0)
+    copy = pltpu.make_async_copy(left_send, left_ref, land_sem.at[2])
+    copy.start()
+    b_copies.append(copy)
     for child in range(BEAMS):
         slot = slots[child]
         distance = slot >> 1
@@ -350,12 +374,18 @@
         split = jnp.minimum(jnp.maximum(split, 0), PER_CHILD)
         start = jnp.where(distance == 2, FIRST + before, near_base + near_via + before)
         again = jnp.where(distance == 2, LINK + FIRST + before + split - from_up[1], start + split + near_pass)
+        near = jnp.where(distance == 2, False, distance != 0)
+        until = LINK - near_via - near_pass - before
+        until = jnp.where(near, jnp.minimum(jnp.maximum(until, 0), PER_CHILD), PER_CHILD)
+        third = jnp.where(distance == 3, 0, LEFT) + near_via + near_pass + before + until - LINK
         stays = distance == 0
-        meta_ref[child * 4] = length
-        meta_ref[child * 4 + 1] = jnp.where(stays, 2 * LINK + (slot & 1) * PER_CHILD, start)
-        meta_ref[child * 4 + 2] = jnp.where(stays, PER_CHILD, split)
-        meta_ref[child * 4 + 3] = jnp.where(stays, 0, again)
-        meta_ref[BEAMS * 4 + child] = slot
+        meta_ref[child * META] = length
+        meta_ref[child * META + 1] = jnp.where(stays, 2 * LINK + (slot & 1) * PER_CHILD, start)
+        meta_ref[child * META + 2] = jnp.where(stays, PER_CHILD, split)
+        meta_ref[child * META + 3] = jnp.where(stays, 0, again)
+        meta_ref[child * META + 4] = until
+        meta_ref[child * META + 5] = jnp.where(near, third, 0)
+        meta_ref[child * META + 6] = slot
     for copy in more_copies:
         copy.wait()
     for side in range(2):
@@ -504,18 +534,42 @@
     pltpu.make_async_copy(recv_ref, cache_ref, out_sem).wait()
 
 
-def place_kernel(recv_ref, raw_ref, new_ref, meta_ref, proj_ref, cache_ref, edge, zeros, out_sem):
+def left_kernel(left_ref, got_ref, send_sem, recv_sem):
+    me = lax.axis_index("dp")
+    y = lax.rem(me, SPAN)
+    targets = [me - y + lax.rem(y + ahead, SPAN) for ahead in (1, SPAN - 1)]
+    barrier = pltpu.get_barrier_semaphore()
+    for target in targets:
+        pl.semaphore_signal(barrier, inc=1, device_id={"dp": target}, device_id_type=MESH)
+    pl.semaphore_wait(barrier, 2)
+    copies = []
+    for side, target in enumerate(targets):
+        copy = pltpu.make_async_remote_copy(
+            src_ref=left_ref.at[side], dst_ref=got_ref.at[side],
+            send_sem=send_sem.at[side], recv_sem=recv_sem.at[side],
+            device_id={"dp": target}, device_id_type=MESH,
+        )
+        copy.start()
+        copies.append(copy)
+    for copy in copies:
+        copy.wait()
+
+
+def place_kernel(with_left, recv_ref, raw_ref, new_ref, meta_ref, *refs):
+    left_ref = refs[0] if with_left else None
+    proj_ref, cache_ref, edge, zeros, out_sem = refs[-5:]
     total = recv_ref.shape[0]
     zeros[...] = jnp.zeros_like(zeros)
     fresh = [new_ref[step].astype(jnp.float32) for step in range(STEPS)]
-    slots = [meta_ref[BEAMS * 4 + child] for child in range(BEAMS)]
+    slots = [meta_ref[child * META + 6] for child in range(BEAMS)]
     per_child = cache_ref.shape[1]
     scale = GRAIN // TILE
     for child in range(BEAMS):
-        length, start, split, again = (meta_ref[child * 4 + at] for at in range(4))
+        length, start, split, again, until, third = (meta_ref[child * META + at] for at in range(6))
         first = length // TILE
         last = (length + STEPS - 1) // TILE
-        split = jnp.minimum(split * scale, first)
+        until = jnp.minimum(until * scale, first) if with_left else first
+        split = jnp.minimum(split * scale, until)
 
         def move(source, source_at, at, count, child=child):
             @pl.when(count > 0)
@@ -525,17 +579,26 @@
                 ).start()
 
         move(recv_ref, start * scale, 0, split)
-        move(recv_ref, again * scale, split, first - split)
+        move(recv_ref, again * scale, split, until - split)
+        if with_left:
+            move(left_ref, third * scale, until, first - until)
         move(zeros, 0, last + 1, per_child - 1 - last)
     for child in range(BEAMS):
-        length, start, split, again = (meta_ref[child * 4 + at] for at in range(4))
+        length, start, split, again, until, third = (meta_ref[child * META + at] for at in range(6))
         first = length // TILE
         last = (length + STEPS - 1) // TILE
 
-        def fix(index, carry, child=child, length=length, first=first, start=start * scale, split=split * scale, again=again * scale):
+        def fix(
+            index, carry, child=child, length=length, first=first, start=start * scale, split=split * scale,
+            again=again * scale, until=until * scale, third=third * scale,
+        ):
             position = index * TILE + lax.broadcasted_iota(jnp.int32, (TILE, 2 * HD), 0)
             at = jnp.minimum(jnp.where(index < split, start + index, again + index - split), total - 1)
-            part = jnp.where(position < length, recv_ref[at].astype(jnp.float32), 0.0)
+            part = recv_ref[at].astype(jnp.float32)
+            if with_left:
+                at = jnp.minimum(jnp.maximum(third + index - until, 0), left_ref.shape[0] - 1)
+                part = jnp.where(index < until, part, left_ref[at].astype(jnp.float32))
+            part = jnp.where(position < length, part, 0.0)
             for step in range(STEPS):
                 part = jnp.where(position == length + step, fresh[step][child:child + 1], part)
             edge[child * 2 + index - first] = part.astype(jnp.bfloat16)
@@ -578,16 +641,17 @@
 
     grain_pool = kv_pool.reshape(-1, GRAIN, channels)
     with jax.named_scope("exchange"):
-        recv, raw, meta, over = pl.pallas_call(
+        recv, raw, left, meta, over = pl.pallas_call(
             exchange_kernel,
             out_shape=(
                 jax.ShapeDtypeStruct((2 * LINK + MOST * PER_CHILD, GRAIN, channels), bf16),
                 jax.ShapeDtypeStruct((SPAN, 2 * rows, wide // 2), bf16),
-                jax.ShapeDtypeStruct((BEAMS * 5,), jnp.int32),
+                jax.ShapeDtypeStruct((2, LEFT, GRAIN, channels), bf16),
+                jax.ShapeDtypeStruct((BEAMS * META,), jnp.int32),
                 jax.ShapeDtypeStruct((1,), jnp.int32),
             ),
             in_specs=[hbm] * 7,
-            out_specs=(free, free, smem, smem),
+            out_specs=(free, free, free, smem, smem),
             scratch_shapes=[
                 pltpu.VMEM(queries.shape, bf16),
                 pltpu.VMEM(new_kv.shape, bf16),
@@ -600,6 +664,7 @@
                 pltpu.VMEM((2, FIRST, GRAIN, channels), bf16),
                 pltpu.VMEM((2, FIRST, GRAIN, channels), bf16),
                 pltpu.VMEM((2, REST, GRAIN, channels), bf16),
+                pltpu.VMEM((2, LEFT, GRAIN, channels), bf16),
                 pltpu.VMEM((SPAN, 2 * rows, (wide + channels) // 2), bf16),
                 pltpu.VMEM((SPAN, 2 * rows, (wide + channels) // 2), bf16),
                 pltpu.VMEM((SPAN * rows, wide), jnp.float32),
@@ -608,7 +673,7 @@
                 pltpu.VMEM((SPAN, 2 * rows, wide // 2), bf16),
                 pltpu.SMEM((SPAN * MOST,), jnp.int32),
                 pltpu.SMEM((SPAN * MOST,), jnp.int32),
-                dma((5,)), dma, dma((shards,)), dma((2,)), dma((2,)),
+                dma((5,)), dma((4,)), dma((shards,)), dma((2,)), dma((3,)),
                 dma((SPAN,)), dma((SPAN,)),
                 dma((8,)), dma((8,)),
                 dma((shards,)), dma((shards,)),
@@ -621,15 +686,15 @@
             name="exchange",
         )(*pinned(queries, new_kv, grain_pool, page_tables, lengths, parents, out_weight))
 
-    def placed():
+    def place(*got):
         with jax.named_scope("place"):
             projected, cache = pl.pallas_call(
-                place_kernel,
+                functools.partial(place_kernel, len(got) > 0),
                 out_shape=(
                     jax.ShapeDtypeStruct(queries.shape, bf16),
                     jax.ShapeDtypeStruct((BEAMS, context // TILE, TILE, channels), bf16),
                 ),
-                in_specs=[vmem, vmem, vmem, smem],
+                in_specs=[vmem, vmem, vmem, smem] + [vmem] * len(got),
                 out_specs=(vmem, free),
                 scratch_shapes=[
                     pltpu.VMEM((2 * BEAMS, TILE, channels), bf16),
@@ -637,9 +702,27 @@
                     dma,
                 ],
                 compiler_params=pltpu.CompilerParams(vmem_limit_bytes=24 * 1024 * 1024),
-                name="place",
-            )(recv.reshape(-1, TILE, channels), raw, new_kv, meta)
+                name="place_left" if got else "place",
+            )(recv.reshape(-1, TILE, channels), raw, new_kv, meta, *got)
             return projected, cache.reshape(BEAMS, context, channels)
+
+    def placed():
+        return place()
+
+    def topped():
+        with jax.named_scope("left"):
+            got = pl.pallas_call(
+                left_kernel,
+                out_shape=jax.ShapeDtypeStruct(left.shape, bf16),
+                in_specs=[free],
+                out_specs=free,
+                scratch_shapes=[dma((2,)), dma((2,))],
+                compiler_params=pltpu.CompilerParams(
+                    collective_id=2, has_side_effects=True, vmem_limit_bytes=4 * 1024 * 1024
+                ),
+                name="left",
+            )(left)
+        return place(got.reshape(-1, TILE, channels))
 
     def resent():
         with jax.named_scope("full"):
@@ -682,7 +765,7 @@
                 name="finish",
             )(whole.reshape(BEAMS, context, channels), raw, new_kv, lengths, parents)
 
-    return lax.switch(over[0], (placed, resent))
+    return lax.switch(over[0], (placed, topped, resent))
 
 
 def solution(mesh):

time: 49.2 us -> 54.5 us (1.11)
  Pallas kernels: 47.6 us -> 53 us
    pallas_call x1 -> x2, Pallas kernels: 3.19 us -> 10.8 us  [the longest x1 7.64 us: topped(): pl.pallas_call(left_kernel, out_shape=jax.ShapeDtypeStruct(left.shape, bf...]
    pallas_call x1, Pallas kernels: 44.4 us -> 42.2 us  [local(): pl.pallas_call(exchange_kernel, out_shape=(jax.ShapeDtypeStruct((2 * LINK...]
where the time goes in v10:
time: 54.5 us; the launch traced here: 54.4 us
  Pallas kernels  53 us (97%)
  between operations  1.3 us (2%)
    pallas_call x1, Pallas kernels, local(): pl.pallas_call(exchange_kernel, out_shape=(jax.ShapeDtypeStruct((2 * LINK...  42.2 us
    pallas_call x1, Pallas kernels, topped(): pl.pallas_call(left_kernel, out_shape=jax.ShapeDtypeStruct(left.shape, bf...  7.64 us
    pallas_call x1, Pallas kernels, place(): pl.pallas_call(functools.partial(place_kernel, len(got) > 0), out_shape=(...  3.18 us

profile of v10, /device:TPU:0, one launch (start us, length us, event | category | flops | bytes accessed | tf_op | source)
XLA Modules:
  0.0 54.4 jit_solution(3592984651310621916)
XLA Ops:
  0.6 0.0 copy-start
  0.6 0.0 copy-start.2
  0.7 42.2 %exchange.1 = (bf16[252,32,256]{2,1,0:T(8,128)(2,1)S(1)}, bf16[4,16,512]{2,1,0:T(8,128)(2,1)S(1)}, bf16[2,12,32,256]{3,2,1,0:T(8,128)(2,1)S(1)}, s32[56]{0:T(128)S(1)}, s32[1]{0:T(128)}) custom-call(bf16[4,8,1024]{2,1,0:T(8,128)(2,1)} %q_hbm.1, bf16[4,8,256]{2,1,0:T(8,128)(2,1)} %new_hbm.1, bf16[256,32,256]{2,1,0:T(8,128)(2,1)} %bitcast.10, ...), custom_call_target="tpu_custom_call" | custom-call | tf_op jit(solution)/shard_map/exchange/exchange/pallas_call | solution.py:644
  43.5 0.0 copy-done
  43.5 0.0 copy-done.2
  43.5 10.9 %conditional.1 = ((bf16[4,8,1024]{2,1,0:T(8,128)(2,1)}, bf16[8,1024,256]{2,1,0:T(8,128)(2,1)})) conditional(s32[]{:T(128)} %bitcast.7, (bf16[252,32,256]{2,1,0:T(8,128)(2,1)S(1)}, bf16[4,16,512]{2,1,0:T(8,128)(2,1)S(1)}, bf16[4,8,256]{2,1,0:T(8,128)(2,1)S(1)}, s32[56]{0:T(128)S(1)}) %tuple.30, (bf16[252,32,256]{2,1,0:T(8,128)(2,1)S(1)}, ...), branch_computations={%region_0.0_spmd, %region_1.0_spmd, %region_2.0_spmd} | conditional | bytes 2084 | solution.py:768
  43.5 7.6 %left.1 = bf16[2,12,32,256]{3,2,1,0:T(8,128)(2,1)S(1)} custom-call(bf16[2,12,32,256]{3,2,1,0:T(8,128)(2,1)S(1)} %get-tuple-element.40.left_ref), custom_call_target="tpu_custom_call" | custom-call | tf_op jit(solution)/shard_map/cond/branch_1_fun/left/left/pallas_call | solution.py:714
  51.2 3.2 %place_left.1 = (bf16[4,8,1024]{2,1,0:T(8,128)(2,1)}, bf16[8,64,16,256]{3,2,1,0:T(8,128)(2,1)}) custom-call(bf16[504,16,256]{2,1,0:T(8,128)(2,1)S(1)} %bitcast.12, bf16[4,16,512]{2,1,0:T(8,128)(2,1)S(1)} %get-tuple-element.37.raw_ref, bf16[4,8,256]{2,1,0:T(8,128)(2,1)S(1)} %get-tuple-element.38.new_ref, s32[56]{0:T(128)S(1)} %get-tuple-element.39.meta_ref, ...), custom_call_target="tpu_custom_call" | custom-call | tf_op jit(solution)/shard_map/cond/branch_1_fun/place/place_left/pallas_call | solution.py:691
Async XLA Ops:
  0.6 42.8 %copy-start = (bf16[4,8,256]{2,1,0:T(8,128)(2,1)S(1)}, bf16[4,8,256]{2,1,0:T(8,128)(2,1)}, u32[]{:S(2)}) copy-start(bf16[4,8,256]{2,1,0:T(8,128)(2,1)} %new_hbm.1) | copy-start | bytes 49156
  0.6 42.8 %copy-start.2 = (s32[128]{0:T(128)S(1)}, s32[128]{0:T(128)}, u32[]{:S(2)}) copy-start(s32[128]{0:T(128)} %len_hbm.1) | copy-start | bytes 1540

commit v11 on v10

--- a/solution.py
+++ b/solution.py
@@ -20,7 +20,7 @@
 TILE = 16
 VIA = 36
 MORE = 18
-REST = 40
+REST = 46
 LEFT = 12
 FIRST = VIA + MORE
 LINK = FIRST + REST
@@ -154,6 +154,59 @@
     slots, owners = slots_of_children(par_ref, me)
     plan = ring_plan(par_ref, len_ref, me >> 2)
     up, down, via_up, via_down = plan
+    flows = {}
+    for ahead in range(SPAN):
+        served = served_beams(par_ref, me, peer(ahead))
+        distance = (SPAN - ahead) % SPAN
+        held = [len_ref[me * BEAMS + served[rank]] for rank in range(MOST)]
+        for rank in range(MOST):
+            beams[distance * MOST + rank] = served[rank]
+            lens[distance * MOST + rank] = held[rank]
+        flows[ahead] = (served[0], served[1], grains(held[0]))
+
+    def grain_at(flow, number):
+        first, second, cut = flow
+        later = number >= cut
+        number = jnp.where(later, number - cut, number)
+        number = jnp.minimum(jnp.maximum(number, 0), PER_CHILD - 1)
+        return table_ref[jnp.where(later, second, first), number >> 2] * PER_PAGE + (number & (PER_PAGE - 1))
+
+    sides = (
+        (flows[1], choose(via_up, y), jnp.int32(0), choose(via_up, (y - 1) & 3), peer(1)),
+        (flows[3], choose(via_down, y), choose(via_up, y), choose(via_down, (y + 1) & 3), peer(3)),
+    )
+    pl.semaphore_wait(barrier, SPAN - 1 + mine)
+    for other in range(1, shards):
+        @pl.when(mine >= other)
+        def _(other=other):
+            pl.semaphore_signal(here_sem, inc=1, device_id={"tensor": mine - other}, device_id_type=MESH)
+    for copy in pool_copies:
+        copy.wait()
+    b_copies = []
+    cuts = (0, 8, VIA, FIRST)
+
+    def send_part(part):
+        for side, (flow, mine_via, skip, _, target) in enumerate(sides):
+            def put(at, carry, side=side, flow=flow, mine_via=mine_via, skip=skip):
+                for at in (2 * at, 2 * at + 1):
+                    far = at < mine_via
+                    chosen = tuple(jnp.where(far, one, two) for one, two in zip(flows[2], flow))
+                    number = jnp.where(far, skip + at, at - mine_via)
+                    first_send[side, at] = pool_v[grain_at(chosen, number)]
+                return carry
+
+            lax.fori_loop(cuts[part] // 2, cuts[part + 1] // 2, put, 0)
+            span = pl.ds(cuts[part], cuts[part + 1] - cuts[part])
+            copy = pltpu.make_async_remote_copy(
+                src_ref=first_send.at[side, span], dst_ref=first_recv.at[side, span],
+                send_sem=bs_sem.at[side * 4 + part], recv_sem=br_sem.at[side * 4 + part],
+                device_id={"dp": target}, device_id_type=MESH,
+            )
+            copy.start()
+            b_copies.append(copy)
+
+    send_part(0)
+
     row = lax.broadcasted_iota(jnp.int32, (SPAN * rows, BEAMS), 0)
     col = lax.broadcasted_iota(jnp.int32, (SPAN * rows, BEAMS), 1)
     slot_at = jnp.zeros_like(col)
@@ -174,13 +227,6 @@
             q_recv[0] = part
         else:
             q_send[distance] = part
-
-    pl.semaphore_wait(barrier, SPAN - 1 + mine)
-    for other in range(1, shards):
-        @pl.when(mine >= other)
-        def _(other=other):
-            pl.semaphore_signal(here_sem, inc=1, device_id={"tensor": mine - other}, device_id_type=MESH)
-
     q_copies = []
     for distance in range(1, SPAN):
         copy = pltpu.make_async_remote_copy(
@@ -190,51 +236,8 @@
         )
         copy.start()
         q_copies.append(copy)
-
-    flows = {}
-    for ahead in range(SPAN):
-        served = served_beams(par_ref, me, peer(ahead))
-        distance = (SPAN - ahead) % SPAN
-        held = [len_ref[me * BEAMS + served[rank]] for rank in range(MOST)]
-        for rank in range(MOST):
-            beams[distance * MOST + rank] = served[rank]
-            lens[distance * MOST + rank] = held[rank]
-        flows[ahead] = (served[0], served[1], grains(held[0]))
-
-    def grain_at(flow, number):
-        first, second, cut = flow
-        later = number >= cut
-        number = jnp.where(later, number - cut, number)
-        number = jnp.minimum(jnp.maximum(number, 0), PER_CHILD - 1)
-        return table_ref[jnp.where(later, second, first), number >> 2] * PER_PAGE + (number & (PER_PAGE - 1))
-
-    sides = (
-        (flows[1], choose(via_up, y), jnp.int32(0), choose(via_up, (y - 1) & 3), peer(1)),
-        (flows[3], choose(via_down, y), choose(via_up, y), choose(via_down, (y + 1) & 3), peer(3)),
-    )
-    for copy in pool_copies:
-        copy.wait()
-    b_copies = []
-    cuts = (0, 8, VIA, FIRST)
-    for part in range(3):
-        for side, (flow, mine_via, skip, _, target) in enumerate(sides):
-            def put(at, carry, side=side, flow=flow, mine_via=mine_via, skip=skip):
-                for at in (2 * at, 2 * at + 1):
-                    far = at < mine_via
-                    chosen = tuple(jnp.where(far, one, two) for one, two in zip(flows[2], flow))
-                    number = jnp.where(far, skip + at, at - mine_via)
-                    first_send[side, at] = pool_v[grain_at(chosen, number)]
-                return carry
-
-            lax.fori_loop(cuts[part] // 2, cuts[part + 1] // 2, put, 0)
-            span = pl.ds(cuts[part], cuts[part + 1] - cuts[part])
-            copy = pltpu.make_async_remote_copy(
-                src_ref=first_send.at[side, span], dst_ref=first_recv.at[side, span],
-                send_sem=bs_sem.at[side * 4 + part], recv_sem=br_sem.at[side * 4 + part],
-                device_id={"dp": target}, device_id_type=MESH,
-            )
-            copy.start()
-            b_copies.append(copy)
+    send_part(1)
+    send_part(2)
     w_copies = []
     for block in range(shards):
         copy = pltpu.make_async_copy(w_ref.at[:, pl.ds(block * wide, wide)], w_v.at[block], w_sem.at[block])
@@ -293,55 +296,6 @@
         return carry
 
     lax.fori_loop(0, SPAN, attend, 0)
-    for copy in b_copies[:4]:
-        copy.wait()
-    more_copies = b_copies[4:]
-    b_copies = []
-    for side, (flow, mine_via, _, passed, target) in enumerate(sides):
-        def put_passed(at, carry, side=side, flow=flow, mine_via=mine_via, passed=passed):
-            for at in (2 * at, 2 * at + 1):
-                here = pool_v[grain_at(flow, FIRST - mine_via + at - passed)]
-                rest_send[side, at] = jnp.where(at < passed, first_recv[side, at], here)
-            return carry
-
-        def put_rest(at, carry, side=side, flow=flow, mine_via=mine_via, passed=passed):
-            for at in (2 * at, 2 * at + 1):
-                rest_send[side, at] = pool_v[grain_at(flow, FIRST - mine_via + at - passed)]
-            return carry
-
-        lax.fori_loop(0, VIA // 2, put_passed, 0)
-        lax.fori_loop(VIA // 2, REST // 2, put_rest, 0)
-        copy = pltpu.make_async_remote_copy(
-            src_ref=rest_send.at[side], dst_ref=recv_ref.at[pl.ds(side * LINK + FIRST, REST)],
-            send_sem=bs_sem.at[side * 4 + 3], recv_sem=br_sem.at[side * 4 + 3],
-            device_id={"dp": target}, device_id_type=MESH,
-        )
-        copy.start()
-        b_copies.append(copy)
-    attended = att[...].astype(jnp.bfloat16)
-    for copy in w_copies:
-        copy.wait()
-
-    def p_copy(other):
-        return pltpu.make_async_remote_copy(
-            src_ref=p_send.at[other], dst_ref=p_recv.at[other],
-            send_sem=ps_sem.at[other], recv_sem=pr_sem.at[other],
-            device_id={"tensor": lax.rem(mine + other, shards)}, device_id_type=MESH,
-        )
-
-    def project(other, carry):
-        product = jnp.dot(attended, w_v[lax.rem(mine + other, shards)], preferred_element_type=jnp.float32)
-        p_send[other] = product.astype(jnp.bfloat16)
-        p_copy(other).start()
-        return carry
-
-    @pl.when(mine < shards - 1)
-    def _():
-        pl.semaphore_wait(here_sem, shards - 1 - mine)
-
-    lax.fori_loop(1, shards, project, 0)
-    own = jnp.dot(attended, w_v[mine], preferred_element_type=jnp.float32)
-
     load = lax.fori_loop(
         0, rings, lambda ring, load: jnp.maximum(load, heaviest(ring_plan(par_ref, len_ref, ring))), jnp.int32(0)
     )
@@ -352,9 +306,8 @@
             return carry
 
         lax.fori_loop(0, LEFT, put_left, 0)
-    copy = pltpu.make_async_copy(left_send, left_ref, land_sem.at[2])
-    copy.start()
-    b_copies.append(copy)
+    left_copy = pltpu.make_async_copy(left_send, left_ref, land_sem.at[2])
+    left_copy.start()
     for child in range(BEAMS):
         slot = slots[child]
         distance = slot >> 1
@@ -386,6 +339,55 @@
         meta_ref[child * META + 4] = until
         meta_ref[child * META + 5] = jnp.where(near, third, 0)
         meta_ref[child * META + 6] = slot
+    for copy in b_copies[:4]:
+        copy.wait()
+    more_copies = b_copies[4:]
+    b_copies = []
+    for side, (flow, mine_via, _, passed, target) in enumerate(sides):
+        def put_passed(at, carry, side=side, flow=flow, mine_via=mine_via, passed=passed):
+            for at in (2 * at, 2 * at + 1):
+                here = pool_v[grain_at(flow, FIRST - mine_via + at - passed)]
+                rest_send[side, at] = jnp.where(at < passed, first_recv[side, at], here)
+            return carry
+
+        def put_rest(at, carry, side=side, flow=flow, mine_via=mine_via, passed=passed):
+            for at in (2 * at, 2 * at + 1):
+                rest_send[side, at] = pool_v[grain_at(flow, FIRST - mine_via + at - passed)]
+            return carry
+
+        lax.fori_loop(0, VIA // 2, put_passed, 0)
+        lax.fori_loop(VIA // 2, REST // 2, put_rest, 0)
+        copy = pltpu.make_async_remote_copy(
+            src_ref=rest_send.at[side], dst_ref=recv_ref.at[pl.ds(side * LINK + FIRST, REST)],
+            send_sem=bs_sem.at[side * 4 + 3], recv_sem=br_sem.at[side * 4 + 3],
+            device_id={"dp": target}, device_id_type=MESH,
+        )
+        copy.start()
+        b_copies.append(copy)
+    attended = att[...].astype(jnp.bfloat16)
+    for copy in w_copies:
+        copy.wait()
+
+    def p_copy(other):
+        return pltpu.make_async_remote_copy(
+            src_ref=p_send.at[other], dst_ref=p_recv.at[other],
+            send_sem=ps_sem.at[other], recv_sem=pr_sem.at[other],
+            device_id={"tensor": lax.rem(mine + other, shards)}, device_id_type=MESH,
+        )
+
+    def project(other, carry):
+        product = jnp.dot(attended, w_v[lax.rem(mine + other, shards)], preferred_element_type=jnp.float32)
+        p_send[other] = product.astype(jnp.bfloat16)
+        p_copy(other).start()
+        return carry
+
+    @pl.when(mine < shards - 1)
+    def _():
+        pl.semaphore_wait(here_sem, shards - 1 - mine)
+
+    lax.fori_loop(1, shards, project, 0)
+    own = jnp.dot(attended, w_v[mine], preferred_element_type=jnp.float32)
+
     for copy in more_copies:
         copy.wait()
     for side in range(2):
@@ -418,6 +420,7 @@
     for copy in b_copies:
         copy.wait()
     own_copy.wait()
+    left_copy.wait()
 
 
 def full_kernel(
@@ -557,7 +560,7 @@
 
 def place_kernel(with_left, recv_ref, raw_ref, new_ref, meta_ref, *refs):
     left_ref = refs[0] if with_left else None
-    proj_ref, cache_ref, edge, zeros, out_sem = refs[-5:]
+    proj_hbm, cache_ref, edge, zeros, proj_ref, out_sem, proj_sem = refs[-7:]
     total = recv_ref.shape[0]
     zeros[...] = jnp.zeros_like(zeros)
     fresh = [new_ref[step].astype(jnp.float32) for step in range(STEPS)]
@@ -621,7 +624,10 @@
     for step in range(STEPS):
         pick = jnp.where(col == slot_at * STEPS + step, 1.0, 0.0).astype(jnp.bfloat16)
         proj_ref[step] = jnp.dot(pick, raw, preferred_element_type=jnp.float32).astype(jnp.bfloat16)
+    proj_copy = pltpu.make_async_copy(proj_ref, proj_hbm, proj_sem)
+    proj_copy.start()
     pltpu.make_async_copy(cache_ref, cache_ref, out_sem).wait()
+    proj_copy.wait()
 
 
 def local(shards, queries, new_kv, kv_pool, page_tables, lengths, parents, out_weight):
@@ -695,11 +701,12 @@
                     jax.ShapeDtypeStruct((BEAMS, context // TILE, TILE, channels), bf16),
                 ),
                 in_specs=[vmem, vmem, vmem, smem] + [vmem] * len(got),
-                out_specs=(vmem, free),
+                out_specs=(free, free),
                 scratch_shapes=[
                     pltpu.VMEM((2 * BEAMS, TILE, channels), bf16),
                     pltpu.VMEM((context // TILE, TILE, channels), bf16),
-                    dma,
+                    pltpu.VMEM(queries.shape, bf16),
+                    dma, dma,
                 ],
                 compiler_params=pltpu.CompilerParams(vmem_limit_bytes=24 * 1024 * 1024),
                 name="place_left" if got else "place",

time: 54.5 us -> 48.3 us (0.89)
  Pallas kernels: 53 us -> 46.9 us
    pallas_call x1 -> x0, Pallas kernels: 7.64 us -> none  [topped(): pl.pallas_call(left_kernel, out_shape=jax.ShapeDtypeStruct(left.shape, bf...]
    pallas_call x1, Pallas kernels: 42.2 us -> 44.3 us  [local(): pl.pallas_call(exchange_kernel, out_shape=(jax.ShapeDtypeStruct((2 * LINK...]
    pallas_call x1, Pallas kernels: 3.18 us -> 2.59 us  [place(): pl.pallas_call(functools.partial(place_kernel, len(got) > 0), out_shape=(...]
where the time goes in v11:
time: 48.3 us; the launch traced here: 48.2 us
  Pallas kernels  46.9 us (97%)
  between operations  1.3 us (3%)
    pallas_call x1, Pallas kernels, local(): pl.pallas_call(exchange_kernel, out_shape=(jax.ShapeDtypeStruct((2 * LINK...  44.3 us
    pallas_call x1, Pallas kernels, place(): pl.pallas_call(functools.partial(place_kernel, len(got) > 0), out_shape=(...  2.59 us

profile of v11, /device:TPU:0, one launch (start us, length us, event | category | flops | bytes accessed | tf_op | source)
XLA Modules:
  0.0 48.2 jit_solution(6242430061287851079)
XLA Ops:
  0.6 0.0 copy-start
  0.6 0.0 copy-start.2
  0.7 44.3 %exchange.1 = (bf16[264,32,256]{2,1,0:T(8,128)(2,1)S(1)}, bf16[4,16,512]{2,1,0:T(8,128)(2,1)S(1)}, bf16[2,12,32,256]{3,2,1,0:T(8,128)(2,1)S(1)}, s32[56]{0:T(128)S(1)}, s32[1]{0:T(128)}) custom-call(bf16[4,8,1024]{2,1,0:T(8,128)(2,1)} %q_hbm.1, bf16[4,8,256]{2,1,0:T(8,128)(2,1)} %new_hbm.1, bf16[256,32,256]{2,1,0:T(8,128)(2,1)} %bitcast.12, ...), custom_call_target="tpu_custom_call" | custom-call | tf_op jit(solution)/shard_map/exchange/exchange/pallas_call | solution.py:650
  45.6 0.0 copy-done
  45.6 0.0 copy-done.2
  45.6 2.6 %conditional.1 = ((bf16[4,8,1024]{2,1,0:T(8,128)(2,1)}, bf16[8,1024,256]{2,1,0:T(8,128)(2,1)})) conditional(s32[]{:T(128)} %bitcast.7, (bf16[264,32,256]{2,1,0:T(8,128)(2,1)S(1)}, bf16[4,16,512]{2,1,0:T(8,128)(2,1)S(1)}, bf16[4,8,256]{2,1,0:T(8,128)(2,1)S(1)}, s32[56]{0:T(128)S(1)}) %tuple.30, (bf16[264,32,256]{2,1,0:T(8,128)(2,1)S(1)}, ...), branch_computations={%region_0.0_spmd, %region_1.0_spmd, %region_2.0_spmd} | conditional | bytes 2084 | solution.py:775
  45.6 2.6 %place.1 = (bf16[4,8,1024]{2,1,0:T(8,128)(2,1)}, bf16[8,64,16,256]{3,2,1,0:T(8,128)(2,1)}) custom-call(bf16[528,16,256]{2,1,0:T(8,128)(2,1)S(1)} %bitcast.10, bf16[4,16,512]{2,1,0:T(8,128)(2,1)S(1)} %get-tuple-element.31.raw_ref, bf16[4,8,256]{2,1,0:T(8,128)(2,1)S(1)} %get-tuple-element.32.new_ref, s32[56]{0:T(128)S(1)} %get-tuple-element.33.meta_ref), custom_call_target="tpu_custom_call" | custom-call | tf_op jit(solution)/shard_map/cond/branch_0_fun/place/place/pallas_call | solution.py:697
Async XLA Ops:
  0.6 45.0 %copy-start = (bf16[4,8,256]{2,1,0:T(8,128)(2,1)S(1)}, bf16[4,8,256]{2,1,0:T(8,128)(2,1)}, u32[]{:S(2)}) copy-start(bf16[4,8,256]{2,1,0:T(8,128)(2,1)} %new_hbm.1) | copy-start | bytes 49156
  0.6 45.0 %copy-start.2 = (s32[128]{0:T(128)S(1)}, s32[128]{0:T(128)}, u32[]{:S(2)}) copy-start(s32[128]{0:T(128)} %len_hbm.1) | copy-start | bytes 1540

commit v12 on v11

--- a/solution.py
+++ b/solution.py
@@ -19,8 +19,8 @@
 PER_PAGE = PAGE // GRAIN
 TILE = 16
 VIA = 36
-MORE = 18
-REST = 46
+MORE = 28
+REST = 36
 LEFT = 12
 FIRST = VIA + MORE
 LINK = FIRST + REST
@@ -296,6 +296,76 @@
         return carry
 
     lax.fori_loop(0, SPAN, attend, 0)
+    for copy in b_copies[:4]:
+        copy.wait()
+    more_copies = b_copies[4:]
+    b_copies = []
+    for side, (flow, mine_via, _, passed, target) in enumerate(sides):
+        def put_passed(at, carry, side=side, flow=flow, mine_via=mine_via, passed=passed):
+            for at in (2 * at, 2 * at + 1):
+                here = pool_v[grain_at(flow, FIRST - mine_via + at - passed)]
+                rest_send[side, at] = jnp.where(at < passed, first_recv[side, at], here)
+            return carry
+
+        lax.fori_loop(0, REST // 2, put_passed, 0)
+        copy = pltpu.make_async_remote_copy(
+            src_ref=rest_send.at[side], dst_ref=recv_ref.at[pl.ds(side * LINK + FIRST, REST)],
+            send_sem=bs_sem.at[side * 4 + 3], recv_sem=br_sem.at[side * 4 + 3],
+            device_id={"dp": target}, device_id_type=MESH,
+        )
+        copy.start()
+        b_copies.append(copy)
+    attended = att[...].astype(jnp.bfloat16)
+    for copy in w_copies:
+        copy.wait()
+
+    def p_copy(other):
+        return pltpu.make_async_remote_copy(
+            src_ref=p_send.at[other], dst_ref=p_recv.at[other],
+            send_sem=ps_sem.at[other], recv_sem=pr_sem.at[other],
+            device_id={"tensor": lax.rem(mine + other, shards)}, device_id_type=MESH,
+        )
+
+    def project(other, carry):
+        product = jnp.dot(attended, w_v[lax.rem(mine + other, shards)], preferred_element_type=jnp.float32)
+        p_send[other] = product.astype(jnp.bfloat16)
+        p_copy(other).start()
+        return carry
+
+    @pl.when(mine < shards - 1)
+    def _():
+        pl.semaphore_wait(here_sem, shards - 1 - mine)
+
+    lax.fori_loop(1, shards, project, 0)
+    own = jnp.dot(attended, w_v[mine], preferred_element_type=jnp.float32)
+
+    for copy in more_copies:
+        copy.wait()
+    for side in range(2):
+        copy = pltpu.make_async_copy(first_recv.at[side], recv_ref.at[pl.ds(side * LINK, FIRST)], land_sem.at[side])
+        copy.start()
+        b_copies.append(copy)
+
+    def gather_sums(other, total):
+        p_copy(other).wait()
+        return total + p_recv[other].astype(jnp.float32)
+
+    summed = lax.fori_loop(1, shards, gather_sums, own)
+    half = wide // 2
+    r_copies = []
+    for distance in range(SPAN):
+        part = summed[distance * rows:(distance + 1) * rows]
+        r_send[distance] = jnp.concatenate([part[:, :half], part[:, half:]], axis=0).astype(jnp.bfloat16)
+        if distance == 0:
+            copy = pltpu.make_async_copy(r_send.at[0], proj_ref.at[0], own_sem.at[1])
+        else:
+            copy = pltpu.make_async_remote_copy(
+                src_ref=r_send.at[distance], dst_ref=proj_ref.at[distance],
+                send_sem=rs_sem.at[distance], recv_sem=rr_sem.at[distance],
+                device_id={"dp": peer(SPAN - distance)}, device_id_type=MESH,
+            )
+        copy.start()
+        r_copies.append(copy)
     load = lax.fori_loop(
         0, rings, lambda ring, load: jnp.maximum(load, heaviest(ring_plan(par_ref, len_ref, ring))), jnp.int32(0)
     )
@@ -339,82 +409,6 @@
         meta_ref[child * META + 4] = until
         meta_ref[child * META + 5] = jnp.where(near, third, 0)
         meta_ref[child * META + 6] = slot
-    for copy in b_copies[:4]:
-        copy.wait()
-    more_copies = b_copies[4:]
-    b_copies = []
-    for side, (flow, mine_via, _, passed, target) in enumerate(sides):
-        def put_passed(at, carry, side=side, flow=flow, mine_via=mine_via, passed=passed):
-            for at in (2 * at, 2 * at + 1):
-                here = pool_v[grain_at(flow, FIRST - mine_via + at - passed)]
-                rest_send[side, at] = jnp.where(at < passed, first_recv[side, at], here)
-            return carry
-
-        def put_rest(at, carry, side=side, flow=flow, mine_via=mine_via, passed=passed):
-            for at in (2 * at, 2 * at + 1):
-                rest_send[side, at] = pool_v[grain_at(flow, FIRST - mine_via + at - passed)]
-            return carry
-
-        lax.fori_loop(0, VIA // 2, put_passed, 0)
-        lax.fori_loop(VIA // 2, REST // 2, put_rest, 0)
-        copy = pltpu.make_async_remote_copy(
-            src_ref=rest_send.at[side], dst_ref=recv_ref.at[pl.ds(side * LINK + FIRST, REST)],
-            send_sem=bs_sem.at[side * 4 + 3], recv_sem=br_sem.at[side * 4 + 3],
-            device_id={"dp": target}, device_id_type=MESH,
-        )
-        copy.start()
-        b_copies.append(copy)
-    attended = att[...].astype(jnp.bfloat16)
-    for copy in w_copies:
-        copy.wait()
-
-    def p_copy(other):
-        return pltpu.make_async_remote_copy(
-            src_ref=p_send.at[other], dst_ref=p_recv.at[other],
-            send_sem=ps_sem.at[other], recv_sem=pr_sem.at[other],
-            device_id={"tensor": lax.rem(mine + other, shards)}, device_id_type=MESH,
-        )
-
-    def project(other, carry):
-        product = jnp.dot(attended, w_v[lax.rem(mine + other, shards)], preferred_element_type=jnp.float32)
-        p_send[other] = product.astype(jnp.bfloat16)
-        p_copy(other).start()
-        return carry
-
-    @pl.when(mine < shards - 1)
-    def _():
-        pl.semaphore_wait(here_sem, shards - 1 - mine)
-
-    lax.fori_loop(1, shards, project, 0)
-    own = jnp.dot(attended, w_v[mine], preferred_element_type=jnp.float32)
-
-    for copy in more_copies:
-        copy.wait()
-    for side in range(2):
-        copy = pltpu.make_async_copy(first_recv.at[side], recv_ref.at[pl.ds(side * LINK, FIRST)], land_sem.at[side])
-        copy.start()
-        b_copies.append(copy)
-
-    def gather_sums(other, total):
-        p_copy(other).wait()
-        return total + p_recv[other].astype(jnp.float32)
-
-    summed = lax.fori_loop(1, shards, gather_sums, own)
-    half = wide // 2
-    r_copies = []
-    for distance in range(SPAN):
-        part = summed[distance * rows:(distance + 1) * rows]
-        r_send[distance] = jnp.concatenate([part[:, :half], part[:, half:]], axis=0).astype(jnp.bfloat16)
-        if distance == 0:
-            copy = pltpu.make_async_copy(r_send.at[0], proj_ref.at[0], own_sem.at[1])
-        else:
-            copy = pltpu.make_async_remote_copy(
-                src_ref=r_send.at[distance], dst_ref=proj_ref.at[distance],
-                send_sem=rs_sem.at[distance], recv_sem=rr_sem.at[distance],
-                device_id={"dp": peer(SPAN - distance)}, device_id_type=MESH,
-            )
-        copy.start()
-        r_copies.append(copy)
     for copy in r_copies:
         copy.wait()
     for copy in b_copies:

time: 48.3 us -> 48.3 us (level)
  no operation moved by 1% of the time
where the time goes in v12:
time: 48.3 us; the launch traced here: 48.2 us
  Pallas kernels  46.9 us (97%)
  between operations  1.3 us (3%)
    pallas_call x1, Pallas kernels, local(): pl.pallas_call(exchange_kernel, out_shape=(jax.ShapeDtypeStruct((2 * LINK...  44.3 us
    pallas_call x1, Pallas kernels, place(): pl.pallas_call(functools.partial(place_kernel, len(got) > 0), out_shape=(...  2.59 us

profile of v12, /device:TPU:0, one launch (start us, length us, event | category | flops | bytes accessed | tf_op | source)
XLA Modules:
  0.0 48.2 jit_solution(3234771212905432824)
XLA Ops:
  0.6 0.0 copy-start
  0.6 0.0 copy-start.2
  0.7 44.3 %exchange.1 = (bf16[264,32,256]{2,1,0:T(8,128)(2,1)S(1)}, bf16[4,16,512]{2,1,0:T(8,128)(2,1)S(1)}, bf16[2,12,32,256]{3,2,1,0:T(8,128)(2,1)S(1)}, s32[56]{0:T(128)S(1)}, s32[1]{0:T(128)}) custom-call(bf16[4,8,1024]{2,1,0:T(8,128)(2,1)} %q_hbm.1, bf16[4,8,256]{2,1,0:T(8,128)(2,1)} %new_hbm.1, bf16[256,32,256]{2,1,0:T(8,128)(2,1)} %bitcast.12, ...), custom_call_target="tpu_custom_call" | custom-call | tf_op jit(solution)/shard_map/exchange/exchange/pallas_call | solution.py:644
  45.6 0.0 copy-done
  45.6 0.0 copy-done.2
  45.6 2.6 %conditional.1 = ((bf16[4,8,1024]{2,1,0:T(8,128)(2,1)}, bf16[8,1024,256]{2,1,0:T(8,128)(2,1)})) conditional(s32[]{:T(128)} %bitcast.7, (bf16[264,32,256]{2,1,0:T(8,128)(2,1)S(1)}, bf16[4,16,512]{2,1,0:T(8,128)(2,1)S(1)}, bf16[4,8,256]{2,1,0:T(8,128)(2,1)S(1)}, s32[56]{0:T(128)S(1)}) %tuple.30, (bf16[264,32,256]{2,1,0:T(8,128)(2,1)S(1)}, ...), branch_computations={%region_0.0_spmd, %region_1.0_spmd, %region_2.0_spmd} | conditional | bytes 2084 | solution.py:769
  45.6 2.6 %place.1 = (bf16[4,8,1024]{2,1,0:T(8,128)(2,1)}, bf16[8,64,16,256]{3,2,1,0:T(8,128)(2,1)}) custom-call(bf16[528,16,256]{2,1,0:T(8,128)(2,1)S(1)} %bitcast.10, bf16[4,16,512]{2,1,0:T(8,128)(2,1)S(1)} %get-tuple-element.31.raw_ref, bf16[4,8,256]{2,1,0:T(8,128)(2,1)S(1)} %get-tuple-element.32.new_ref, s32[56]{0:T(128)S(1)} %get-tuple-element.33.meta_ref), custom_call_target="tpu_custom_call" | custom-call | tf_op jit(solution)/shard_map/cond/branch_0_fun/place/place/pallas_call | solution.py:691
Async XLA Ops:
  0.6 45.0 %copy-start = (bf16[4,8,256]{2,1,0:T(8,128)(2,1)S(1)}, bf16[4,8,256]{2,1,0:T(8,128)(2,1)}, u32[]{:S(2)}) copy-start(bf16[4,8,256]{2,1,0:T(8,128)(2,1)} %new_hbm.1) | copy-start | bytes 49156
  0.6 45.0 %copy-start.2 = (s32[128]{0:T(128)S(1)}, s32[128]{0:T(128)}, u32[]{:S(2)}) copy-start(s32[128]{0:T(128)} %len_hbm.1) | copy-start | bytes 1540

commit v13 on v12

--- a/solution.py
+++ b/solution.py
@@ -39,6 +39,19 @@
     return out
 
 
+def balanced(up, far, down):
+    via_up = [jnp.minimum(count >> 1, VIA) for count in far]
+    for at in range(SPAN):
+        via_down = [far[i] - via_up[i] for i in range(SPAN)]
+        nxt, prv = (at + 1) % SPAN, (at - 1) % SPAN
+        load_up = jnp.maximum(up[at] + via_up[prv], up[nxt] + via_up[nxt])
+        load_down = jnp.maximum(down[at] + via_down[nxt], down[prv] + via_down[prv])
+        best = (load_down + far[at] - load_up) >> 1
+        via_up[at] = jnp.minimum(jnp.maximum(best, jnp.maximum(far[at] - VIA, 0)), jnp.minimum(far[at], VIA))
+    via_down = [far[i] - via_up[i] for i in range(SPAN)]
+    return via_up, via_down
+
+
 def ring_plan(parents, lengths, ring):
     flows = [[jnp.int32(0)] * SPAN for _ in range(SPAN)]
     for target in range(SPAN):
@@ -57,26 +70,40 @@
     up = [flow[1] for flow in flows]
     far = [flow[2] for flow in flows]
     down = [flow[3] for flow in flows]
-    via_up = [jnp.minimum(count >> 1, VIA) for count in far]
-    for at in range(SPAN):
-        via_down = [far[i] - via_up[i] for i in range(SPAN)]
-        nxt, prv = (at + 1) % SPAN, (at - 1) % SPAN
-        load_up = jnp.maximum(up[at] + via_up[prv], up[nxt] + via_up[nxt])
-        load_down = jnp.maximum(down[at] + via_down[nxt], down[prv] + via_down[prv])
-        best = (load_down + far[at] - load_up) >> 1
-        via_up[at] = jnp.minimum(jnp.maximum(best, jnp.maximum(far[at] - VIA, 0)), jnp.minimum(far[at], VIA))
-    via_down = [far[i] - via_up[i] for i in range(SPAN)]
+    via_up, via_down = balanced(up, far, down)
     return up, down, via_up, via_down
 
 
-def heaviest(plan):
-    up, down, via_up, via_down = plan
-    out = jnp.int32(0)
+def heaviest(parents, lengths, rings):
+    beams = rings * SPAN * BEAMS
+    counts = grains(lengths).astype(jnp.float32).astype(jnp.bfloat16)
+    beam = lax.broadcasted_iota(jnp.int32, (beams, beams), 0)
+    chosen = jnp.where(beam == parents, 1.0, 0.0).astype(jnp.bfloat16)
+    counts = jnp.dot(jnp.broadcast_to(counts, (16, beams)), chosen, preferred_element_type=jnp.float32)[:1]
+    lane = lax.broadcasted_iota(jnp.int32, (1, beams), 1)
+    for back in range(1, BEAMS):
+        same = (pltpu.roll(parents, back, 1) == parents) & (lane % BEAMS >= back)
+        counts = jnp.where(same, 0.0, counts)
+    source = (parents // BEAMS) % SPAN
+    rows = jnp.concatenate([jnp.where(source == at, counts, 0.0) for at in range(SPAN)] * 4, axis=0).astype(jnp.bfloat16)
+    child = lax.broadcasted_iota(jnp.int32, (beams, 128), 0)
+    ring = lax.broadcasted_iota(jnp.int32, (beams, 128), 1)
+    flows = []
+    for target in range(SPAN):
+        member = (child // BEAMS % SPAN == target) & (child // (BEAMS * SPAN) == ring)
+        flows.append(jnp.dot(rows, jnp.where(member, 1.0, 0.0).astype(jnp.bfloat16), preferred_element_type=jnp.float32))
+
+    def flow(at, ahead):
+        return flows[(at + ahead) % SPAN][at:at + 1].astype(jnp.int32)
+
+    up, far, down = ([flow(at, ahead) for at in range(SPAN)] for ahead in (1, 2, 3))
+    via_up, via_down = balanced(up, far, down)
+    out = jnp.zeros_like(up[0])
     for at in range(SPAN):
         load_up = up[at] + via_up[at] + via_up[(at - 1) % SPAN]
         load_down = down[at] + via_down[at] + via_down[(at + 1) % SPAN]
         out = jnp.maximum(out, jnp.maximum(load_up, load_down))
-    return out
+    return jnp.max(out)
 
 
 def slots_of_children(parents, me):
@@ -110,7 +137,7 @@
 def exchange_kernel(
     q_hbm, new_hbm, pool_ref, table_hbm, len_hbm, par_hbm, w_ref,
     recv_ref, proj_ref, left_ref, meta_ref, over_ref,
-    q_ref, new_ref, table_ref, len_ref, par_ref,
+    q_ref, new_ref, table_ref, len_ref, par_ref, len_row, par_row,
     pool_v, w_v, stage, first_send, first_recv, rest_send, left_send, q_send, q_recv, att, p_send, p_recv, r_send, lens, beams,
     in_sem, pool_sem, w_sem, own_sem, land_sem, qs_sem, qr_sem, bs_sem, br_sem, ps_sem, pr_sem, rs_sem, rr_sem, here_sem,
 ):
@@ -137,10 +164,16 @@
             pl.semaphore_signal(barrier, inc=1, device_id={"tensor": mine + other}, device_id_type=MESH)
     in_copies = []
     operands = ((par_hbm, par_ref), (q_hbm, q_ref), (new_hbm, new_ref), (table_hbm, table_ref), (len_hbm, len_ref))
+    rows_in = ((par_hbm, par_row.at[0]), (len_hbm, len_row.at[0]))
     for at, (source, target) in enumerate(operands):
         copy = pltpu.make_async_copy(source, target, in_sem.at[at])
         copy.start()
         in_copies.append(copy)
+    row_copies = []
+    for at, (source, target) in enumerate(rows_in):
+        copy = pltpu.make_async_copy(source, target, in_sem.at[5 + at])
+        copy.start()
+        row_copies.append(copy)
     quarter = pool_v.shape[0] // 4
     pool_copies = []
     for at in range(4):
@@ -188,14 +221,14 @@
     def send_part(part):
         for side, (flow, mine_via, skip, _, target) in enumerate(sides):
             def put(at, carry, side=side, flow=flow, mine_via=mine_via, skip=skip):
-                for at in (2 * at, 2 * at + 1):
+                for at in [4 * at + more for more in range(4)]:
                     far = at < mine_via
                     chosen = tuple(jnp.where(far, one, two) for one, two in zip(flows[2], flow))
                     number = jnp.where(far, skip + at, at - mine_via)
                     first_send[side, at] = pool_v[grain_at(chosen, number)]
                 return carry
 
-            lax.fori_loop(cuts[part] // 2, cuts[part + 1] // 2, put, 0)
+            lax.fori_loop(cuts[part] // 4, cuts[part + 1] // 4, put, 0)
             span = pl.ds(cuts[part], cuts[part + 1] - cuts[part])
             copy = pltpu.make_async_remote_copy(
                 src_ref=first_send.at[side, span], dst_ref=first_recv.at[side, span],
@@ -258,7 +291,7 @@
     for copy in q_copies:
         copy.wait()
 
-    def attend(distance, carry):
+    def attend(distance):
         message = q_recv[distance].astype(jnp.float32)
         message = jnp.concatenate([message[:rows], message[rows:]], axis=1)
         q_rows = jnp.concatenate([message[:, h * HD:(h + 1) * HD] for h in range(heads)], axis=0).astype(jnp.bfloat16)
@@ -293,21 +326,25 @@
         out += jnp.dot(w_new, fresh[:, HD:], preferred_element_type=jnp.float32)
         out = jnp.concatenate([out[h * rows:(h + 1) * rows] for h in range(heads)], axis=1)
         att[pl.ds(pl.multiple_of(distance * rows, rows), rows), :] = out
+
+    def attend_two(at, carry):
+        attend(2 * at)
+        attend(2 * at + 1)
         return carry
 
-    lax.fori_loop(0, SPAN, attend, 0)
+    lax.fori_loop(0, SPAN // 2, attend_two, 0)
     for copy in b_copies[:4]:
         copy.wait()
     more_copies = b_copies[4:]
     b_copies = []
     for side, (flow, mine_via, _, passed, target) in enumerate(sides):
         def put_passed(at, carry, side=side, flow=flow, mine_via=mine_via, passed=passed):
-            for at in (2 * at, 2 * at + 1):
+            for at in [4 * at + more for more in range(4)]:
                 here = pool_v[grain_at(flow, FIRST - mine_via + at - passed)]
                 rest_send[side, at] = jnp.where(at < passed, first_recv[side, at], here)
             return carry
 
-        lax.fori_loop(0, REST // 2, put_passed, 0)
+        lax.fori_loop(0, REST // 4, put_passed, 0)
         copy = pltpu.make_async_remote_copy(
             src_ref=rest_send.at[side], dst_ref=recv_ref.at[pl.ds(side * LINK + FIRST, REST)],
             send_sem=bs_sem.at[side * 4 + 3], recv_sem=br_sem.at[side * 4 + 3],
@@ -366,16 +403,17 @@
             )
         copy.start()
         r_copies.append(copy)
-    load = lax.fori_loop(
-        0, rings, lambda ring, load: jnp.maximum(load, heaviest(ring_plan(par_ref, len_ref, ring))), jnp.int32(0)
-    )
+    for copy in row_copies:
+        copy.wait()
+    load = heaviest(par_row[...], len_row[...], rings)
     over_ref[0] = jnp.where(load > LINK, 1, 0) + jnp.where(load > LINK + LEFT, 1, 0)
     for side, (flow, mine_via, _, passed, _) in enumerate(sides):
         def put_left(at, carry, side=side, flow=flow, mine_via=mine_via, passed=passed):
-            left_send[side, at] = pool_v[grain_at(flow, LINK - mine_via - passed + at)]
+            for at in [4 * at + more for more in range(4)]:
+                left_send[side, at] = pool_v[grain_at(flow, LINK - mine_via - passed + at)]
             return carry
 
-        lax.fori_loop(0, LEFT, put_left, 0)
+        lax.fori_loop(0, LEFT // 4, put_left, 0)
     left_copy = pltpu.make_async_copy(left_send, left_ref, land_sem.at[2])
     left_copy.start()
     for child in range(BEAMS):
@@ -658,6 +696,8 @@
                 pltpu.SMEM(page_tables.shape, jnp.int32),
                 pltpu.SMEM(lengths.shape, jnp.int32),
                 pltpu.SMEM(parents.shape, jnp.int32),
+                pltpu.VMEM((1, *lengths.shape), jnp.int32),
+                pltpu.VMEM((1, *parents.shape), jnp.int32),
                 pltpu.VMEM(grain_pool.shape, bf16),
                 pltpu.VMEM((shards, out_weight.shape[0], wide), bf16),
                 pltpu.VMEM((SPAN, MOST * PER_CHILD, GRAIN, channels), bf16),
@@ -673,7 +713,7 @@
                 pltpu.VMEM((SPAN, 2 * rows, wide // 2), bf16),
                 pltpu.SMEM((SPAN * MOST,), jnp.int32),
                 pltpu.SMEM((SPAN * MOST,), jnp.int32),
-                dma((5,)), dma((4,)), dma((shards,)), dma((2,)), dma((3,)),
+                dma((7,)), dma((4,)), dma((shards,)), dma((2,)), dma((3,)),
                 dma((SPAN,)), dma((SPAN,)),
                 dma((8,)), dma((8,)),
                 dma((shards,)), dma((shards,)),

time: 48.3 us -> 48.2 us (level)
  no operation moved by 1% of the time
where the time goes in v13:
time: 48.2 us; the launch traced here: 48.1 us
  Pallas kernels  46.8 us (97%)
  between operations  1.3 us (3%)
    pallas_call x1, Pallas kernels, local(): pl.pallas_call(exchange_kernel, out_shape=(jax.ShapeDtypeStruct((2 * LINK...  44.2 us
    pallas_call x1, Pallas kernels, place(): pl.pallas_call(functools.partial(place_kernel, len(got) > 0), out_shape=(...  2.59 us

profile of v13, /device:TPU:0, one launch (start us, length us, event | category | flops | bytes accessed | tf_op | source)
XLA Modules:
  0.0 48.1 jit_solution(671969038183088093)
XLA Ops:
  0.6 0.0 copy-start
  0.6 0.0 copy-start.2
  0.7 44.2 %exchange.1 = (bf16[264,32,256]{2,1,0:T(8,128)(2,1)S(1)}, bf16[4,16,512]{2,1,0:T(8,128)(2,1)S(1)}, bf16[2,12,32,256]{3,2,1,0:T(8,128)(2,1)S(1)}, s32[56]{0:T(128)S(1)}, s32[1]{0:T(128)}) custom-call(bf16[4,8,1024]{2,1,0:T(8,128)(2,1)} %q_hbm.1, bf16[4,8,256]{2,1,0:T(8,128)(2,1)} %new_hbm.1, bf16[256,32,256]{2,1,0:T(8,128)(2,1)} %bitcast.12, ...), custom_call_target="tpu_custom_call" | custom-call | tf_op jit(solution)/shard_map/exchange/exchange/pallas_call | solution.py:682
  45.5 0.0 copy-done
  45.5 0.0 copy-done.2
  45.5 2.6 %conditional.1 = ((bf16[4,8,1024]{2,1,0:T(8,128)(2,1)}, bf16[8,1024,256]{2,1,0:T(8,128)(2,1)})) conditional(s32[]{:T(128)} %bitcast.7, (bf16[264,32,256]{2,1,0:T(8,128)(2,1)S(1)}, bf16[4,16,512]{2,1,0:T(8,128)(2,1)S(1)}, bf16[4,8,256]{2,1,0:T(8,128)(2,1)S(1)}, s32[56]{0:T(128)S(1)}) %tuple.30, (bf16[264,32,256]{2,1,0:T(8,128)(2,1)S(1)}, ...), branch_computations={%region_0.0_spmd, %region_1.0_spmd, %region_2.0_spmd} | conditional | bytes 2084 | solution.py:809
  45.5 2.6 %place.1 = (bf16[4,8,1024]{2,1,0:T(8,128)(2,1)}, bf16[8,64,16,256]{3,2,1,0:T(8,128)(2,1)}) custom-call(bf16[528,16,256]{2,1,0:T(8,128)(2,1)S(1)} %bitcast.10, bf16[4,16,512]{2,1,0:T(8,128)(2,1)S(1)} %get-tuple-element.31.raw_ref, bf16[4,8,256]{2,1,0:T(8,128)(2,1)S(1)} %get-tuple-element.32.new_ref, s32[56]{0:T(128)S(1)} %get-tuple-element.33.meta_ref), custom_call_target="tpu_custom_call" | custom-call | tf_op jit(solution)/shard_map/cond/branch_0_fun/place/place/pallas_call | solution.py:731
Async XLA Ops:
  0.6 44.9 %copy-start = (bf16[4,8,256]{2,1,0:T(8,128)(2,1)S(1)}, bf16[4,8,256]{2,1,0:T(8,128)(2,1)}, u32[]{:S(2)}) copy-start(bf16[4,8,256]{2,1,0:T(8,128)(2,1)} %new_hbm.1) | copy-start | bytes 49156
  0.6 44.9 %copy-start.2 = (s32[128]{0:T(128)S(1)}, s32[128]{0:T(128)}, u32[]{:S(2)}) copy-start(s32[128]{0:T(128)} %len_hbm.1) | copy-start | bytes 1540

commit v14 on v13

--- a/solution.py
+++ b/solution.py
@@ -19,7 +19,7 @@
 PER_PAGE = PAGE // GRAIN
 TILE = 16
 VIA = 36
-MORE = 28
+MORE = 24
 REST = 36
 LEFT = 12
 FIRST = VIA + MORE
@@ -39,39 +39,68 @@
     return out
 
 
-def balanced(up, far, down):
-    via_up = [jnp.minimum(count >> 1, VIA) for count in far]
+def balanced(up, far, down, keep_up, keep_down):
+    least = [jnp.maximum(keep_up[i], far[i] - VIA) for i in range(SPAN)]
+    most = [jnp.minimum(far[i] - keep_down[i], VIA) for i in range(SPAN)]
+    via_up = [jnp.minimum(jnp.maximum(far[i] >> 1, least[i]), most[i]) for i in range(SPAN)]
     for at in range(SPAN):
         via_down = [far[i] - via_up[i] for i in range(SPAN)]
         nxt, prv = (at + 1) % SPAN, (at - 1) % SPAN
         load_up = jnp.maximum(up[at] + via_up[prv], up[nxt] + via_up[nxt])
         load_down = jnp.maximum(down[at] + via_down[nxt], down[prv] + via_down[prv])
         best = (load_down + far[at] - load_up) >> 1
-        via_up[at] = jnp.minimum(jnp.maximum(best, jnp.maximum(far[at] - VIA, 0)), jnp.minimum(far[at], VIA))
+        via_up[at] = jnp.minimum(jnp.maximum(best, least[at]), most[at])
     via_down = [far[i] - via_up[i] for i in range(SPAN)]
     return via_up, via_down
 
 
+def planned(flows):
+    names = ("up", "down", "far", "first", "second", "cut", "up_id", "down_id", "keep_up", "keep_down")
+    plan = {name: [] for name in names}
+    for at in range(SPAN):
+        u0, u1, gu0, gu1 = flows[at][1]
+        f0, f1, gf0, gf1 = flows[at][2]
+        d0, d1, gd0, gd1 = flows[at][3]
+        gu1 = jnp.where(u0 == u1, 0, gu1)
+        gf1 = jnp.where(f0 == f1, 0, gf1)
+        gd1 = jnp.where(d0 == d1, 0, gd1)
+
+        def shared(parent, count, one, two):
+            return jnp.where((parent == one) | (parent == two), count, 0)
+
+        straight = shared(f0, gf0, u0, u1) + shared(f1, gf1, d0, d1)
+        crossed = shared(f1, gf1, u0, u1) + shared(f0, gf0, d0, d1)
+        swap = crossed > straight
+        first, second = jnp.where(swap, f1, f0), jnp.where(swap, f0, f1)
+        cut, rest = jnp.where(swap, gf1, gf0), jnp.where(swap, gf0, gf1)
+        keep_up, keep_down = shared(first, cut, u0, u1), shared(second, rest, d0, d1)
+        values = (
+            gu0 + gu1 - keep_up, gd0 + gd1 - keep_down, gf0 + gf1, first, second, cut,
+            jnp.where(keep_up > 0, first, -1), jnp.where(keep_down > 0, second, -1), keep_up, keep_down,
+        )
+        for name, value in zip(names, values):
+            plan[name].append(value)
+    plan["via_up"], plan["via_down"] = balanced(
+        plan["up"], plan["far"], plan["down"], plan["keep_up"], plan["keep_down"]
+    )
+    return plan
+
+
 def ring_plan(parents, lengths, ring):
-    flows = [[jnp.int32(0)] * SPAN for _ in range(SPAN)]
+    flows = [[None] * SPAN for _ in range(SPAN)]
     for target in range(SPAN):
-        seen = []
-        for child in range(BEAMS):
-            parent = parents[(ring * SPAN + target) * BEAMS + child]
-            count = grains(lengths[parent])
-            for other in seen:
-                count = jnp.where(parent == other, 0, count)
-            seen.append(parent)
-            source = (parent >> 3) & (SPAN - 1)
-            for at in range(SPAN):
-                if at != target:
-                    ahead = (target - at) % SPAN
-                    flows[at][ahead] = flows[at][ahead] + jnp.where(source == at, count, 0)
-    up = [flow[1] for flow in flows]
-    far = [flow[2] for flow in flows]
-    down = [flow[3] for flow in flows]
-    via_up, via_down = balanced(up, far, down)
-    return up, down, via_up, via_down
+        owners = [parents[(ring * SPAN + target) * BEAMS + child] for child in range(BEAMS)]
+        sources = [(owner >> 3) & (SPAN - 1) for owner in owners]
+        for at in range(SPAN):
+            if at != target:
+                one, two = owners[0], owners[0]
+                for child in range(1, BEAMS):
+                    two = jnp.where(sources[child] == at, owners[child], two)
+                one = owners[BEAMS - 1]
+                for child in range(BEAMS - 2, -1, -1):
+                    one = jnp.where(sources[child] == at, owners[child], one)
+                flows[at][(target - at) % SPAN] = (one, two, grains(lengths[one]), grains(lengths[two]))
+    return planned(flows)
 
 
 def heaviest(parents, lengths, rings):
@@ -81,27 +110,31 @@
     chosen = jnp.where(beam == parents, 1.0, 0.0).astype(jnp.bfloat16)
     counts = jnp.dot(jnp.broadcast_to(counts, (16, beams)), chosen, preferred_element_type=jnp.float32)[:1]
     lane = lax.broadcasted_iota(jnp.int32, (1, beams), 1)
+    source = (parents // BEAMS) % SPAN
+    rank = jnp.zeros_like(lane)
     for back in range(1, BEAMS):
-        same = (pltpu.roll(parents, back, 1) == parents) & (lane % BEAMS >= back)
-        counts = jnp.where(same, 0.0, counts)
-    source = (parents // BEAMS) % SPAN
-    rows = jnp.concatenate([jnp.where(source == at, counts, 0.0) for at in range(SPAN)] * 4, axis=0).astype(jnp.bfloat16)
+        rank = rank + jnp.where((pltpu.roll(source, back, 1) == source) & (lane % BEAMS >= back), 1, 0)
+    names = (parents % (SPAN * BEAMS)).astype(jnp.float32)
+    rows = [
+        jnp.where((source == at) & (rank == order), value, 0.0)
+        for value in (names, counts) for at in range(SPAN) for order in range(MOST)
+    ]
+    rows = jnp.concatenate(rows, axis=0).astype(jnp.bfloat16)
     child = lax.broadcasted_iota(jnp.int32, (beams, 128), 0)
     ring = lax.broadcasted_iota(jnp.int32, (beams, 128), 1)
-    flows = []
+    flows = [[None] * SPAN for _ in range(SPAN)]
     for target in range(SPAN):
         member = (child // BEAMS % SPAN == target) & (child // (BEAMS * SPAN) == ring)
-        flows.append(jnp.dot(rows, jnp.where(member, 1.0, 0.0).astype(jnp.bfloat16), preferred_element_type=jnp.float32))
-
-    def flow(at, ahead):
-        return flows[(at + ahead) % SPAN][at:at + 1].astype(jnp.int32)
-
-    up, far, down = ([flow(at, ahead) for at in range(SPAN)] for ahead in (1, 2, 3))
-    via_up, via_down = balanced(up, far, down)
-    out = jnp.zeros_like(up[0])
+        member = jnp.where(member, 1.0, 0.0).astype(jnp.bfloat16)
+        found = jnp.dot(rows, member, preferred_element_type=jnp.float32).astype(jnp.int32)
+        for at in range(SPAN):
+            wanted = (at * MOST, at * MOST + 1, (SPAN + at) * MOST, (SPAN + at) * MOST + 1)
+            flows[at][(target - at) % SPAN] = tuple(found[one:one + 1] for one in wanted)
+    plan = planned(flows)
+    out = jnp.zeros_like(plan["far"][0])
     for at in range(SPAN):
-        load_up = up[at] + via_up[at] + via_up[(at - 1) % SPAN]
-        load_down = down[at] + via_down[at] + via_down[(at + 1) % SPAN]
+        load_up = plan["up"][at] + plan["via_up"][at] + plan["via_up"][(at - 1) % SPAN]
+        load_down = plan["down"][at] + plan["via_down"][at] + plan["via_down"][(at + 1) % SPAN]
         out = jnp.maximum(out, jnp.maximum(load_up, load_down))
     return jnp.max(out)
 
@@ -186,7 +219,7 @@
 
     slots, owners = slots_of_children(par_ref, me)
     plan = ring_plan(par_ref, len_ref, me >> 2)
-    up, down, via_up, via_down = plan
+    via_up, via_down = plan["via_up"], plan["via_down"]
     flows = {}
     for ahead in range(SPAN):
         served = served_beams(par_ref, me, peer(ahead))
@@ -196,6 +229,11 @@
             beams[distance * MOST + rank] = served[rank]
             lens[distance * MOST + rank] = held[rank]
         flows[ahead] = (served[0], served[1], grains(held[0]))
+
+    for ahead, kept in ((1, "up_id"), (3, "down_id")):
+        first, second, cut = flows[ahead]
+        flows[ahead] = (first, second, jnp.where(me * BEAMS + first == choose(plan[kept], y), 0, cut))
+    flows[2] = (choose(plan["first"], y) & 7, choose(plan["second"], y) & 7, choose(plan["cut"], y))
 
     def grain_at(flow, number):
         first, second, cut = flow
@@ -420,12 +458,15 @@
         slot = slots[child]
         distance = slot >> 1
         length = len_ref[owners[child]]
+        kept = jnp.where(distance == 3, choose(plan["up_id"], (y - 1) & 3), choose(plan["down_id"], (y + 1) & 3))
         before = jnp.int32(0)
         for other in range(BEAMS):
             if other != child:
                 mate = (slots[other] >> 1 == distance) & (slots[other] < slot)
-                differs = owners[other] != owners[child]
-                before = jnp.where(mate & differs, grains(len_ref[owners[other]]), before)
+                counts = (owners[other] != owners[child]) & (owners[other] != kept)
+                before = jnp.where(mate & counts, grains(len_ref[owners[other]]), before)
+        far_before = jnp.where(owners[child] == choose(plan["first"], (y + 2) & 3), 0, choose(plan["cut"], (y + 2) & 3))
+        before = jnp.where(distance == 2, far_before, before)
         from_up = choose(via_up, (y - 1) & 3), choose(via_up, (y + 2) & 3)
         from_down = choose(via_down, (y + 1) & 3), choose(via_down, (y + 2) & 3)
         near_via = jnp.where(distance == 3, from_up[0], from_down[0])
@@ -435,10 +476,17 @@
         split = jnp.minimum(jnp.maximum(split, 0), PER_CHILD)
         start = jnp.where(distance == 2, FIRST + before, near_base + near_via + before)
         again = jnp.where(distance == 2, LINK + FIRST + before + split - from_up[1], start + split + near_pass)
-        near = jnp.where(distance == 2, False, distance != 0)
+        near = (distance == 1) | (distance == 3)
         until = LINK - near_via - near_pass - before
         until = jnp.where(near, jnp.minimum(jnp.maximum(until, 0), PER_CHILD), PER_CHILD)
         third = jnp.where(distance == 3, 0, LEFT) + near_via + near_pass + before + until - LINK
+        held = near & (owners[child] == kept)
+        kept_down = LINK + choose(via_down, (y + 1) & 3) - choose(plan["keep_down"], (y + 1) & 3)
+        start = jnp.where(held, jnp.where(distance == 3, 0, kept_down), start)
+        split = jnp.where(held, PER_CHILD, split)
+        again = jnp.where(held, 0, again)
+        until = jnp.where(held, PER_CHILD, until)
+        third = jnp.where(held, 0, third)
         stays = distance == 0
         meta_ref[child * META] = length
         meta_ref[child * META + 1] = jnp.where(stays, 2 * LINK + (slot & 1) * PER_CHILD, start)

time: 48.2 us -> 46.8 us (0.971)
  Pallas kernels: 46.8 us -> 45.4 us
    pallas_call x1, Pallas kernels: 44.2 us -> 42.8 us  [local(): pl.pallas_call(exchange_kernel, out_shape=(jax.ShapeDtypeStruct((2 * LINK...]
where the time goes in v14:
time: 46.8 us; the launch traced here: 46.7 us
  Pallas kernels  45.4 us (97%)
  between operations  1.3 us (3%)
    pallas_call x1, Pallas kernels, local(): pl.pallas_call(exchange_kernel, out_shape=(jax.ShapeDtypeStruct((2 * LINK...  42.8 us
    pallas_call x1, Pallas kernels, place(): pl.pallas_call(functools.partial(place_kernel, len(got) > 0), out_shape=(...  2.6 us

profile of v14, /device:TPU:0, one launch (start us, length us, event | category | flops | bytes accessed | tf_op | source)
XLA Modules:
  0.0 46.7 jit_solution(1319162319087522918)
XLA Ops:
  0.6 0.0 copy-start
  0.6 0.0 copy-start.2
  0.7 42.8 %exchange.1 = (bf16[256,32,256]{2,1,0:T(8,128)(2,1)S(1)}, bf16[4,16,512]{2,1,0:T(8,128)(2,1)S(1)}, bf16[2,12,32,256]{3,2,1,0:T(8,128)(2,1)S(1)}, s32[56]{0:T(128)S(1)}, s32[1]{0:T(128)}) custom-call(bf16[4,8,1024]{2,1,0:T(8,128)(2,1)} %q_hbm.1, bf16[4,8,256]{2,1,0:T(8,128)(2,1)} %new_hbm.1, bf16[256,32,256]{2,1,0:T(8,128)(2,1)} %bitcast.10, ...), custom_call_target="tpu_custom_call" | custom-call | tf_op jit(solution)/shard_map/exchange/exchange/pallas_call | solution.py:730
  44.1 0.0 copy-done
  44.1 0.0 copy-done.2
  44.1 2.6 %conditional.1 = ((bf16[4,8,1024]{2,1,0:T(8,128)(2,1)}, bf16[8,1024,256]{2,1,0:T(8,128)(2,1)})) conditional(s32[]{:T(128)} %bitcast.7, (bf16[256,32,256]{2,1,0:T(8,128)(2,1)S(1)}, bf16[4,16,512]{2,1,0:T(8,128)(2,1)S(1)}, bf16[4,8,256]{2,1,0:T(8,128)(2,1)S(1)}, s32[56]{0:T(128)S(1)}) %tuple.30, (bf16[256,32,256]{2,1,0:T(8,128)(2,1)S(1)}, ...), branch_computations={%region_0.0_spmd, %region_1.0_spmd, %region_2.0_spmd} | conditional | bytes 2084 | solution.py:857
  44.1 2.6 %place.1 = (bf16[4,8,1024]{2,1,0:T(8,128)(2,1)}, bf16[8,64,16,256]{3,2,1,0:T(8,128)(2,1)}) custom-call(bf16[512,16,256]{2,1,0:T(8,128)(2,1)S(1)} %bitcast.11, bf16[4,16,512]{2,1,0:T(8,128)(2,1)S(1)} %get-tuple-element.31.raw_ref, bf16[4,8,256]{2,1,0:T(8,128)(2,1)S(1)} %get-tuple-element.32.new_ref, s32[56]{0:T(128)S(1)} %get-tuple-element.33.meta_ref), custom_call_target="tpu_custom_call" | custom-call | tf_op jit(solution)/shard_map/cond/branch_0_fun/place/place/pallas_call | solution.py:779
Async XLA Ops:
  0.6 43.5 %copy-start = (bf16[4,8,256]{2,1,0:T(8,128)(2,1)S(1)}, bf16[4,8,256]{2,1,0:T(8,128)(2,1)}, u32[]{:S(2)}) copy-start(bf16[4,8,256]{2,1,0:T(8,128)(2,1)} %new_hbm.1) | copy-start | bytes 49156
  0.6 43.5 %copy-start.2 = (s32[128]{0:T(128)S(1)}, s32[128]{0:T(128)}, u32[]{:S(2)}) copy-start(s32[128]{0:T(128)} %len_hbm.1) | copy-start | bytes 1540

commit v15 on v14

--- a/solution.py
+++ b/solution.py
@@ -18,10 +18,11 @@
 PER_CHILD = 32
 PER_PAGE = PAGE // GRAIN
 TILE = 16
-VIA = 36
+VIA = 32
 MORE = 24
-REST = 36
-LEFT = 12
+REST = 32
+SOME = 6
+LEFT = 20
 FIRST = VIA + MORE
 LINK = FIRST + REST
 META = 7
@@ -444,7 +445,7 @@
     for copy in row_copies:
         copy.wait()
     load = heaviest(par_row[...], len_row[...], rings)
-    over_ref[0] = jnp.where(load > LINK, 1, 0) + jnp.where(load > LINK + LEFT, 1, 0)
+    over_ref[0] = sum(jnp.where(load > limit, 1, 0) for limit in (LINK, LINK + SOME, LINK + LEFT))
     for side, (flow, mine_via, _, passed, _) in enumerate(sides):
         def put_left(at, carry, side=side, flow=flow, mine_via=mine_via, passed=passed):
             for at in [4 * at + more for more in range(4)]:
@@ -617,7 +618,7 @@
     pltpu.make_async_copy(recv_ref, cache_ref, out_sem).wait()
 
 
-def left_kernel(left_ref, got_ref, send_sem, recv_sem):
+def left_kernel(count, left_ref, got_ref, send_sem, recv_sem):
     me = lax.axis_index("dp")
     y = lax.rem(me, SPAN)
     targets = [me - y + lax.rem(y + ahead, SPAN) for ahead in (1, SPAN - 1)]
@@ -628,7 +629,7 @@
     copies = []
     for side, target in enumerate(targets):
         copy = pltpu.make_async_remote_copy(
-            src_ref=left_ref.at[side], dst_ref=got_ref.at[side],
+            src_ref=left_ref.at[side, pl.ds(0, count)], dst_ref=got_ref.at[side, pl.ds(0, count)],
             send_sem=send_sem.at[side], recv_sem=recv_sem.at[side],
             device_id={"dp": target}, device_id_type=MESH,
         )
@@ -798,16 +799,16 @@
     def placed():
         return place()
 
-    def topped():
+    def topped(count, number):
         with jax.named_scope("left"):
             got = pl.pallas_call(
-                left_kernel,
+                functools.partial(left_kernel, count),
                 out_shape=jax.ShapeDtypeStruct(left.shape, bf16),
                 in_specs=[free],
                 out_specs=free,
                 scratch_shapes=[dma((2,)), dma((2,))],
                 compiler_params=pltpu.CompilerParams(
-                    collective_id=2, has_side_effects=True, vmem_limit_bytes=4 * 1024 * 1024
+                    collective_id=number, has_side_effects=True, vmem_limit_bytes=4 * 1024 * 1024
                 ),
                 name="left",
             )(left)
@@ -854,7 +855,7 @@
                 name="finish",
             )(whole.reshape(BEAMS, context, channels), raw, new_kv, lengths, parents)
 
-    return lax.switch(over[0], (placed, topped, resent))
+    return lax.switch(over[0], (placed, functools.partial(topped, SOME, 2), functools.partial(topped, LEFT, 3), resent))
 
 
 def solution(mesh):

time: 46.8 us -> 44 us (0.940)
  Pallas kernels: 45.4 us -> 42.6 us
    pallas_call x1, Pallas kernels: 42.8 us -> 40 us  [local(): pl.pallas_call(exchange_kernel, out_shape=(jax.ShapeDtypeStruct((2 * LINK...]
where the time goes in v15:
time: 44 us; the launch traced here: 43.9 us
  Pallas kernels  42.6 us (97%)
  between operations  1.29 us (3%)
    pallas_call x1, Pallas kernels, local(): pl.pallas_call(exchange_kernel, out_shape=(jax.ShapeDtypeStruct((2 * LINK...  40 us
    pallas_call x1, Pallas kernels, place(): pl.pallas_call(functools.partial(place_kernel, len(got) > 0), out_shape=(...  2.59 us

profile of v15, /device:TPU:0, one launch (start us, length us, event | category | flops | bytes accessed | tf_op | source)
XLA Modules:
  0.0 43.9 jit_solution(2636676061780944311)
XLA Ops:
  0.6 0.0 copy-start
  0.6 0.0 copy-start.2
  0.7 40.0 %exchange.1 = (bf16[240,32,256]{2,1,0:T(8,128)(2,1)S(1)}, bf16[4,16,512]{2,1,0:T(8,128)(2,1)S(1)}, bf16[2,20,32,256]{3,2,1,0:T(8,128)(2,1)S(1)}, s32[56]{0:T(128)S(1)}, s32[1]{0:T(128)}) custom-call(bf16[4,8,1024]{2,1,0:T(8,128)(2,1)} %q_hbm.1, bf16[4,8,256]{2,1,0:T(8,128)(2,1)} %new_hbm.1, bf16[256,32,256]{2,1,0:T(8,128)(2,1)} %bitcast.17, ...), custom_call_target="tpu_custom_call" | custom-call | tf_op jit(solution)/shard_map/exchange/exchange/pallas_call | solution.py:731
  41.3 0.0 copy-done
  41.3 0.0 copy-done.2
  41.3 2.6 %conditional.1 = ((bf16[4,8,1024]{2,1,0:T(8,128)(2,1)}, bf16[8,1024,256]{2,1,0:T(8,128)(2,1)})) conditional(s32[]{:T(128)} %bitcast.10, (bf16[240,32,256]{2,1,0:T(8,128)(2,1)S(1)}, bf16[4,16,512]{2,1,0:T(8,128)(2,1)S(1)}, bf16[4,8,256]{2,1,0:T(8,128)(2,1)S(1)}, s32[56]{0:T(128)S(1)}) %tuple.37, ...), branch_computations={%region_0.0_spmd, %region_1.0_spmd, %region_2.0_spmd, %region_3.0_... | conditional | bytes 2084 | solution.py:858
  41.3 2.6 %place.1 = (bf16[4,8,1024]{2,1,0:T(8,128)(2,1)}, bf16[8,64,16,256]{3,2,1,0:T(8,128)(2,1)}) custom-call(bf16[480,16,256]{2,1,0:T(8,128)(2,1)S(1)} %bitcast.14, bf16[4,16,512]{2,1,0:T(8,128)(2,1)S(1)} %get-tuple-element.41.raw_ref, bf16[4,8,256]{2,1,0:T(8,128)(2,1)S(1)} %get-tuple-element.42.new_ref, s32[56]{0:T(128)S(1)} %get-tuple-element.43.meta_ref), custom_call_target="tpu_custom_call" | custom-call | tf_op jit(solution)/shard_map/cond/branch_0_fun/place/place/pallas_call | solution.py:780
Async XLA Ops:
  0.6 40.6 %copy-start = (bf16[4,8,256]{2,1,0:T(8,128)(2,1)S(1)}, bf16[4,8,256]{2,1,0:T(8,128)(2,1)}, u32[]{:S(2)}) copy-start(bf16[4,8,256]{2,1,0:T(8,128)(2,1)} %new_hbm.1) | copy-start | bytes 49156
  0.6 40.6 %copy-start.2 = (s32[128]{0:T(128)S(1)}, s32[128]{0:T(128)}, u32[]{:S(2)}) copy-start(s32[128]{0:T(128)} %len_hbm.1) | copy-start | bytes 1540

commit v16 on v15

--- a/solution.py
+++ b/solution.py
@@ -18,11 +18,11 @@
 PER_CHILD = 32
 PER_PAGE = PAGE // GRAIN
 TILE = 16
-VIA = 32
-MORE = 24
-REST = 32
-SOME = 6
-LEFT = 20
+VIA = 36
+MORE = 16
+REST = 36
+TIERS = (4, 10, 24)
+LEFT = TIERS[-1]
 FIRST = VIA + MORE
 LINK = FIRST + REST
 META = 7
@@ -208,13 +208,8 @@
         copy = pltpu.make_async_copy(source, target, in_sem.at[5 + at])
         copy.start()
         row_copies.append(copy)
-    quarter = pool_v.shape[0] // 4
-    pool_copies = []
-    for at in range(4):
-        span = pl.ds(at * quarter, quarter)
-        copy = pltpu.make_async_copy(pool_ref.at[span], pool_v.at[span], pool_sem.at[at])
-        copy.start()
-        pool_copies.append(copy)
+    pool_copy = pltpu.make_async_copy(pool_ref, pool_v, pool_sem)
+    pool_copy.start()
     for copy in in_copies:
         copy.wait()
 
@@ -252,8 +247,7 @@
         @pl.when(mine >= other)
         def _(other=other):
             pl.semaphore_signal(here_sem, inc=1, device_id={"tensor": mine - other}, device_id_type=MESH)
-    for copy in pool_copies:
-        copy.wait()
+    pool_copy.wait()
     b_copies = []
     cuts = (0, 8, VIA, FIRST)
 
@@ -445,7 +439,7 @@
     for copy in row_copies:
         copy.wait()
     load = heaviest(par_row[...], len_row[...], rings)
-    over_ref[0] = sum(jnp.where(load > limit, 1, 0) for limit in (LINK, LINK + SOME, LINK + LEFT))
+    over_ref[0] = sum(jnp.where(load > limit, 1, 0) for limit in (LINK, *(LINK + count for count in TIERS)))
     for side, (flow, mine_via, _, passed, _) in enumerate(sides):
         def put_left(at, carry, side=side, flow=flow, mine_via=mine_via, passed=passed):
             for at in [4 * at + more for more in range(4)]:
@@ -762,7 +756,7 @@
                 pltpu.VMEM((SPAN, 2 * rows, wide // 2), bf16),
                 pltpu.SMEM((SPAN * MOST,), jnp.int32),
                 pltpu.SMEM((SPAN * MOST,), jnp.int32),
-                dma((7,)), dma((4,)), dma((shards,)), dma((2,)), dma((3,)),
+                dma((7,)), dma, dma((shards,)), dma((2,)), dma((3,)),
                 dma((SPAN,)), dma((SPAN,)),
                 dma((8,)), dma((8,)),
                 dma((shards,)), dma((shards,)),
@@ -855,7 +849,8 @@
                 name="finish",
             )(whole.reshape(BEAMS, context, channels), raw, new_kv, lengths, parents)
 
-    return lax.switch(over[0], (placed, functools.partial(topped, SOME, 2), functools.partial(topped, LEFT, 3), resent))
+    topping = [functools.partial(topped, count, 2 + at) for at, count in enumerate(TIERS)]
+    return lax.switch(over[0], [placed, *topping, resent])
 
 
 def solution(mesh):

time: 44 us -> 49.6 us (1.13)
  Pallas kernels: 42.6 us -> 48.2 us
    pallas_call x0 -> x1, Pallas kernels: none -> 5.61 us  [topped(): pl.pallas_call(functools.partial(left_kernel, count), out_shape=jax.Shape...]
where the time goes in v16:
time: 49.6 us; the launch traced here: 49.5 us
  Pallas kernels  48.2 us (97%)
  between operations  1.23 us (2%)
    pallas_call x1, Pallas kernels, local(): pl.pallas_call(exchange_kernel, out_shape=(jax.ShapeDtypeStruct((2 * LINK...  40 us
    pallas_call x1, Pallas kernels, topped(): pl.pallas_call(functools.partial(left_kernel, count), out_shape=jax.Shape...  5.61 us
    pallas_call x1, Pallas kernels, place(): pl.pallas_call(functools.partial(place_kernel, len(got) > 0), out_shape=(...  2.61 us

profile of v16, /device:TPU:0, one launch (start us, length us, event | category | flops | bytes accessed | tf_op | source)
XLA Modules:
  0.0 49.5 jit_solution(8308324177434476152)
XLA Ops:
  0.6 0.0 copy-start
  0.6 0.0 copy-start.2
  0.7 40.0 %exchange.1 = (bf16[240,32,256]{2,1,0:T(8,128)(2,1)S(1)}, bf16[4,16,512]{2,1,0:T(8,128)(2,1)S(1)}, bf16[2,24,32,256]{3,2,1,0:T(8,128)(2,1)S(1)}, s32[56]{0:T(128)S(1)}, s32[1]{0:T(128)}) custom-call(bf16[4,8,1024]{2,1,0:T(8,128)(2,1)} %q_hbm.1, bf16[4,8,256]{2,1,0:T(8,128)(2,1)} %new_hbm.1, bf16[256,32,256]{2,1,0:T(8,128)(2,1)} %bitcast.22, ...), custom_call_target="tpu_custom_call" | custom-call | tf_op jit(solution)/shard_map/exchange/exchange/pallas_call | solution.py:725
  41.2 0.0 copy-done
  41.2 0.0 copy-done.2
  41.2 8.3 %conditional.1 = ((bf16[4,8,1024]{2,1,0:T(8,128)(2,1)}, bf16[8,1024,256]{2,1,0:T(8,128)(2,1)})) conditional(s32[]{:T(128)} %bitcast.13, (bf16[240,32,256]{2,1,0:T(8,128)(2,1)S(1)}, bf16[4,16,512]{2,1,0:T(8,128)(2,1)S(1)}, bf16[4,8,256]{2,1,0:T(8,128)(2,1)S(1)}, s32[56]{0:T(128)S(1)}) %tuple.44, ...), branch_computations={%region_0.0_spmd, %region_1.0_spmd, %region_2.0_spmd, %region_3.0_... | conditional | bytes 2084 | solution.py:853
  41.2 5.6 %left.3 = bf16[2,24,32,256]{3,2,1,0:T(8,128)(2,1)S(1)} custom-call(bf16[2,24,32,256]{3,2,1,0:T(8,128)(2,1)S(1)} %get-tuple-element.60.left_ref), custom_call_target="tpu_custom_call" | custom-call | tf_op jit(solution)/shard_map/cond/branch_1_fun/left/left/pallas_call | solution.py:798
  46.9 2.6 %place_left.3 = (bf16[4,8,1024]{2,1,0:T(8,128)(2,1)}, bf16[8,64,16,256]{3,2,1,0:T(8,128)(2,1)}) custom-call(bf16[480,16,256]{2,1,0:T(8,128)(2,1)S(1)} %bitcast.19, bf16[4,16,512]{2,1,0:T(8,128)(2,1)S(1)} %get-tuple-element.57.raw_ref, bf16[4,8,256]{2,1,0:T(8,128)(2,1)S(1)} %get-tuple-element.58.new_ref, s32[56]{0:T(128)S(1)} %get-tuple-element.59.meta_ref, ...), custom_call_target="tpu_custom_call" | custom-call | tf_op jit(solution)/shard_map/cond/branch_1_fun/place/place_left/pallas_call | solution.py:774
Async XLA Ops:
  0.6 40.6 %copy-start = (bf16[4,8,256]{2,1,0:T(8,128)(2,1)S(1)}, bf16[4,8,256]{2,1,0:T(8,128)(2,1)}, u32[]{:S(2)}) copy-start(bf16[4,8,256]{2,1,0:T(8,128)(2,1)} %new_hbm.1) | copy-start | bytes 49156
  0.6 40.6 %copy-start.2 = (s32[128]{0:T(128)S(1)}, s32[128]{0:T(128)}, u32[]{:S(2)}) copy-start(s32[128]{0:T(128)} %len_hbm.1) | copy-start | bytes 1540

commit v17 on v16

--- a/solution.py
+++ b/solution.py
@@ -101,7 +101,7 @@
                 for child in range(BEAMS - 2, -1, -1):
                     one = jnp.where(sources[child] == at, owners[child], one)
                 flows[at][(target - at) % SPAN] = (one, two, grains(lengths[one]), grains(lengths[two]))
-    return planned(flows)
+    return {**planned(flows), "flows": flows}
 
 
 def heaviest(parents, lengths, rings):
@@ -189,6 +189,14 @@
     def peer(distance):
         return base + lax.rem(y + distance, SPAN)
 
+    pairs = (
+        (par_hbm, par_ref), (len_hbm, len_ref), (table_hbm, table_ref), (q_hbm, q_ref), (new_hbm, new_ref),
+        (par_hbm, par_row.at[0]), (len_hbm, len_row.at[0]),
+    )
+    in_copies = [pltpu.make_async_copy(source, target, in_sem.at[at]) for at, (source, target) in enumerate(pairs)]
+    pool_copy = pltpu.make_async_copy(pool_ref, pool_v, pool_sem)
+    for copy in (*in_copies[:3], pool_copy, *in_copies[3:]):
+        copy.start()
     barrier = pltpu.get_barrier_semaphore()
     for distance in range(1, SPAN):
         pl.semaphore_signal(barrier, inc=1, device_id={"dp": peer(distance)}, device_id_type=MESH)
@@ -196,36 +204,15 @@
         @pl.when(mine + other < shards)
         def _(other=other):
             pl.semaphore_signal(barrier, inc=1, device_id={"tensor": mine + other}, device_id_type=MESH)
-    in_copies = []
-    operands = ((par_hbm, par_ref), (q_hbm, q_ref), (new_hbm, new_ref), (table_hbm, table_ref), (len_hbm, len_ref))
-    rows_in = ((par_hbm, par_row.at[0]), (len_hbm, len_row.at[0]))
-    for at, (source, target) in enumerate(operands):
-        copy = pltpu.make_async_copy(source, target, in_sem.at[at])
-        copy.start()
-        in_copies.append(copy)
-    row_copies = []
-    for at, (source, target) in enumerate(rows_in):
-        copy = pltpu.make_async_copy(source, target, in_sem.at[5 + at])
-        copy.start()
-        row_copies.append(copy)
-    pool_copy = pltpu.make_async_copy(pool_ref, pool_v, pool_sem)
-    pool_copy.start()
-    for copy in in_copies:
-        copy.wait()
-
-    slots, owners = slots_of_children(par_ref, me)
+    for copy in in_copies[:3]:
+        copy.wait()
+
     plan = ring_plan(par_ref, len_ref, me >> 2)
     via_up, via_down = plan["via_up"], plan["via_down"]
     flows = {}
-    for ahead in range(SPAN):
-        served = served_beams(par_ref, me, peer(ahead))
-        distance = (SPAN - ahead) % SPAN
-        held = [len_ref[me * BEAMS + served[rank]] for rank in range(MOST)]
-        for rank in range(MOST):
-            beams[distance * MOST + rank] = served[rank]
-            lens[distance * MOST + rank] = held[rank]
-        flows[ahead] = (served[0], served[1], grains(held[0]))
-
+    for ahead in (1, 3):
+        first, second, cut = (choose([plan["flows"][at][ahead][of] for at in range(SPAN)], y) for of in range(3))
+        flows[ahead] = (first & 7, second & 7, cut)
     for ahead, kept in ((1, "up_id"), (3, "down_id")):
         first, second, cut = flows[ahead]
         flows[ahead] = (first, second, jnp.where(me * BEAMS + first == choose(plan[kept], y), 0, cut))
@@ -243,13 +230,9 @@
         (flows[3], choose(via_down, y), choose(via_up, y), choose(via_down, (y + 1) & 3), peer(3)),
     )
     pl.semaphore_wait(barrier, SPAN - 1 + mine)
-    for other in range(1, shards):
-        @pl.when(mine >= other)
-        def _(other=other):
-            pl.semaphore_signal(here_sem, inc=1, device_id={"tensor": mine - other}, device_id_type=MESH)
     pool_copy.wait()
     b_copies = []
-    cuts = (0, 8, VIA, FIRST)
+    cuts = (0, 12, VIA, FIRST)
 
     def send_part(part):
         for side, (flow, mine_via, skip, _, target) in enumerate(sides):
@@ -272,7 +255,13 @@
             b_copies.append(copy)
 
     send_part(0)
-
+    for other in range(1, shards):
+        @pl.when(mine >= other)
+        def _(other=other):
+            pl.semaphore_signal(here_sem, inc=1, device_id={"tensor": mine - other}, device_id_type=MESH)
+    slots, owners = slots_of_children(par_ref, me)
+    for copy in in_copies[3:5]:
+        copy.wait()
     row = lax.broadcasted_iota(jnp.int32, (SPAN * rows, BEAMS), 0)
     col = lax.broadcasted_iota(jnp.int32, (SPAN * rows, BEAMS), 1)
     slot_at = jnp.zeros_like(col)
@@ -304,6 +293,12 @@
         q_copies.append(copy)
     send_part(1)
     send_part(2)
+    for ahead in range(SPAN):
+        served = served_beams(par_ref, me, peer(ahead))
+        for rank in range(MOST):
+            at = (SPAN - ahead) % SPAN * MOST + rank
+            beams[at] = served[rank]
+            lens[at] = len_ref[me * BEAMS + served[rank]]
     w_copies = []
     for block in range(shards):
         copy = pltpu.make_async_copy(w_ref.at[:, pl.ds(block * wide, wide)], w_v.at[block], w_sem.at[block])
@@ -436,7 +431,7 @@
             )
         copy.start()
         r_copies.append(copy)
-    for copy in row_copies:
+    for copy in in_copies[5:]:
         copy.wait()
     load = heaviest(par_row[...], len_row[...], rings)
     over_ref[0] = sum(jnp.where(load > limit, 1, 0) for limit in (LINK, *(LINK + count for count in TIERS)))

time: 49.6 us -> 43.9 us (0.89)
  Pallas kernels: 48.2 us -> 42.5 us
    pallas_call x1 -> x0, Pallas kernels: 5.61 us -> none  [topped(): pl.pallas_call(functools.partial(left_kernel, count), out_shape=jax.Shape...]
where the time goes in v17:
time: 43.9 us; the launch traced here: 43.8 us
  Pallas kernels  42.5 us (97%)
  between operations  1.23 us (3%)
    pallas_call x1, Pallas kernels, local(): pl.pallas_call(exchange_kernel, out_shape=(jax.ShapeDtypeStruct((2 * LINK...  39.9 us
    pallas_call x1, Pallas kernels, place(): pl.pallas_call(functools.partial(place_kernel, len(got) > 0), out_shape=(...  2.6 us

profile of v17, /device:TPU:0, one launch (start us, length us, event | category | flops | bytes accessed | tf_op | source)
XLA Modules:
  0.0 43.8 jit_solution(13487659976564831978)
XLA Ops:
  0.6 0.0 copy-start
  0.6 0.0 copy-start.2
  0.7 39.9 %exchange.1 = (bf16[240,32,256]{2,1,0:T(8,128)(2,1)S(1)}, bf16[4,16,512]{2,1,0:T(8,128)(2,1)S(1)}, bf16[2,24,32,256]{3,2,1,0:T(8,128)(2,1)S(1)}, s32[56]{0:T(128)S(1)}, s32[1]{0:T(128)}) custom-call(bf16[4,8,1024]{2,1,0:T(8,128)(2,1)} %q_hbm.1, bf16[4,8,256]{2,1,0:T(8,128)(2,1)} %new_hbm.1, bf16[256,32,256]{2,1,0:T(8,128)(2,1)} %bitcast.22, ...), custom_call_target="tpu_custom_call" | custom-call | tf_op jit(solution)/shard_map/exchange/exchange/pallas_call | solution.py:720
  41.1 0.0 copy-done
  41.1 0.0 copy-done.2
  41.1 2.6 %conditional.1 = ((bf16[4,8,1024]{2,1,0:T(8,128)(2,1)}, bf16[8,1024,256]{2,1,0:T(8,128)(2,1)})) conditional(s32[]{:T(128)} %bitcast.13, (bf16[240,32,256]{2,1,0:T(8,128)(2,1)S(1)}, bf16[4,16,512]{2,1,0:T(8,128)(2,1)S(1)}, bf16[4,8,256]{2,1,0:T(8,128)(2,1)S(1)}, s32[56]{0:T(128)S(1)}) %tuple.44, ...), branch_computations={%region_0.0_spmd, %region_1.0_spmd, %region_2.0_spmd, %region_3.0_... | conditional | bytes 2084 | solution.py:848
  41.2 2.6 %place.1 = (bf16[4,8,1024]{2,1,0:T(8,128)(2,1)}, bf16[8,64,16,256]{3,2,1,0:T(8,128)(2,1)}) custom-call(bf16[480,16,256]{2,1,0:T(8,128)(2,1)S(1)} %bitcast.18, bf16[4,16,512]{2,1,0:T(8,128)(2,1)S(1)} %get-tuple-element.51.raw_ref, bf16[4,8,256]{2,1,0:T(8,128)(2,1)S(1)} %get-tuple-element.52.new_ref, s32[56]{0:T(128)S(1)} %get-tuple-element.53.meta_ref), custom_call_target="tpu_custom_call" | custom-call | tf_op jit(solution)/shard_map/cond/branch_0_fun/place/place/pallas_call | solution.py:769
Async XLA Ops:
  0.6 40.5 %copy-start = (bf16[4,8,256]{2,1,0:T(8,128)(2,1)S(1)}, bf16[4,8,256]{2,1,0:T(8,128)(2,1)}, u32[]{:S(2)}) copy-start(bf16[4,8,256]{2,1,0:T(8,128)(2,1)} %new_hbm.1) | copy-start | bytes 49156
  0.6 40.5 %copy-start.2 = (s32[128]{0:T(128)S(1)}, s32[128]{0:T(128)}, u32[]{:S(2)}) copy-start(s32[128]{0:T(128)} %len_hbm.1) | copy-start | bytes 1540

commit v18 on v17

--- a/solution.py
+++ b/solution.py
@@ -299,12 +299,6 @@
             at = (SPAN - ahead) % SPAN * MOST + rank
             beams[at] = served[rank]
             lens[at] = len_ref[me * BEAMS + served[rank]]
-    w_copies = []
-    for block in range(shards):
-        copy = pltpu.make_async_copy(w_ref.at[:, pl.ds(block * wide, wide)], w_v.at[block], w_sem.at[block])
-        copy.start()
-        w_copies.append(copy)
-
     def put_all(index, carry):
         slot = index // PAGES
         page = table_ref[beams[slot], index % PAGES]
@@ -361,6 +355,13 @@
         return carry
 
     lax.fori_loop(0, SPAN // 2, attend_two, 0)
+    def w_copy(other):
+        block = lax.rem(mine + other, shards)
+        source = w_ref.at[:, pl.ds(pl.multiple_of(block * wide, wide), wide)]
+        return pltpu.make_async_copy(source, w_v.at[block], w_sem.at[block])
+
+    for other in range(1, 4):
+        w_copy(other).start()
     for copy in b_copies[:4]:
         copy.wait()
     more_copies = b_copies[4:]
@@ -381,8 +382,6 @@
         copy.start()
         b_copies.append(copy)
     attended = att[...].astype(jnp.bfloat16)
-    for copy in w_copies:
-        copy.wait()
 
     def p_copy(other):
         return pltpu.make_async_remote_copy(
@@ -392,6 +391,12 @@
         )
 
     def project(other, carry):
+        w_copy(other).wait()
+
+        @pl.when(other + 3 <= shards)
+        def _():
+            w_copy(other + 3).start()
+
         product = jnp.dot(attended, w_v[lax.rem(mine + other, shards)], preferred_element_type=jnp.float32)
         p_send[other] = product.astype(jnp.bfloat16)
         p_copy(other).start()
@@ -402,6 +407,7 @@
         pl.semaphore_wait(here_sem, shards - 1 - mine)
 
     lax.fori_loop(1, shards, project, 0)
+    w_copy(shards).wait()
     own = jnp.dot(attended, w_v[mine], preferred_element_type=jnp.float32)
 
     for copy in more_copies:

time: 43.9 us -> 49.5 us (1.13)
  Pallas kernels: 42.5 us -> 48.1 us
    pallas_call x0 -> x1, Pallas kernels: none -> 5.61 us  [topped(): pl.pallas_call(functools.partial(left_kernel, count), out_shape=jax.Shape...]
where the time goes in v18:
time: 49.5 us; the launch traced here: 49.4 us
  Pallas kernels  48.1 us (97%)
  between operations  1.23 us (2%)
    pallas_call x1, Pallas kernels, local(): pl.pallas_call(exchange_kernel, out_shape=(jax.ShapeDtypeStruct((2 * LINK...  39.9 us
    pallas_call x1, Pallas kernels, topped(): pl.pallas_call(functools.partial(left_kernel, count), out_shape=jax.Shape...  5.61 us
    pallas_call x1, Pallas kernels, place(): pl.pallas_call(functools.partial(place_kernel, len(got) > 0), out_shape=(...  2.6 us

profile of v18, /device:TPU:0, one launch (start us, length us, event | category | flops | bytes accessed | tf_op | source)
XLA Modules:
  0.0 49.4 jit_solution(18214746224743354926)
XLA Ops:
  0.6 0.0 copy-start
  0.6 0.0 copy-start.2
  0.7 39.9 %exchange.1 = (bf16[240,32,256]{2,1,0:T(8,128)(2,1)S(1)}, bf16[4,16,512]{2,1,0:T(8,128)(2,1)S(1)}, bf16[2,24,32,256]{3,2,1,0:T(8,128)(2,1)S(1)}, s32[56]{0:T(128)S(1)}, s32[1]{0:T(128)}) custom-call(bf16[4,8,1024]{2,1,0:T(8,128)(2,1)} %q_hbm.1, bf16[4,8,256]{2,1,0:T(8,128)(2,1)} %new_hbm.1, bf16[256,32,256]{2,1,0:T(8,128)(2,1)} %bitcast.22, ...), custom_call_target="tpu_custom_call" | custom-call | tf_op jit(solution)/shard_map/exchange/exchange/pallas_call | solution.py:726
  41.1 0.0 copy-done
  41.1 0.0 copy-done.2
  41.1 8.2 %conditional.1 = ((bf16[4,8,1024]{2,1,0:T(8,128)(2,1)}, bf16[8,1024,256]{2,1,0:T(8,128)(2,1)})) conditional(s32[]{:T(128)} %bitcast.13, (bf16[240,32,256]{2,1,0:T(8,128)(2,1)S(1)}, bf16[4,16,512]{2,1,0:T(8,128)(2,1)S(1)}, bf16[4,8,256]{2,1,0:T(8,128)(2,1)S(1)}, s32[56]{0:T(128)S(1)}) %tuple.44, ...), branch_computations={%region_0.0_spmd, %region_1.0_spmd, %region_2.0_spmd, %region_3.0_... | conditional | bytes 2084 | solution.py:854
  41.2 5.6 %left.3 = bf16[2,24,32,256]{3,2,1,0:T(8,128)(2,1)S(1)} custom-call(bf16[2,24,32,256]{3,2,1,0:T(8,128)(2,1)S(1)} %get-tuple-element.60.left_ref), custom_call_target="tpu_custom_call" | custom-call | tf_op jit(solution)/shard_map/cond/branch_1_fun/left/left/pallas_call | solution.py:799
  46.8 2.6 %place_left.3 = (bf16[4,8,1024]{2,1,0:T(8,128)(2,1)}, bf16[8,64,16,256]{3,2,1,0:T(8,128)(2,1)}) custom-call(bf16[480,16,256]{2,1,0:T(8,128)(2,1)S(1)} %bitcast.19, bf16[4,16,512]{2,1,0:T(8,128)(2,1)S(1)} %get-tuple-element.57.raw_ref, bf16[4,8,256]{2,1,0:T(8,128)(2,1)S(1)} %get-tuple-element.58.new_ref, s32[56]{0:T(128)S(1)} %get-tuple-element.59.meta_ref, ...), custom_call_target="tpu_custom_call" | custom-call | tf_op jit(solution)/shard_map/cond/branch_1_fun/place/place_left/pallas_call | solution.py:775
Async XLA Ops:
  0.6 40.5 %copy-start = (bf16[4,8,256]{2,1,0:T(8,128)(2,1)S(1)}, bf16[4,8,256]{2,1,0:T(8,128)(2,1)}, u32[]{:S(2)}) copy-start(bf16[4,8,256]{2,1,0:T(8,128)(2,1)} %new_hbm.1) | copy-start | bytes 49156
  0.6 40.5 %copy-start.2 = (s32[128]{0:T(128)S(1)}, s32[128]{0:T(128)}, u32[]{:S(2)}) copy-start(s32[128]{0:T(128)} %len_hbm.1) | copy-start | bytes 1540

commit v19 on v17

--- a/solution.py
+++ b/solution.py
@@ -14,14 +14,15 @@
 STEPS = 4
 PAGE = 128
 PAGES = 8
-GRAIN = 32
-PER_CHILD = 32
+GRAIN = 16
+PER_CHILD = 64
 PER_PAGE = PAGE // GRAIN
+PAGE_BITS = PER_PAGE.bit_length() - 1
 TILE = 16
-VIA = 36
-MORE = 16
-REST = 36
-TIERS = (4, 10, 24)
+VIA = 72
+MORE = 28
+REST = 72
+TIERS = (8, 20, 48)
 LEFT = TIERS[-1]
 FIRST = VIA + MORE
 LINK = FIRST + REST
@@ -44,7 +45,7 @@
     least = [jnp.maximum(keep_up[i], far[i] - VIA) for i in range(SPAN)]
     most = [jnp.minimum(far[i] - keep_down[i], VIA) for i in range(SPAN)]
     via_up = [jnp.minimum(jnp.maximum(far[i] >> 1, least[i]), most[i]) for i in range(SPAN)]
-    for at in range(SPAN):
+    for at in (*range(SPAN), *range(SPAN)):
         via_down = [far[i] - via_up[i] for i in range(SPAN)]
         nxt, prv = (at + 1) % SPAN, (at - 1) % SPAN
         load_up = jnp.maximum(up[at] + via_up[prv], up[nxt] + via_up[nxt])
@@ -223,7 +224,7 @@
         later = number >= cut
         number = jnp.where(later, number - cut, number)
         number = jnp.minimum(jnp.maximum(number, 0), PER_CHILD - 1)
-        return table_ref[jnp.where(later, second, first), number >> 2] * PER_PAGE + (number & (PER_PAGE - 1))
+        return table_ref[jnp.where(later, second, first), number >> PAGE_BITS] * PER_PAGE + (number & (PER_PAGE - 1))
 
     sides = (
         (flows[1], choose(via_up, y), jnp.int32(0), choose(via_up, (y - 1) & 3), peer(1)),
@@ -232,7 +233,7 @@
     pl.semaphore_wait(barrier, SPAN - 1 + mine)
     pool_copy.wait()
     b_copies = []
-    cuts = (0, 12, VIA, FIRST)
+    cuts = (0, 24, VIA, FIRST)
 
     def send_part(part):
         for side, (flow, mine_via, skip, _, target) in enumerate(sides):

time: 43.9 us -> 48.9 us (1.11)
  Pallas kernels: 42.5 us -> 47.5 us
    pallas_call x0 -> x1, Pallas kernels: none -> 5.61 us  [topped(): pl.pallas_call(functools.partial(left_kernel, count), out_shape=jax.Shape...]
    pallas_call x1, Pallas kernels: 39.9 us -> 39.3 us  [local(): pl.pallas_call(exchange_kernel, out_shape=(jax.ShapeDtypeStruct((2 * LINK...]
where the time goes in v19:
time: 48.9 us; the launch traced here: 48.8 us
  Pallas kernels  47.5 us (97%)
  between operations  1.23 us (3%)
    pallas_call x1, Pallas kernels, local(): pl.pallas_call(exchange_kernel, out_shape=(jax.ShapeDtypeStruct((2 * LINK...  39.3 us
    pallas_call x1, Pallas kernels, topped(): pl.pallas_call(functools.partial(left_kernel, count), out_shape=jax.Shape...  5.61 us
    pallas_call x1, Pallas kernels, place(): pl.pallas_call(functools.partial(place_kernel, len(got) > 0), out_shape=(...  2.59 us

profile of v19, /device:TPU:0, one launch (start us, length us, event | category | flops | bytes accessed | tf_op | source)
XLA Modules:
  0.0 48.8 jit_solution(13704050603978060277)
XLA Ops:
  0.6 0.0 copy-start
  0.6 0.0 copy-start.2
  0.7 39.3 %exchange.1 = (bf16[472,16,256]{2,1,0:T(8,128)(2,1)S(1)}, bf16[4,16,512]{2,1,0:T(8,128)(2,1)S(1)}, bf16[2,48,16,256]{3,2,1,0:T(8,128)(2,1)S(1)}, s32[56]{0:T(128)S(1)}, s32[1]{0:T(128)}) custom-call(bf16[4,8,1024]{2,1,0:T(8,128)(2,1)} %q_hbm.1, bf16[4,8,256]{2,1,0:T(8,128)(2,1)} %new_hbm.1, bf16[512,16,256]{2,1,0:T(8,128)(2,1)} %bitcast.14, ...), custom_call_target="tpu_custom_call" | custom-call | tf_op jit(solution)/shard_map/exchange/exchange/pallas_call | solution.py:721
  40.5 0.0 copy-done
  40.5 0.0 copy-done.2
  40.5 8.2 %conditional.1 = ((bf16[4,8,1024]{2,1,0:T(8,128)(2,1)}, bf16[8,1024,256]{2,1,0:T(8,128)(2,1)})) conditional(s32[]{:T(128)} %bitcast.9, (bf16[472,16,256]{2,1,0:T(8,128)(2,1)S(1)}, bf16[4,16,512]{2,1,0:T(8,128)(2,1)S(1)}, bf16[4,8,256]{2,1,0:T(8,128)(2,1)S(1)}, s32[56]{0:T(128)S(1)}) %tuple.44, ...), branch_computations={%region_0.0_spmd, %region_1.0_spmd, %region_2.0_spmd, %region_3.0_... | conditional | bytes 2084 | solution.py:849
  40.6 5.6 %left.3 = bf16[2,48,16,256]{3,2,1,0:T(8,128)(2,1)S(1)} custom-call(bf16[2,48,16,256]{3,2,1,0:T(8,128)(2,1)S(1)} %get-tuple-element.60.left_ref), custom_call_target="tpu_custom_call" | custom-call | tf_op jit(solution)/shard_map/cond/branch_1_fun/left/left/pallas_call | solution.py:794
  46.2 2.6 %place_left.3 = (bf16[4,8,1024]{2,1,0:T(8,128)(2,1)}, bf16[8,64,16,256]{3,2,1,0:T(8,128)(2,1)}) custom-call(bf16[472,16,256]{2,1,0:T(8,128)(2,1)S(1)} %get-tuple-element.56.recv_ref, bf16[4,16,512]{2,1,0:T(8,128)(2,1)S(1)} %get-tuple-element.57.raw_ref, bf16[4,8,256]{2,1,0:T(8,128)(2,1)S(1)} %get-tuple-element.58.new_ref, s32[56]{0:T(128)S(1)} %get-tuple-element.59.meta_ref, ...), custom_call_target="tpu_custom_call" | custom-call | tf_op jit(solution)/shard_map/cond/branch_1_fun/place/place_left/pallas_call | solution.py:770
Async XLA Ops:
  0.6 39.9 %copy-start = (bf16[4,8,256]{2,1,0:T(8,128)(2,1)S(1)}, bf16[4,8,256]{2,1,0:T(8,128)(2,1)}, u32[]{:S(2)}) copy-start(bf16[4,8,256]{2,1,0:T(8,128)(2,1)} %new_hbm.1) | copy-start | bytes 49156
  0.6 39.9 %copy-start.2 = (s32[128]{0:T(128)S(1)}, s32[128]{0:T(128)}, u32[]{:S(2)}) copy-start(s32[128]{0:T(128)} %len_hbm.1) | copy-start | bytes 1540

commit v20 on v19

--- a/solution.py
+++ b/solution.py
@@ -208,58 +208,6 @@
     for copy in in_copies[:3]:
         copy.wait()
 
-    plan = ring_plan(par_ref, len_ref, me >> 2)
-    via_up, via_down = plan["via_up"], plan["via_down"]
-    flows = {}
-    for ahead in (1, 3):
-        first, second, cut = (choose([plan["flows"][at][ahead][of] for at in range(SPAN)], y) for of in range(3))
-        flows[ahead] = (first & 7, second & 7, cut)
-    for ahead, kept in ((1, "up_id"), (3, "down_id")):
-        first, second, cut = flows[ahead]
-        flows[ahead] = (first, second, jnp.where(me * BEAMS + first == choose(plan[kept], y), 0, cut))
-    flows[2] = (choose(plan["first"], y) & 7, choose(plan["second"], y) & 7, choose(plan["cut"], y))
-
-    def grain_at(flow, number):
-        first, second, cut = flow
-        later = number >= cut
-        number = jnp.where(later, number - cut, number)
-        number = jnp.minimum(jnp.maximum(number, 0), PER_CHILD - 1)
-        return table_ref[jnp.where(later, second, first), number >> PAGE_BITS] * PER_PAGE + (number & (PER_PAGE - 1))
-
-    sides = (
-        (flows[1], choose(via_up, y), jnp.int32(0), choose(via_up, (y - 1) & 3), peer(1)),
-        (flows[3], choose(via_down, y), choose(via_up, y), choose(via_down, (y + 1) & 3), peer(3)),
-    )
-    pl.semaphore_wait(barrier, SPAN - 1 + mine)
-    pool_copy.wait()
-    b_copies = []
-    cuts = (0, 24, VIA, FIRST)
-
-    def send_part(part):
-        for side, (flow, mine_via, skip, _, target) in enumerate(sides):
-            def put(at, carry, side=side, flow=flow, mine_via=mine_via, skip=skip):
-                for at in [4 * at + more for more in range(4)]:
-                    far = at < mine_via
-                    chosen = tuple(jnp.where(far, one, two) for one, two in zip(flows[2], flow))
-                    number = jnp.where(far, skip + at, at - mine_via)
-                    first_send[side, at] = pool_v[grain_at(chosen, number)]
-                return carry
-
-            lax.fori_loop(cuts[part] // 4, cuts[part + 1] // 4, put, 0)
-            span = pl.ds(cuts[part], cuts[part + 1] - cuts[part])
-            copy = pltpu.make_async_remote_copy(
-                src_ref=first_send.at[side, span], dst_ref=first_recv.at[side, span],
-                send_sem=bs_sem.at[side * 4 + part], recv_sem=br_sem.at[side * 4 + part],
-                device_id={"dp": target}, device_id_type=MESH,
-            )
-            copy.start()
-            b_copies.append(copy)
-
-    send_part(0)
-    for other in range(1, shards):
-        @pl.when(mine >= other)
-        def _(other=other):
-            pl.semaphore_signal(here_sem, inc=1, device_id={"tensor": mine - other}, device_id_type=MESH)
     slots, owners = slots_of_children(par_ref, me)
     for copy in in_copies[3:5]:
         copy.wait()
@@ -283,6 +231,30 @@
             q_recv[0] = part
         else:
             q_send[distance] = part
+
+    plan = ring_plan(par_ref, len_ref, me >> 2)
+    via_up, via_down = plan["via_up"], plan["via_down"]
+    flows = {}
+    for ahead in (1, 3):
+        first, second, cut = (choose([plan["flows"][at][ahead][of] for at in range(SPAN)], y) for of in range(3))
+        flows[ahead] = (first & 7, second & 7, cut)
+    for ahead, kept in ((1, "up_id"), (3, "down_id")):
+        first, second, cut = flows[ahead]
+        flows[ahead] = (first, second, jnp.where(me * BEAMS + first == choose(plan[kept], y), 0, cut))
+    flows[2] = (choose(plan["first"], y) & 7, choose(plan["second"], y) & 7, choose(plan["cut"], y))
+
+    def grain_at(flow, number):
+        first, second, cut = flow
+        later = number >= cut
+        number = jnp.where(later, number - cut, number)
+        number = jnp.minimum(jnp.maximum(number, 0), PER_CHILD - 1)
+        return table_ref[jnp.where(later, second, first), number >> PAGE_BITS] * PER_PAGE + (number & (PER_PAGE - 1))
+
+    sides = (
+        (flows[1], choose(via_up, y), jnp.int32(0), choose(via_up, (y - 1) & 3), peer(1)),
+        (flows[3], choose(via_down, y), choose(via_up, y), choose(via_down, (y + 1) & 3), peer(3)),
+    )
+    pl.semaphore_wait(barrier, SPAN - 1 + mine)
     q_copies = []
     for distance in range(1, SPAN):
         copy = pltpu.make_async_remote_copy(
@@ -292,6 +264,35 @@
         )
         copy.start()
         q_copies.append(copy)
+    pool_copy.wait()
+    b_copies = []
+    cuts = (0, 24, VIA, FIRST)
+
+    def send_part(part):
+        for side, (flow, mine_via, skip, _, target) in enumerate(sides):
+            def put(at, carry, side=side, flow=flow, mine_via=mine_via, skip=skip):
+                for at in [4 * at + more for more in range(4)]:
+                    far = at < mine_via
+                    chosen = tuple(jnp.where(far, one, two) for one, two in zip(flows[2], flow))
+                    number = jnp.where(far, skip + at, at - mine_via)
+                    first_send[side, at] = pool_v[grain_at(chosen, number)]
+                return carry
+
+            lax.fori_loop(cuts[part] // 4, cuts[part + 1] // 4, put, 0)
+            span = pl.ds(cuts[part], cuts[part + 1] - cuts[part])
+            copy = pltpu.make_async_remote_copy(
+                src_ref=first_send.at[side, span], dst_ref=first_recv.at[side, span],
+                send_sem=bs_sem.at[side * 4 + part], recv_sem=br_sem.at[side * 4 + part],
+                device_id={"dp": target}, device_id_type=MESH,
+            )
+            copy.start()
+            b_copies.append(copy)
+
+    send_part(0)
+    for other in range(1, shards):
+        @pl.when(mine >= other)
+        def _(other=other):
+            pl.semaphore_signal(here_sem, inc=1, device_id={"tensor": mine - other}, device_id_type=MESH)
     send_part(1)
     send_part(2)
     for ahead in range(SPAN):

time: 48.9 us -> 42.8 us (0.88)
  Pallas kernels: 47.5 us -> 41.2 us
    pallas_call x1 -> x0, Pallas kernels: 5.61 us -> none  [topped(): pl.pallas_call(functools.partial(left_kernel, count), out_shape=jax.Shape...]
    pallas_call x1, Pallas kernels: 39.3 us -> 38.6 us  [local(): pl.pallas_call(exchange_kernel, out_shape=(jax.ShapeDtypeStruct((2 * LINK...]
where the time goes in v20:
time: 42.8 us; the launch traced here: 42.5 us
  Pallas kernels  41.2 us (96%)
  between operations  1.23 us (3%)
    pallas_call x1, Pallas kernels, local(): pl.pallas_call(exchange_kernel, out_shape=(jax.ShapeDtypeStruct((2 * LINK...  38.6 us
    pallas_call x1, Pallas kernels, place(): pl.pallas_call(functools.partial(place_kernel, len(got) > 0), out_shape=(...  2.59 us

profile of v20, /device:TPU:0, one launch (start us, length us, event | category | flops | bytes accessed | tf_op | source)
XLA Modules:
  0.0 42.5 jit_solution(9627141671036111125)
XLA Ops:
  0.6 0.0 copy-start
  0.6 0.0 copy-start.2
  0.7 38.6 %exchange.1 = (bf16[472,16,256]{2,1,0:T(8,128)(2,1)S(1)}, bf16[4,16,512]{2,1,0:T(8,128)(2,1)S(1)}, bf16[2,48,16,256]{3,2,1,0:T(8,128)(2,1)S(1)}, s32[56]{0:T(128)S(1)}, s32[1]{0:T(128)}) custom-call(bf16[4,8,1024]{2,1,0:T(8,128)(2,1)} %q_hbm.1, bf16[4,8,256]{2,1,0:T(8,128)(2,1)} %new_hbm.1, bf16[512,16,256]{2,1,0:T(8,128)(2,1)} %bitcast.14, ...), custom_call_target="tpu_custom_call" | custom-call | tf_op jit(solution)/shard_map/exchange/exchange/pallas_call | solution.py:722
  39.8 0.0 copy-done
  39.9 0.0 copy-done.2
  39.9 2.6 %conditional.1 = ((bf16[4,8,1024]{2,1,0:T(8,128)(2,1)}, bf16[8,1024,256]{2,1,0:T(8,128)(2,1)})) conditional(s32[]{:T(128)} %bitcast.9, (bf16[472,16,256]{2,1,0:T(8,128)(2,1)S(1)}, bf16[4,16,512]{2,1,0:T(8,128)(2,1)S(1)}, bf16[4,8,256]{2,1,0:T(8,128)(2,1)S(1)}, s32[56]{0:T(128)S(1)}) %tuple.44, ...), branch_computations={%region_0.0_spmd, %region_1.0_spmd, %region_2.0_spmd, %region_3.0_... | conditional | bytes 2084 | solution.py:850
  39.9 2.6 %place.1 = (bf16[4,8,1024]{2,1,0:T(8,128)(2,1)}, bf16[8,64,16,256]{3,2,1,0:T(8,128)(2,1)}) custom-call(bf16[472,16,256]{2,1,0:T(8,128)(2,1)S(1)} %get-tuple-element.50.recv_ref, bf16[4,16,512]{2,1,0:T(8,128)(2,1)S(1)} %get-tuple-element.51.raw_ref, bf16[4,8,256]{2,1,0:T(8,128)(2,1)S(1)} %get-tuple-element.52.new_ref, s32[56]{0:T(128)S(1)} %get-tuple-element.53.meta_ref), custom_call_target="tpu_custom_call" | custom-call | tf_op jit(solution)/shard_map/cond/branch_0_fun/place/place/pallas_call | solution.py:771
Async XLA Ops:
  0.6 39.2 %copy-start = (bf16[4,8,256]{2,1,0:T(8,128)(2,1)S(1)}, bf16[4,8,256]{2,1,0:T(8,128)(2,1)}, u32[]{:S(2)}) copy-start(bf16[4,8,256]{2,1,0:T(8,128)(2,1)} %new_hbm.1) | copy-start | bytes 49156
  0.6 39.2 %copy-start.2 = (s32[128]{0:T(128)S(1)}, s32[128]{0:T(128)}, u32[]{:S(2)}) copy-start(s32[128]{0:T(128)} %len_hbm.1) | copy-start | bytes 1540

commit v21 on v20

--- a/solution.py
+++ b/solution.py
@@ -266,7 +266,7 @@
         q_copies.append(copy)
     pool_copy.wait()
     b_copies = []
-    cuts = (0, 24, VIA, FIRST)
+    cuts = (0, 12, VIA, FIRST)
 
     def send_part(part):
         for side, (flow, mine_via, skip, _, target) in enumerate(sides):
@@ -289,12 +289,12 @@
             b_copies.append(copy)
 
     send_part(0)
+    send_part(1)
+    send_part(2)
     for other in range(1, shards):
         @pl.when(mine >= other)
         def _(other=other):
             pl.semaphore_signal(here_sem, inc=1, device_id={"tensor": mine - other}, device_id_type=MESH)
-    send_part(1)
-    send_part(2)
     for ahead in range(SPAN):
         served = served_beams(par_ref, me, peer(ahead))
         for rank in range(MOST):

time: 42.8 us -> 42.9 us (level)
  no operation moved by 1% of the time
where the time goes in v21:
time: 42.9 us; the launch traced here: 42.5 us
  Pallas kernels  41.2 us (96%)
  between operations  1.23 us (3%)
    pallas_call x1, Pallas kernels, local(): pl.pallas_call(exchange_kernel, out_shape=(jax.ShapeDtypeStruct((2 * LINK...  38.6 us
    pallas_call x1, Pallas kernels, place(): pl.pallas_call(functools.partial(place_kernel, len(got) > 0), out_shape=(...  2.59 us

profile of v21, /device:TPU:0, one launch (start us, length us, event | category | flops | bytes accessed | tf_op | source)
XLA Modules:
  0.0 42.5 jit_solution(10881121198977679305)
XLA Ops:
  0.6 0.0 copy-start
  0.6 0.0 copy-start.2
  0.7 38.6 %exchange.1 = (bf16[472,16,256]{2,1,0:T(8,128)(2,1)S(1)}, bf16[4,16,512]{2,1,0:T(8,128)(2,1)S(1)}, bf16[2,48,16,256]{3,2,1,0:T(8,128)(2,1)S(1)}, s32[56]{0:T(128)S(1)}, s32[1]{0:T(128)}) custom-call(bf16[4,8,1024]{2,1,0:T(8,128)(2,1)} %q_hbm.1, bf16[4,8,256]{2,1,0:T(8,128)(2,1)} %new_hbm.1, bf16[512,16,256]{2,1,0:T(8,128)(2,1)} %bitcast.14, ...), custom_call_target="tpu_custom_call" | custom-call | tf_op jit(solution)/shard_map/exchange/exchange/pallas_call | solution.py:722
  39.8 0.0 copy-done
  39.8 0.0 copy-done.2
  39.9 2.6 %conditional.1 = ((bf16[4,8,1024]{2,1,0:T(8,128)(2,1)}, bf16[8,1024,256]{2,1,0:T(8,128)(2,1)})) conditional(s32[]{:T(128)} %bitcast.9, (bf16[472,16,256]{2,1,0:T(8,128)(2,1)S(1)}, bf16[4,16,512]{2,1,0:T(8,128)(2,1)S(1)}, bf16[4,8,256]{2,1,0:T(8,128)(2,1)S(1)}, s32[56]{0:T(128)S(1)}) %tuple.44, ...), branch_computations={%region_0.0_spmd, %region_1.0_spmd, %region_2.0_spmd, %region_3.0_... | conditional | bytes 2084 | solution.py:850
  39.9 2.6 %place.1 = (bf16[4,8,1024]{2,1,0:T(8,128)(2,1)}, bf16[8,64,16,256]{3,2,1,0:T(8,128)(2,1)}) custom-call(bf16[472,16,256]{2,1,0:T(8,128)(2,1)S(1)} %get-tuple-element.50.recv_ref, bf16[4,16,512]{2,1,0:T(8,128)(2,1)S(1)} %get-tuple-element.51.raw_ref, bf16[4,8,256]{2,1,0:T(8,128)(2,1)S(1)} %get-tuple-element.52.new_ref, s32[56]{0:T(128)S(1)} %get-tuple-element.53.meta_ref), custom_call_target="tpu_custom_call" | custom-call | tf_op jit(solution)/shard_map/cond/branch_0_fun/place/place/pallas_call | solution.py:771
Async XLA Ops:
  0.6 39.2 %copy-start = (bf16[4,8,256]{2,1,0:T(8,128)(2,1)S(1)}, bf16[4,8,256]{2,1,0:T(8,128)(2,1)}, u32[]{:S(2)}) copy-start(bf16[4,8,256]{2,1,0:T(8,128)(2,1)} %new_hbm.1) | copy-start | bytes 49156
  0.6 39.2 %copy-start.2 = (s32[128]{0:T(128)S(1)}, s32[128]{0:T(128)}, u32[]{:S(2)}) copy-start(s32[128]{0:T(128)} %len_hbm.1) | copy-start | bytes 1540
